TPU v7x, 32 devices: a whole 2x2x4 slice. The times are simulated.
32 devices in a mesh: dp: 8 (over z, x), expert: 4 (over y, core).
Axes of the slice: x: 2, y: 2, z: 4, core: 2. Of those that a mesh axis runs over, the one named last changes fastest.
Arguments:
- tokens: bfloat16 [32768, 768], P(('dp', 'expert')), may hold values from -6 to 6
- cotangent: bfloat16 [32768, 768], P(('dp', 'expert')), may hold values from -6 to 6
- attention_norm_gain: float32 [768], replicated, may hold values from 0.5 to 1.5
- query_key_value_weight: bfloat16 [768, 2304], replicated, may hold values from -0.21875 to 0.21875
- attention_output_weight: bfloat16 [768, 768], replicated, may hold values from -3 to 3
- adapter_attention_down_maps: bfloat16 [4, 768, 128], replicated, may hold values from -0.21875 to 0.21875
- adapter_query_key_value_up_maps: bfloat16 [3, 128, 768], replicated, may hold values from -0.75 to 0.75
- adapter_output_up_map: bfloat16 [128, 768], replicated, may hold values from -6 to 6
- experts_norm_gain: float32 [768], replicated, may hold values from 0.5 to 1.5
- router_weight: bfloat16 [768, 8], replicated, may hold values from -0.15625 to 0.15625
- constant_expert_mixing: bfloat16 [768, 4], replicated, may hold values from -0.21875 to 0.21875
- constant_expert_vectors: float32 [2, 768], replicated, may hold values from -6 to 6
- expert_gate_up_weight: bfloat16 [4, 768, 4096], P('expert'), may hold values from -0.21875 to 0.21875
- expert_down_weight: bfloat16 [4, 2048, 768], P('expert'), may hold values from -0.125 to 0.125
- adapter_expert_gate_up_down_maps: bfloat16 [4, 2, 768, 128], P('expert'), may hold values from -0.21875 to 0.21875
- adapter_expert_gate_up_up_maps: bfloat16 [4, 2, 128, 2048], P('expert'), may hold values from -0.75 to 0.75
- adapter_expert_down_down_maps: bfloat16 [4, 2048, 128], P('expert'), may hold values from -0.125 to 0.125
- adapter_expert_down_up_maps: bfloat16 [4, 128, 768], P('expert'), may hold values from -0.75 to 0.75
- routes: int32 [32768, 2], P(('dp', 'expert')), may hold values from 0 to 7, all different within a row; in each aligned block of 1024 rows (0 to 1023, 1024 to 2047, ...) at most 512 rows name the same one
- router_logits_carried: float32 [32768, 8], P(('dp', 'expert')), may hold values from -3 to 3
- picture_span_starts: int32 [32, 2], P(('dp', 'expert')), may hold values from 0 to 768, as said below
- sequence_adapter_index: int32 [32], replicated, may hold values from 0 to 7
Outputs:
- result: bfloat16 [32768, 768], P(('dp', 'expert'))
- grad_tokens: bfloat16 [32768, 768], P(('dp', 'expert'))
- grad_lora_a_attn: float32 [4, 768, 128], replicated
- grad_lora_b_qkv: float32 [3, 128, 768], replicated
- grad_lora_b_out: float32 [128, 768], replicated
- grad_lora_a_gate_up: float32 [4, 2, 768, 128], P('expert')
- grad_lora_b_gate_up: float32 [4, 2, 128, 2048], P('expert')
- grad_lora_a_down: float32 [4, 2048, 128], P('expert')
- grad_lora_b_down: float32 [4, 128, 768], P('expert')
Inputs may be any that keep to these rules, and one draw needn't show every extreme that they name: `routes`: each token names two different targets. Within the 1024 rows of one sequence no target is named by more than 512 rows, and in some sequences one target is named by exactly 512 rows. `picture_span_starts`: the j-th picture span of a sequence starts within positions j * (512) to (j + 1) * 512 - 256, so spans never intersect and end inside the sequence. Sequence s uses adapter sequence_adapter_index[s].
All inputs are finite; a program needn't handle non-finite values.
Results may differ from a plain program's by a relative error of at most 0.018.
Values may be sent and summed in bfloat16 or wider, within the bound.
A program may use at most 448 MiB of HBM per device.

v0:
```python
import jax
import jax.numpy as jnp
from jax import lax
from jax.sharding import PartitionSpec as P

HEADS = 12
HD = 64
ADAPTER_RANK = 16
PIC = 256


HIGH_ACCURACY = lax.Precision.HIGHEST
EPS = 1e-06


def rms_scale(inputs, weights):
    return inputs * lax.rsqrt(jnp.mean(inputs * inputs, axis=-1, keepdims=True) + EPS) * weights


def rotate(inputs, cosine, sine):
    halfway = inputs.shape[-1] // 2
    turned = jnp.concatenate([-inputs[..., halfway:], inputs[..., :halfway]], axis=-1)
    return inputs * cosine[:, None, :] + turned * sine[:, None, :]


def tables(length):
    positions = jnp.arange(length, dtype=jnp.float32)
    spacing = 10000.0 ** (-jnp.arange(0, HD, 2, dtype=jnp.float32) / HD)
    angles = positions[:, None] * spacing[None, :]
    angles = jnp.concatenate([angles, angles], axis=1)
    return (jnp.cos(angles), jnp.sin(angles))


def span_index(starts, length):
    positions = jnp.arange(length, dtype=jnp.int32)
    inside = (positions[None, :] >= starts[:, None]) & (positions[None, :] < starts[:, None] + PIC)
    labels = jnp.arange(starts.shape[0], dtype=jnp.int32)[:, None] + 1
    return jnp.sum(inside.astype(jnp.int32) * labels, axis=0)


def visible(offset, block_rows, labels, length):
    query_pos = offset + jnp.arange(block_rows, dtype=jnp.int32)
    key_pos = jnp.arange(length, dtype=jnp.int32)
    causal = key_pos[None, :] <= query_pos[:, None]
    return causal | (labels[:, None] == labels[None, :]) & (labels[:, None] > 0)


def mix_experts(normed, gathered, linear, residual, routes, constant_expert_vectors, experts):
    length = normed.shape[0]
    logits = linear[:, : experts + 4] + residual
    targets = jnp.arange(experts + 4, dtype=jnp.int32)
    picks = (routes[:, :, None] == targets[None, None, :]).astype(jnp.float32)
    chosen = jnp.sum(picks * logits[:, None, :], axis=2)
    gates = jax.nn.softmax(chosen, axis=1)
    mixes = jax.nn.softmax(linear[:, experts + 4 :].reshape(length, 2, 2), axis=2)
    constant = (
        mixes[:, :, 0:1] * normed[:, None, :]
        + mixes[:, :, 1:2] * constant_expert_vectors[None, :, :]
    )
    copied = picks[:, :, experts + 1 : experts + 2] * normed[:, None, :]
    fixed_out = (
        picks[:, :, experts + 2 : experts + 3] * constant[:, 0:1, :]
        + picks[:, :, experts + 3 : experts + 4] * constant[:, 1:2, :]
    )
    return jnp.sum(gates[:, :, None] * (gathered + copied + fixed_out), axis=1)


def swiglu(gate_values, up_projection_part):
    return jax.nn.silu(gate_values) * up_projection_part


def owning_device_forward(
    received_rows, sender_mask, expert_gate_up_weight, gate_up_down_map, gate_up_up_map, a_down
):
    hidden_width = expert_gate_up_weight.shape[1] // 2
    base = jnp.einsum(
        "snd,df->snf", received_rows, expert_gate_up_weight, preferred_element_type=jnp.float32
    )
    adapter_input = jnp.einsum(
        "ewu,tuj->tewj", received_rows, gate_up_down_map, preferred_element_type=jnp.float32
    )
    adapter_input = (adapter_input * sender_mask[None, :, None, :]).astype(jnp.bfloat16)
    extra_terms = jnp.einsum(
        "zlid,zde->zlie", adapter_input, gate_up_up_map, preferred_element_type=jnp.float32
    )
    gate_values = base[:, :, :hidden_width] + extra_terms[0]
    up_projection_part = base[:, :, hidden_width:] + extra_terms[1]
    hidden_state = swiglu(gate_values, up_projection_part).astype(jnp.bfloat16)
    down_projection_input = jnp.einsum(
        "snf,fr->snr", hidden_state, a_down, preferred_element_type=jnp.float32
    )
    down_projection_input = (down_projection_input * sender_mask[:, None, :]).astype(jnp.bfloat16)
    return (adapter_input, gate_values, up_projection_part, hidden_state, down_projection_input)


def owner_backward(
    received_rows,
    grad_rows,
    sender_mask,
    expert_gate_up_weight,
    expert_down_weight,
    gate_up_down_map,
    gate_up_up_map,
    a_down,
    b_down,
):
    hidden_width = expert_gate_up_weight.shape[1] // 2
    adapter_input, gate_values, up_projection_part, hidden_state, down_projection_input = (
        owning_device_forward(
            received_rows,
            sender_mask,
            expert_gate_up_weight,
            gate_up_down_map,
            gate_up_up_map,
            a_down,
        )
    )
    down_grad = jnp.einsum("snd,rd->snr", grad_rows, b_down, preferred_element_type=jnp.float32)
    down_grad = (down_grad * sender_mask[:, None, :]).astype(jnp.bfloat16)
    grad_b_down = jnp.einsum(
        "snr,snd->rd", down_projection_input, grad_rows, preferred_element_type=jnp.float32
    )
    grad_a_down = jnp.einsum(
        "snf,snr->fr", hidden_state, down_grad, preferred_element_type=jnp.float32
    )
    grad_hidden = jnp.einsum(
        "snd,fd->snf", grad_rows, expert_down_weight, preferred_element_type=jnp.float32
    )
    grad_hidden = grad_hidden + jnp.einsum(
        "snr,fr->snf", down_grad, a_down, preferred_element_type=jnp.float32
    )
    unused, pull = jax.vjp(swiglu, gate_values, up_projection_part)
    grad_gate, grad_up = pull(grad_hidden)
    paired_gradients = jnp.stack([grad_gate, grad_up]).astype(jnp.bfloat16)
    adapter_gradient = jnp.einsum(
        "psnf,prf->psnr", paired_gradients, gate_up_up_map, preferred_element_type=jnp.float32
    )
    adapter_gradient = (adapter_gradient * sender_mask[None, :, None, :]).astype(jnp.bfloat16)
    grad_b_gate_up = jnp.einsum(
        "vydz,vydx->vzx", adapter_input, paired_gradients, preferred_element_type=jnp.float32
    )
    grad_a_gate_up = jnp.einsum(
        "vzj,tvze->tje", received_rows, adapter_gradient, preferred_element_type=jnp.float32
    )
    grad_in = jnp.einsum(
        "snf,df->snd",
        paired_gradients[0],
        expert_gate_up_weight[:, :hidden_width],
        preferred_element_type=jnp.float32,
    )
    grad_in = grad_in + jnp.einsum(
        "snf,df->snd",
        paired_gradients[1],
        expert_gate_up_weight[:, hidden_width:],
        preferred_element_type=jnp.float32,
    )
    grad_in = grad_in + jnp.einsum(
        "mwju,mou->wjo", adapter_gradient, gate_up_down_map, preferred_element_type=jnp.float32
    )
    return (grad_in.astype(jnp.bfloat16), grad_a_gate_up, grad_b_gate_up, grad_a_down, grad_b_down)


def body(
    tokens,
    cotangent,
    attention_norm_gain,
    query_key_value_weight,
    attention_output_weight,
    adapter_attention_down_maps,
    adapter_query_key_value_up_maps,
    adapter_output_up_map,
    experts_norm_gain,
    router_weight,
    constant_expert_mixing,
    constant_expert_vectors,
    expert_gate_up_weight,
    expert_down_weight,
    adapter_expert_gate_up_down_maps,
    adapter_expert_gate_up_up_maps,
    adapter_expert_down_down_maps,
    adapter_expert_down_up_maps,
    routes,
    router_logits_carried,
    picture_span_starts,
    sequence_adapter_index,
):
    groups = lax.axis_size("expert")
    length = tokens.shape[0]
    width = tokens.shape[1]
    experts = groups * expert_down_weight.shape[0]
    capacity = 8 * (length * 2 // ((experts + 4) * 4))
    column_indices = (
        jnp.arange(adapter_attention_down_maps.shape[2], dtype=jnp.int32) // ADAPTER_RANK
    )
    group_first = lax.axis_index("dp") * groups
    own_adapter = lax.dynamic_slice_in_dim(
        sequence_adapter_index, group_first + lax.axis_index("expert"), 1, 0
    )
    owned_rows_mask = (column_indices == own_adapter[0]).astype(jnp.float32)
    sources = lax.dynamic_slice_in_dim(sequence_adapter_index, group_first, groups, 0)
    sender_mask = (column_indices[None, :] == sources[:, None]).astype(jnp.float32)

    def norm_attn(inputs):
        return rms_scale(inputs, attention_norm_gain)

    def norm_moe(inputs):
        return rms_scale(inputs, experts_norm_gain)

    h_start = tokens.astype(jnp.float32)
    normed_attn, pull_attn_norm = jax.vjp(norm_attn, h_start)
    attention_input = normed_attn.astype(jnp.bfloat16)
    adapter_query_key_value = jnp.einsum(
        "cz,mzg->mcg",
        attention_input,
        adapter_attention_down_maps[:3],
        preferred_element_type=jnp.float32,
    )
    adapter_query_key_value = (adapter_query_key_value * owned_rows_mask).astype(jnp.bfloat16)
    linear_output = jnp.dot(
        attention_input, query_key_value_weight, preferred_element_type=jnp.float32
    ).reshape(length, 3, width)
    linear_output = linear_output + jnp.einsum(
        "uaj,ujy->auy",
        adapter_query_key_value,
        adapter_query_key_value_up_maps,
        preferred_element_type=jnp.float32,
    )
    cosine, sine = tables(length)
    queries = rotate(linear_output[:, 0].reshape(length, HEADS, HD), cosine, sine).astype(
        jnp.bfloat16
    )
    keys_all = rotate(linear_output[:, 1].reshape(length, HEADS, HD), cosine, sine).astype(
        jnp.bfloat16
    )
    values_all = linear_output[:, 2].reshape(length, HEADS, HD).astype(jnp.bfloat16)
    labels = span_index(picture_span_starts[0], length)
    block_rows = min(1024, length)

    def block_scores(offset):
        allowed = visible(offset, block_rows, labels, length)
        raw_scores = (
            jnp.einsum("qhd,khd->hqk", queries, keys_all, preferred_element_type=jnp.float32)
            * 0.125
        )
        return jnp.where(allowed[None], raw_scores, -1e30)

    block = 0
    scores = block_scores(block * block_rows)
    largest = jnp.max(scores, axis=2, keepdims=True)
    log_sum = largest + jnp.log(jnp.sum(jnp.exp(scores - largest), axis=2, keepdims=True))
    weights = jnp.exp(scores - log_sum).astype(jnp.bfloat16)
    attn_blocks = jnp.einsum(
        "hqk,khd->qhd", weights, values_all, preferred_element_type=jnp.float32
    )
    log_sums = [log_sum]
    attention_output = attn_blocks.reshape(length, width).astype(jnp.bfloat16)
    adapter_output = (
        jnp.dot(
            attention_output, adapter_attention_down_maps[3], preferred_element_type=jnp.float32
        )
        * owned_rows_mask
    ).astype(jnp.bfloat16)
    branch_output = jnp.dot(
        attention_output, attention_output_weight, preferred_element_type=jnp.float32
    ) + jnp.dot(adapter_output, adapter_output_up_map, preferred_element_type=jnp.float32)
    h_mid = h_start + branch_output
    normed, pull_moe_norm = jax.vjp(norm_moe, h_mid)
    sent = normed.astype(jnp.bfloat16)
    router_columns = jnp.concatenate([router_weight, constant_expert_mixing], axis=1)
    linear_router = jnp.dot(sent, router_columns, preferred_element_type=jnp.float32)
    targets = routes.reshape(-1)
    one_hot = (targets[:, None] == jnp.arange(experts, dtype=jnp.int32)[None, :]).astype(jnp.int32)
    slot_index = jnp.sum((jnp.cumsum(one_hot, axis=0) - 1) * one_hot, axis=1)
    places = jnp.where(targets < experts, targets * capacity + slot_index, experts * capacity)

    def to_slots(entries):
        filled = jnp.zeros((experts * capacity + 1, width), jnp.bfloat16).at[places].set(entries)
        return filled[: experts * capacity].reshape(groups, experts * capacity // groups, width)

    def from_slots(holding_buffer):
        padded = jnp.concatenate(
            [
                holding_buffer.reshape(experts * capacity, width),
                jnp.zeros((1, width), jnp.bfloat16),
            ],
            axis=0,
        )
        return padded[places].reshape(length, 2, width)

    send_rows = to_slots(jnp.repeat(sent, 2, axis=0))
    received_rows = lax.all_to_all(send_rows, "expert", split_axis=0, concat_axis=0, tiled=True)
    adapter_input, gate_values, up_projection_part, hidden_state, down_projection_input = (
        owning_device_forward(
            received_rows,
            sender_mask,
            expert_gate_up_weight[0],
            adapter_expert_gate_up_down_maps[0],
            adapter_expert_gate_up_up_maps[0],
            adapter_expert_down_down_maps[0],
        )
    )
    answer = jnp.einsum(
        "snf,fd->snd", hidden_state, expert_down_weight[0], preferred_element_type=jnp.float32
    )
    answer = (
        answer
        + jnp.einsum(
            "lxt,tb->lxb",
            down_projection_input,
            adapter_expert_down_up_maps[0],
            preferred_element_type=jnp.float32,
        )
    ).astype(jnp.bfloat16)
    returned = lax.all_to_all(answer, "expert", split_axis=0, concat_axis=0, tiled=True)
    gathered = from_slots(returned).astype(jnp.float32)

    def mixing(normed_in, gathered_in, linear_in):
        return mix_experts(
            normed_in,
            gathered_in,
            linear_in,
            router_logits_carried,
            routes,
            constant_expert_vectors,
            experts,
        )

    moe_out, pull_mix = jax.vjp(mixing, normed, gathered, linear_router)
    result = (h_mid + moe_out).astype(jnp.bfloat16)
    grad_out = cotangent.astype(jnp.float32)
    grad_normed, grad_gathered, grad_linear = pull_mix(grad_out)
    grad_normed = grad_normed + jnp.dot(
        grad_linear, router_columns.astype(jnp.float32).T, precision=HIGH_ACCURACY
    )
    grad_send = to_slots(grad_gathered.astype(jnp.bfloat16).reshape(2 * length, width))
    grad_rows, rows_in = (
        lax.all_to_all(grad_send, "expert", split_axis=0, concat_axis=0, tiled=True),
        lax.all_to_all(send_rows, "expert", split_axis=0, concat_axis=0, tiled=True),
    )
    grad_in, grad_a_gu, grad_b_gu, grad_a_dn, grad_b_dn = owner_backward(
        rows_in,
        grad_rows,
        sender_mask,
        expert_gate_up_weight[0],
        expert_down_weight[0],
        adapter_expert_gate_up_down_maps[0],
        adapter_expert_gate_up_up_maps[0],
        adapter_expert_down_down_maps[0],
        adapter_expert_down_up_maps[0],
    )
    grad_back = lax.all_to_all(grad_in, "expert", split_axis=0, concat_axis=0, tiled=True)
    grad_normed = grad_normed + jnp.sum(from_slots(grad_back).astype(jnp.float32), axis=1)
    grad_mid = grad_out + pull_moe_norm(grad_normed)[0]
    branch_gradient = grad_mid.astype(jnp.bfloat16)
    adapter_output_gradient = (
        jnp.einsum(
            "si,yi->sy", branch_gradient, adapter_output_up_map, preferred_element_type=jnp.float32
        )
        * owned_rows_mask
    ).astype(jnp.bfloat16)
    output_up_map_gradient = jnp.einsum(
        "em,ea->ma", adapter_output, branch_gradient, preferred_element_type=jnp.float32
    )
    grad_a_out = jnp.einsum(
        "nw,np->wp", attention_output, adapter_output_gradient, preferred_element_type=jnp.float32
    )
    grad_attn = jnp.einsum(
        "ld,ed->le", branch_gradient, attention_output_weight, preferred_element_type=jnp.float32
    )
    grad_attn = grad_attn + jnp.einsum(
        "ui,qi->uq",
        adapter_output_gradient,
        adapter_attention_down_maps[3],
        preferred_element_type=jnp.float32,
    )
    grad_heads = grad_attn.astype(jnp.bfloat16).reshape(length, HEADS, HD)
    block = 0
    offset = block * block_rows
    scores = block_scores(offset)
    probs = jnp.exp(scores - log_sums[block])
    weights = probs.astype(jnp.bfloat16)
    grad_probs = jnp.einsum(
        "qhd,khd->hqk", grad_heads, values_all, preferred_element_type=jnp.float32
    )
    center = jnp.sum(probs * grad_probs, axis=2, keepdims=True)
    grad_scores = (probs * (grad_probs - center) * 0.125).astype(jnp.bfloat16)
    grad_queries = jnp.einsum(
        "hqk,khd->qhd", grad_scores, keys_all, preferred_element_type=jnp.float32
    )
    grad_keys = jnp.einsum("hqk,qhd->khd", grad_scores, queries, preferred_element_type=jnp.float32)
    grad_values = jnp.einsum(
        "hqk,qhd->khd", weights, grad_heads, preferred_element_type=jnp.float32
    )
    grad_query_all = rotate(grad_queries, cosine, -sine)
    grad_key_all = rotate(grad_keys, cosine, -sine)
    linear_gradient = jnp.stack(
        [
            grad_query_all.reshape(length, width),
            grad_key_all.reshape(length, width),
            grad_values.reshape(length, width),
        ],
        axis=1,
    ).astype(jnp.bfloat16)
    adapter_query_key_value_gradient = (
        jnp.einsum(
            "yiz,inz->iyn",
            linear_gradient,
            adapter_query_key_value_up_maps,
            preferred_element_type=jnp.float32,
        )
        * owned_rows_mask
    ).astype(jnp.bfloat16)
    grad_b_qkv = jnp.einsum(
        "ckh,kct->cht", adapter_query_key_value, linear_gradient, preferred_element_type=jnp.float32
    )
    grad_a_qkv = jnp.einsum(
        "sf,xsb->xfb",
        attention_input,
        adapter_query_key_value_gradient,
        preferred_element_type=jnp.float32,
    )
    grad_attn_in = jnp.einsum(
        "lf,df->ld",
        linear_gradient.reshape(length, 3 * width),
        query_key_value_weight,
        preferred_element_type=jnp.float32,
    )
    grad_attn_in = grad_attn_in + jnp.einsum(
        "wxm,wqm->xq",
        adapter_query_key_value_gradient,
        adapter_attention_down_maps[:3],
        preferred_element_type=jnp.float32,
    )
    grad_tokens = (grad_mid + pull_attn_norm(grad_attn_in)[0]).astype(jnp.bfloat16)
    grad_a_attn = jnp.concatenate([grad_a_qkv, grad_a_out[None]], axis=0)
    attn_sum = lax.psum((grad_a_attn, grad_b_qkv, output_up_map_gradient), ("dp", "expert"))
    expert_sum = (
        lax.psum(grad_a_gu[None].astype(jnp.bfloat16), "dp").astype(jnp.float32),
        lax.psum(grad_b_gu[None].astype(jnp.bfloat16), "dp").astype(jnp.float32),
        lax.psum(grad_a_dn[None].astype(jnp.bfloat16), "dp").astype(jnp.float32),
        lax.psum(grad_b_dn[None].astype(jnp.bfloat16), "dp").astype(jnp.float32),
    )
    return (
        result,
        grad_tokens,
        attn_sum[0],
        attn_sum[1],
        attn_sum[2],
        expert_sum[0],
        expert_sum[1],
        expert_sum[2],
        expert_sum[3],
    )


def solution(mesh):
    in_specs = (
        P(("dp", "expert"), None),
        P(("dp", "expert"), None),
        P(),
        P(),
        P(),
        P(),
        P(),
        P(),
        P(),
        P(),
        P(),
        P(),
        P("expert", None, None),
        P("expert", None, None),
        P("expert", None, None, None),
        P("expert", None, None, None),
        P("expert", None, None),
        P("expert", None, None),
        P(("dp", "expert"), None),
        P(("dp", "expert"), None),
        P(("dp", "expert"), None),
        P(),
    )
    out_specs = (
        P(("dp", "expert"), None),
        P(("dp", "expert"), None),
        P(),
        P(),
        P(),
        P("expert", None, None, None),
        P("expert", None, None, None),
        P("expert", None, None),
        P("expert", None, None),
    )
    return jax.shard_map(body, mesh=mesh, in_specs=in_specs, out_specs=out_specs, check_vma=False)
```

profile of v0, /device:TPU:0, one launch (start us, length us, event | category | flops | bytes accessed | tf_op | source)
XLA Modules:
  0.0 1102.7 jit_solution(8590513433224080191)
XLA Ops:
  47.8 22.3 %fusion.2 = (f32[12,1024]{1,0:T(8,128)}, f32[12,1024,1024]{1,2,0:T(8,128)}) fusion(pred[1024,1024]{0,1:T(8,128)(4,1)} %fusion.43, bf16[1024,12,64]{0,2,1:T(8,128)(2,1)} %get-tuple-element.105, bf16[1024,12,64]{0,2,1:T(8,128)(2,1)} %get-tuple-element.104), kind=kOutput, calls=%fused_computation.11 | convolution fusion | flops 1648349184 | bytes 54575104 | tf_op jit(solution)/shard_map/qhd,khd->hqk/dot_general | solution.py:242
  70.1 21.4 %exponential_reduce_fusion = f32[12,1024]{1,0:T(8,128)S(1)} fusion(f32[12,1024,1024]{1,2,0:T(8,128)} %get-tuple-element.110, f32[12,1024]{1,0:T(8,128)} %get-tuple-element.109, pred[1024,1024]{0,1:T(8,128)(4,1)} %fusion.43), kind=kLoop, calls=%fused_computation.9 | loop fusion | flops 50319360 | bytes 51478528 | tf_op jit(solution)/shard_map/reduce_sum | solution.py:250
  91.6 19.6 %convolution_convert_fusion = bf16[12,64,1024]{2,1,0:T(8,128)(2,1)S(1)} fusion(bf16[1024,12,64]{0,2,1:T(8,128)(2,1)S(1)} %bitcast.278, f32[12,1024,1024]{1,2,0:T(8,128)} %get-tuple-element.110, f32[12,1024]{1,0:T(8,128)S(1)} %log_add_fusion, pred[1024,1024]{0,1:T(8,128)(4,1)S(1)} %copy-done.15), kind=kOutput, calls=%fused_computation.125 | convolution fusion | flops 1661730816 | bytes 54575104 | tf_op jit(solution)/shard_map/hqk,khd->qhd/dot_general | solution.py:252
  146.8 12.3 %scatter_custom_fusion = bf16[2049,768]{1,0:T(8,128)(2,1)} fusion(s32[2048]{0:T(1024)} %bitcast.292, bf16[2048,768]{1,0:T(8,128)(2,1)} %reshape.563, bf16[]{:T(256)} %constant.88.clone.1), kind=kCustom, calls=%fused_computation.127 | custom fusion | bytes 3147776 | tf_op jit(solution)/shard_map/scatter | solution.py:277
  207.8 13.2 %scatter_custom_fusion.1 = bf16[2049,768]{1,0:T(8,128)(2,1)} fusion(s32[2048]{0:T(1024)} %bitcast.293, f32[2048,768]{1,0:T(8,128)} %broadcast_in_dim.52, f32[2048]{0:T(1024)S(1)} %div.116, bf16[]{:T(256)} %constant.88.clone.1), kind=kCustom, calls=%fused_computation.80 | custom fusion | flops 3145728 | bytes 9447424 | tf_op jit(solution)/shard_map/scatter | solution.py:277
  240.0 12.7 %fusion.184 = (f32[1024,1,768]{2,1,0:T(1,128)}, f32[1024,1,768]{2,1,0:T(1,128)}) fusion(f32[1024,2,768]{2,1,0:T(2,128)} %multiply_add_fusion), kind=kLoop, calls=%fused_computation.255 | loop fusion | bytes 12582912 | tf_op jit(solution)/shard_map/jvp()/slice | solution.py:62
  268.9 13.2 %fusion.123 = f32[2,4,512,2048]{3,2,1,0:T(8,128)} fusion(bf16[1,2,128,2048]{3,2,1,0:T(8,128)(2,1)S(1)} %copy-done.42, bf16[2,4,512,128]{3,2,0,1:T(8,128)(2,1)S(1)} %fusion.101), kind=kOutput, calls=%fused_computation.159 | convolution fusion | flops 2147483648 | bytes 35651584 | tf_op jit(solution)/shard_map/zlid,zde->zlie/dot_general | solution.py:83
  282.0 13.2 %all-to-all-done.2 = bf16[4,512,768]{2,1,0:T(8,128)(2,1)} async-done(((bf16[4,512,768]{2,1,0:T(8,128)(2,1)}), bf16[4,512,768]{2,1,0:T(8,128)(2,1)}, u32[]{:S(2)}, u32[]{:S(2)}) %all-to-all-start.2) | async-done | bytes 3145760 | tf_op jit(solution)/shard_map/all_to_all | solution.py:337
  307.0 22.4 %fusion.40 = f32[4,512,4096]{2,1,0:T(8,128)} fusion(bf16[4,512,768]{2,1,0:T(8,128)(2,1)} %all-to-all-done, bf16[1,768,4096]{2,1,0:T(8,128)(2,1)} %param.34), kind=kOutput, calls=%fused_computation.48 | convolution fusion | flops 12884901888 | bytes 42991616 | tf_op jit(solution)/shard_map/snd,df->snf/dot_general | solution.py:76
  329.4 39.3 %multiply_convert_fusion.1 = (bf16[4,512,2048]{2,1,0:T(8,128)(2,1)}, bf16[4,512,2048]{2,1,0:T(8,128)(2,1)}, bf16[4,512,2048]{2,1,0:T(8,128)(2,1)}) fusion(f32[4,512,2048]{2,1,0:T(8,128)} %fusion.128, f32[2,4,512,2048]{3,2,1,0:T(8,128)} %fusion.123, f32[4,512,4096]{2,1,0:T(8,128)} %fusion.40, bf16[4,512,768]{2,1,0:T(8,128)(2,1)} %all-to-all-done.2, ...), kind=kOutput, calls=%fused_computation.34 | convolution fusion | flops 6522142720 | bytes 115343360 | tf_op jit(solution)/shard_map/snd,fd->snf/dot_general | solution.py:126
  368.7 8.5 fusion.76
  409.9 11.8 %fusion.52 = f32[4,512,768]{2,1,0:T(8,128)} fusion(bf16[4,512,2048]{2,1,0:T(8,128)(2,1)} %get-tuple-element.80, bf16[768,4096]{1,0:T(8,128)(2,1)} %bitcast.298), kind=kOutput, calls=%fused_computation.82 | convolution fusion | flops 6442450944 | bytes 17825792 | tf_op jit(solution)/shard_map/snf,df->snd/dot_general | solution.py:151
  428.7 10.2 fusion.53
  444.5 91.6 %all-reduce.15.cloned.1.call-done = (bf16[1,2,768,128]{2,3,1,0:T(8,128)(2,1)}, bf16[1,2,128,2048]{3,2,1,0:T(8,128)(2,1)}, bf16[1,2048,128]{2,1,0:T(8,128)(2,1)}, bf16[1,128,768]{2,1,0:T(8,128)(2,1)}) async-done(((bf16[1,2,768,128]{2,3,1,0:T(8,128)(2,1)}, bf16[1,2,128,2048]{3,2,1,0:T(8,128)(2,1)}, bf16[1,2048,128]{2,1,0:T(8,128)(2,1)}, bf16[1,128,768]{2,1,0:T(8,128)(2,1)}), ...) | async-done | bytes 2162704 | tf_op jit(solution)/shard_map/psum | solution.py:438
  552.2 12.9 %gather_fusion = bf16[2048,768]{1,0:T(8,128)(2,1)} fusion(bf16[2049,768]{1,0:T(8,128)(2,1)} %concatenate.42, s32[2048]{0:T(1024)S(1)} %copy-done.64), kind=kCustom, calls=%fused_computation | custom fusion | bytes 6299648 | tf_op jit(solution)/shard_map/gather | solution.py:288
  572.9 48.7 %multiply_reduce_fusion.1 = (f32[1024,2]{1,0:T(8,128)}, f32[1024,768]{1,0:T(8,128)}, f32[1024,768]{1,0:T(8,128)}, f32[1024,768]{1,0:T(8,128)}, f32[1024,768]{1,0:T(8,128)}) fusion(f32[1024,768]{1,0:T(8,128)} %copy.240, f32[1024,2]{1,0:T(8,128)} %fusion.135, f32[1024,2]{1,0:T(8,128)} %get-tuple-element.87, f32[1024,2]{1,0:T(8,128)} %get-tuple-element.89, ...), kind=kLoop, calls=%fused_computation.51 | loop fusion | flops 23590912 | bytes 31498240 | tf_op jit(solution)/shard_map/transpose(jvp())/reduce_sum | solution.py:65
  633.0 20.9 %multiply_reduce_fusion.3 = (f32[1024,2]{1,0:T(8,128)}, f32[1024,2]{1,0:T(8,128)}, f32[1024,768]{1,0:T(8,128)}) fusion(f32[2,768]{1,0:T(2,128)} %param.33, f32[1024,1,768]{2,1,0:T(1,128)} %reshape.534, f32[1024,1,768]{2,1,0:T(1,128)} %reshape.533, f32[1024,768]{1,0:T(8,128)} %copy.235, f32[1024,2]{1,0:T(8,128)} %copy-done.26), kind=kLoop, calls=%fused_computation.53 | loop fusion | flops 10219520 | bytes 12613632 | tf_op jit(solution)/shard_map/transpose(jvp())/reduce_sum | solution.py:58
  678.6 12.4 %gather_fusion.1 = bf16[2048,768]{1,0:T(8,128)(2,1)} fusion(bf16[2049,768]{1,0:T(8,128)(2,1)} %concatenate.43, s32[2048]{0:T(1024)S(1)} %copy-done.64), kind=kCustom, calls=%fused_computation.1 | custom fusion | bytes 6299648 | tf_op jit(solution)/shard_map/gather | solution.py:288
  698.8 11.9 %reduce_sum.261 = f32[1024,768]{1,0:T(8,128)} reduce(f32[1024,2,768]{2,1,0:T(2,128)} %reshape.542, f32[]{:T(128)} %constant.32.clone.1), dimensions={1}, to_apply=%region_26.27 | reduce | flops 786432 | bytes 9437188 | tf_op jit(solution)/shard_map/reduce_sum | solution.py:352
  741.0 21.0 %fusion.187 = f32[12,1024,1024]{1,2,0:T(8,128)} fusion(bf16[1024,12,64]{0,2,1:T(8,128)(2,1)} %bitcast.279, bf16[1024,12,64]{0,2,1:T(8,128)(2,1)} %bitcast.277), kind=kOutput, calls=%fused_computation.258 | convolution fusion | flops 1610612736 | bytes 53477376 | tf_op jit(solution)/shard_map/qhd,khd->hqk/dot_general | solution.py:382
  762.0 67.1 %fusion.84 = f32[1024,12,64]{0,2,1:T(8,128)} fusion(bf16[1024,12,64]{0,2,1:T(8,128)(2,1)} %get-tuple-element.105, f32[12,1024,1024]{1,2,0:T(8,128)} %fusion.187, f32[12,1024,1024]{1,2,0:T(8,128)} %get-tuple-element.110, f32[12,1024]{1,0:T(8,128)} %copy-done.68, pred[1024,1024]{0,1:T(8,128)(4,1)} %fusion.43), kind=kOutput, calls=%fused_computation.124 | convolution fusion | flops 1749038080 | bytes 106479616 | tf_op jit(solution)/shard_map/hqk,qhd->khd/dot_general | solution.py:390
  829.1 66.2 %fusion.81 = f32[1024,12,64]{0,2,1:T(8,128)} fusion(bf16[1024,12,64]{0,2,1:T(8,128)(2,1)} %get-tuple-element.104, f32[12,1024,1024]{1,2,0:T(8,128)} %fusion.187, f32[12,1024,1024]{1,2,0:T(8,128)} %get-tuple-element.110, f32[12,1024]{1,0:T(8,128)} %copy-done.68, pred[1024,1024]{0,1:T(8,128)(4,1)} %fusion.43), kind=kOutput, calls=%fused_computation.123 | convolution fusion | flops 1749038080 | bytes 106479616 | tf_op jit(solution)/shard_map/hqk,khd->qhd/dot_general | solution.py:387
  895.3 21.3 %fusion.145 = bf16[12,64,1024]{2,1,0:T(8,128)(2,1)} fusion(bf16[1024,12,64]{0,2,1:T(8,128)(2,1)} %bitcast.280, f32[12,1024,1024]{1,2,0:T(8,128)} %get-tuple-element.110, f32[12,1024]{1,0:T(8,128)} %copy-done.68, pred[1024,1024]{0,1:T(8,128)(4,1)} %fusion.43), kind=kOutput, calls=%fused_computation.196 | convolution fusion | flops 1660944384 | bytes 54575104 | tf_op jit(solution)/shard_map/hqk,qhd->khd/dot_general | solution.py:391
  965.4 122.5 %all-reduce.13.cloned.1.call-done = (f32[4,768,128]{1,2,0:T(8,128)}, f32[3,128,768]{2,1,0:T(8,128)}, f32[128,768]{1,0:T(8,128)}) async-done(((f32[4,768,128]{1,2,0:T(8,128)}, f32[3,128,768]{2,1,0:T(8,128)}, f32[128,768]{1,0:T(8,128)}), (f32[4,768,128]{1,2,0:T(8,128)}, f32[3,128,768]{2,1,0:T(8,128)}, f32[128,768]{1,0:T(8,128)})) %all-reduce.13.cloned.1.call-update) | async-done | bytes 3145744 | tf_op jit(solution)/shard_map/psum | solution.py:436
  (341 shorter events, 369.2 us)
Async XLA Ops:
  10.7 10.7 copy-start.85
  70.1 21.5 %copy-start.53 = (f32[12,1024]{1,0:T(8,128)S(1)}, f32[12,1024]{1,0:T(8,128)}, u32[]{:S(2)}) copy-start(f32[12,1024]{1,0:T(8,128)} %get-tuple-element.109) | copy-start | bytes 147460
  70.1 21.5 %copy-start.15 = (pred[1024,1024]{0,1:T(8,128)(4,1)S(1)}, pred[1024,1024]{0,1:T(8,128)(4,1)}, u32[]{:S(2)}) copy-start(pred[1024,1024]{0,1:T(8,128)(4,1)} %fusion.43) | copy-start | bytes 3145732
  70.1 21.5 %copy-start.21 = (bf16[1024,1,768]{0,2,1:T(8,128)(2,1)S(1)}, bf16[1024,1,768]{0,2,1:T(8,128)(2,1)}, u32[]{:S(2)}) copy-start(bf16[1024,1,768]{0,2,1:T(8,128)(2,1)} %slice.230) | copy-start | bytes 4718596
  91.6 19.7 %copy-start.68 = (f32[12,1024]{1,0:T(8,128)}, f32[12,1024]{1,0:T(8,128)S(1)}, u32[]{:S(2)}) copy-start(f32[12,1024]{1,0:T(8,128)S(1)} %log_add_fusion) | copy-start | bytes 147460
  91.6 19.7 %copy-start.86 = (f32[128]{0:T(128)S(1)}, f32[128]{0:T(128)}, u32[]{:S(2)}) copy-start(f32[128]{0:T(128)} %copy-done.85) | copy-start | bytes 1540
  91.6 21.5 %copy-start.89 = (bf16[768,768]{1,0:T(8,128)(2,1)S(1)}, bf16[768,768]{1,0:T(8,128)(2,1)}, u32[]{:S(2)}) copy-start(bf16[768,768]{1,0:T(8,128)(2,1)} %param.26) | copy-start | bytes 3538948
  126.2 14.0 %copy-start.76 = (s32[1024,2]{0,1:T(2,128)S(1)}, s32[1024,2]{0,1:T(2,128)}, u32[]{:S(2)}) copy-start(s32[1024,2]{0,1:T(2,128)} %broadcast_multiply_fusion) | copy-start | bytes 24580
  162.8 89.9 %all-to-all-start = ((bf16[4,512,768]{2,1,0:T(8,128)(2,1)}), bf16[4,512,768]{2,1,0:T(8,128)(2,1)}, u32[]{:S(2)}, u32[]{:S(2)}) async-start(bf16[4,512,768]{2,1,0:T(8,128)(2,1)} %bitcast.274), calls=%async_computation | async-start | bytes 6291456 | tf_op jit(solution)/shard_map/all_to_all | solution.py:291
  180.6 11.9 %copy-start.61 = (f32[1024]{0:T(1024)}, f32[1024]{0:T(1024)S(1)}, u32[]{:S(2)}) copy-start(f32[1024]{0:T(1024)S(1)} %reduce_max.28) | copy-start | bytes 12292
  252.7 42.5 %all-to-all-start.2 = ((bf16[4,512,768]{2,1,0:T(8,128)(2,1)}), bf16[4,512,768]{2,1,0:T(8,128)(2,1)}, u32[]{:S(2)}, u32[]{:S(2)}) async-start(bf16[4,512,768]{2,1,0:T(8,128)(2,1)} %bitcast.275), calls=%async_computation.2 | async-start | bytes 6291456 | tf_op jit(solution)/shard_map/all_to_all | solution.py:337
  368.7 8.6 copy-start.43
  368.7 9.2 copy-start.91
  368.7 11.6 %copy-start.92 = (bf16[4,512,2048]{2,1,0:T(8,128)(2,1)S(1)}, bf16[4,512,2048]{2,1,0:T(8,128)(2,1)}, u32[]{:S(2)}) copy-start(bf16[4,512,2048]{2,1,0:T(8,128)(2,1)} %get-tuple-element.80) | copy-start | bytes 25165828
  404.9 138.8 %all-to-all-start.1 = ((bf16[4,512,768]{2,1,0:T(8,128)(2,1)}), bf16[4,512,768]{2,1,0:T(8,128)(2,1)}, u32[]{:S(2)}, u32[]{:S(2)}) async-start(bf16[4,512,768]{2,1,0:T(8,128)(2,1)} %add_convert_fusion), calls=%async_computation.1 | async-start | bytes 6291456 | tf_op jit(solution)/shard_map/all_to_all | solution.py:314
  409.8 126.3 %all-reduce.15.cloned.1.call-start = ((), (), s32[]{:S(2)}) async-start(), calls=%async_computation.5 | async-start | bytes 4325376 | tf_op jit(solution)/shard_map/psum | solution.py:438
  409.9 11.8 %copy-start.30 = (bf16[2,4,512,128]{3,2,1,0:T(8,128)(2,1)S(1)}, bf16[2,4,512,128]{3,2,1,0:T(8,128)(2,1)}, u32[]{:S(2)}) copy-start(bf16[2,4,512,128]{3,2,1,0:T(8,128)(2,1)} %multiply_convert_fusion.5) | copy-start | bytes 3145732
  428.6 10.2 copy-start.31
  428.7 10.2 copy-start.58
  543.7 131.2 %all-to-all-start.3 = ((bf16[4,512,768]{2,1,0:T(8,128)(2,1)}), bf16[4,512,768]{2,1,0:T(8,128)(2,1)}, u32[]{:S(2)}, u32[]{:S(2)}) async-start(bf16[4,512,768]{2,1,0:T(8,128)(2,1)} %fusion.39), calls=%async_computation.3 | async-start | bytes 6291456 | tf_op jit(solution)/shard_map/all_to_all | solution.py:351
  548.4 539.5 %all-reduce.13.cloned.1.call-start = ((), (), s32[]{:S(2)}) async-start(), calls=%async_computation.4 | async-start | bytes 6291456 | tf_op jit(solution)/shard_map/psum | solution.py:436
  714.3 8.4 copy-start.74
  895.3 21.3 %copy-start.5 = (f32[1024,768]{0,1:T(8,128)S(1)}, f32[1024,768]{0,1:T(8,128)}, u32[]{:S(2)}) copy-start(f32[1024,768]{0,1:T(8,128)} %copy-done.4) | copy-start | bytes 9437188
  895.3 21.3 %copy-start.45 = (bf16[1024,128]{1,0:T(8,128)(2,1)S(1)}, bf16[1024,128]{1,0:T(8,128)(2,1)}, u32[]{:S(2)}) copy-start(bf16[1024,128]{1,0:T(8,128)(2,1)} %copy-done.44) | copy-start | bytes 786436
  (76 other events, 261.9 us)
Sparse Core Ops, SparseCore 0:
  428.8 107.2 all-reduce.14
Sparse Core Ops, SparseCore 1:
  950.3 137.5 all-reduce.12
where the time goes:
time: 1110 us; the launch traced here: 1100 us
  matrix products  418 us (38%)
  waiting for transfers between devices  227 us (20%)
  local copies, waits for them, and re-layouts  226 us (20%)
  other arithmetic  195 us (18%)
  starting transfers between devices  19.7 us (2%)
  between operations  16.9 us (2%)
    psum x1, waiting for transfers between devices, body(): lax.psum((grad_a_attn, grad_b_qkv, output_up_map_gradient), ('dp', 'exper...  122 us
    psum x1, waiting for transfers between devices, body(): lax.psum(grad_a_gu[None].astype(jnp.bfloat16), 'dp').astype(jnp.float32)  91.6 us
    dot_general x1, matrix products, body(): jnp.einsum('hqk,qhd->khd', grad_scores, queries, preferred_element_type=j...  67.1 us
    dot_general x1, matrix products, body(): jnp.einsum('hqk,khd->qhd', grad_scores, keys_all, preferred_element_type=...  66.2 us
    reduce_sum x1, other arithmetic, mix_experts(): return jnp.sum(gates[:, :, None] * (gathered + copied + fixed_out), axis=1)  48.7 us
    unnamed x200, local copies, waits for them, and re-layouts  41.2 us
    dot_general x1, matrix products, owner_backward(): jnp.einsum('snd,fd->snf', grad_rows, expert_down_weight, preferred_elemen...  39.3 us
    gather x2, local copies, waits for them, and re-layouts, from_slots(): return padded[places].reshape(length, 2, width)  25.3 us
  transfers between devices with their start and end apart: 6, of which 3 were waited for; matrix products, arithmetic and copies ran while one was open for 26% of the time, Pallas kernels for 0%

commit v1 on v0

v1 whole, which is shorter than its diff:
```python
import functools

import jax
import jax.numpy as jnp
import numpy as np
from jax import lax
from jax.experimental import pallas as pl
from jax.experimental.pallas import tpu as pltpu
from jax.sharding import PartitionSpec as P

HEADS = 12
HD = 64
RANK = 16
PIC = 256
GROUP = 256
HALF = 512
EPS = 1e-06
NEG = -1e30
BF = jnp.bfloat16
F32 = jnp.float32
MIB = 1024 * 1024


def mm(a, b):
    return jnp.dot(a, b, preferred_element_type=F32)


def mm_t(a, b):
    return lax.dot_general(a, b, (((1,), (1,)), ((), ())), preferred_element_type=F32)


def t_mm(a, b):
    return lax.dot_general(a, b, (((0,), (0,)), ((), ())), preferred_element_type=F32)


def iota(shape, dim):
    return lax.broadcasted_iota(jnp.int32, shape, dim)


def one_hot(condition):
    return jnp.where(condition, 1.0, 0.0).astype(BF)


def picker(adapter, place, rows=128, columns=128):
    row, column = iota((rows, columns), 0), iota((rows, columns), 1)
    return one_hot((row - adapter * RANK == column - place * RANK) & (column // RANK == place))


def placer(adapter, place, rows=128, columns=128):
    row, column = iota((rows, columns), 0), iota((rows, columns), 1)
    return one_hot((column - adapter * RANK == row - place * RANK) & (row // RANK == place))


def head_order(back):
    row, column = iota((GROUP, GROUP), 0), iota((GROUP, GROUP), 1)
    a, b = (column, row) if back else (row, column)
    return one_hot(a == (b % 128 // 32) * 64 + b // 128 * 32 + b % 32)


def rope_tables(length):
    spacing = 10000.0 ** (-np.arange(0, HD, 2, dtype=np.float32) / np.float32(HD))
    angles = np.arange(length, dtype=np.float32)[:, None] * spacing.astype(np.float32)[None, :]
    angles = np.tile(angles, (1, 4))
    return np.cos(angles).astype(np.float32), np.sin(angles).astype(np.float32)


def rope(pair, cosine, sine):
    low, high = pair[:, :128], pair[:, 128:]
    return jnp.concatenate([low * cosine - high * sine, high * cosine + low * sine], axis=1)


def span_bias(start, transposed):
    a, b = iota((HALF, HALF), 0), iota((HALF, HALF), 1)
    query, key = (b, a) if transposed else (a, b)
    inside = (query >= start) & (query < start + PIC) & (key >= start) & (key < start + PIC)
    return jnp.where((key <= query) | inside, 0.0, NEG)


def attention_forward_kernel(
    spans, adapter_ref, tok, gain_a, wqkv, down, up, wo, up_out, gain_m, wr, cos, sin,
    xa_ref, q_ref, k_ref, v_ref, ob_ref, ua_ref, uo_ref, lse_ref, h1_ref, xb_ref, lin_ref, wqk_ref,
    down_ref, up_s,
    bias,
):
    length, width = tok.shape
    groups = width // GROUP
    adapter = adapter_ref[0]
    order = head_order(False)
    down_s = sum(mm(down[p], picker(adapter, p)) for p in range(3)).astype(BF)
    down_o = mm(down[3], picker(adapter, 0)).astype(BF)
    up_o = mm(placer(adapter, 0), up_out[...]).astype(BF)
    down_ref[0] = down_s
    down_ref[1] = down_o
    up_s[:, pl.ds(3 * width, width)] = up_o
    for p in range(3):
        rows = mm(placer(adapter, p), up[p]).astype(BF)
        for g in range(groups):
            block = rows[:, g * GROUP : (g + 1) * GROUP]
            if p < 2:
                block = mm(block, order).astype(BF)
            up_s[:, pl.ds(p * width + g * GROUP, GROUP)] = block
    for g in range(2 * groups):
        at = pl.ds(g * GROUP, GROUP)
        wqk_ref[:, at] = mm(wqkv[:, at], order).astype(BF)
    for half in range(length // HALF):
        bias[half] = span_bias(spans[half] - half * HALF, False)

    def project(block, carry):
        at = pl.ds(pl.multiple_of(block * 256, 256), 256)
        h0 = tok[at, :].astype(F32)
        x = h0 * lax.rsqrt(jnp.mean(h0 * h0, axis=1, keepdims=True) + EPS) * gain_a[...]
        x = x.astype(BF)
        xa_ref[at, :] = x
        u = mm(x, down_s).astype(BF)
        ua_ref[at, :] = u
        c, s = cos[at, :], sin[at, :]
        for p, out in enumerate((q_ref, k_ref)):
            for g in range(groups):
                lanes = pl.ds(p * width + g * GROUP, GROUP)
                lin = mm(x, wqk_ref[:, lanes]) + mm(u, up_s[:, lanes])
                out[at, pl.ds(g * GROUP, GROUP)] = rope(lin, c, s).astype(BF)
        lanes = pl.ds(2 * width, width)
        v_ref[at, :] = (mm(x, wqkv[:, lanes]) + mm(u, up_s[:, lanes])).astype(BF)
        return carry

    lax.fori_loop(0, length // 256, project, 0)

    lane = iota((1, GROUP), 1)
    lse_ref[...] = jnp.zeros(lse_ref.shape, F32)
    ob_f = ob_ref

    def attend(head, carry):
        g, h = head // 4, head % 4
        lanes = pl.ds(pl.multiple_of(g * GROUP, GROUP), GROUP)
        qk_own = jnp.where((lane % 128) // 32 == h, 1.0, 0.0).astype(BF)
        v_own = jnp.where(lane // 64 == h, 1.0, 0.0)
        kh = k_ref[:, lanes] * qk_own
        vh = v_ref[:, lanes] * v_own.astype(BF)
        for half in range(length // HALF):
            at = pl.ds(half * HALF, HALF)
            q = q_ref[at, lanes] * BF(0.125)
            keys = (half + 1) * HALF
            diag = mm_t(q, kh[half * HALF : keys]) + bias[half]
            top = jnp.max(diag, axis=1, keepdims=True)
            if half:
                past = mm_t(q, kh[: half * HALF])
                top = jnp.maximum(top, jnp.max(past, axis=1, keepdims=True))
            e = jnp.exp(diag - top)
            total = jnp.sum(e, axis=1, keepdims=True)
            o = mm(e.astype(BF), vh[half * HALF : keys])
            if half:
                e = jnp.exp(past - top)
                total = total + jnp.sum(e, axis=1, keepdims=True)
                o = o + mm(e.astype(BF), vh[: half * HALF])
            o = o * pl.reciprocal(total, approx=False)
            lse = top + jnp.log(total)
            lse_ref[at, :] = jnp.where(iota((1, 128), 1) == head, lse, lse_ref[at, :])
            old = jnp.where(v_own > 0.5, 0.0, ob_f[at, lanes].astype(F32))
            ob_f[at, lanes] = jnp.where(v_own > 0.5, o, old).astype(BF)
        return carry

    lax.fori_loop(0, HEADS, attend, 0)

    def finish(block, carry):
        at = pl.ds(pl.multiple_of(block * 256, 256), 256)
        o = ob_ref[at, :]
        u = mm(o, down_o).astype(BF)
        uo_ref[at, :] = u
        h1 = tok[at, :].astype(F32) + (mm(o, wo[...]) + mm(u, up_o))
        h1_ref[at, :] = h1
        x = h1 * lax.rsqrt(jnp.mean(h1 * h1, axis=1, keepdims=True) + EPS) * gain_m[...]
        x = x.astype(BF)
        xb_ref[at, :] = x
        lin_ref[at, :] = mm(x, wr[...])
        return carry

    lax.fori_loop(0, length // 256, finish, 0)


def attention_forward(tok, gain_a, wqkv, down, up, wo, up_out, gain_m, wr, spans, adapter):
    length, width = tok.shape
    cos, sin = rope_tables(length)
    shapes = [
        ((length, width), BF),
        ((length, width), BF),
        ((length, width), BF),
        ((length, width), BF),
        ((length, width), BF),
        ((length, 128), BF),
        ((length, 128), BF),
        ((length, 128), F32),
        ((length, width), F32),
        ((length, width), BF),
        ((length, 128), F32),
        ((width, 2 * width), BF),
        ((2, width, 128), BF),
        ((128, 4 * width), BF),
    ]
    vmem, smem = pl.BlockSpec(memory_space=pltpu.VMEM), pl.BlockSpec(memory_space=pltpu.SMEM)
    return pl.pallas_call(
        attention_forward_kernel,
        out_shape=[jax.ShapeDtypeStruct(s, t) for s, t in shapes],
        in_specs=[smem, smem] + [vmem] * 11,
        out_specs=[vmem] * len(shapes),
        scratch_shapes=[pltpu.VMEM((length // HALF, HALF, HALF), F32)],
        compiler_params=pltpu.CompilerParams(vmem_limit_bytes=56 * MIB),
        name="attention_forward",
    )(spans, adapter, tok, gain_a, wqkv, down, up, wo, up_out, gain_m, wr, cos, sin)


def attention_backward_kernel(
    spans, dh1_ref, tok, gain_a, wqkv, wqk, wo, down_ref, up_s, cos, sin,
    xa_ref, q_ref, k_ref, v_ref, ob_ref, ua_ref, uo_ref, lse_ref,
    grad_tok, grad_maps,
    bias, dob, datt, duo, lse_t, center_t, dq, dk, dv, dlin, dua,
):
    length, width = tok.shape
    groups = width // GROUP
    for half in range(length // HALF):
        bias[half] = span_bias(spans[half] - half * HALF, True)
    of_head = one_hot(iota((128, width), 1) // HD == iota((128, width), 0))

    def outer(block, carry):
        at = pl.ds(pl.multiple_of(block * 256, 256), 256)
        d = dh1_ref[at, :].astype(BF)
        datt[at, :] = d
        u = mm_t(d, up_s[:, pl.ds(3 * width, width)]).astype(BF)
        duo[at, :] = u
        do = (mm_t(d, wo[...]) + mm_t(u, down_ref[1])).astype(BF)
        dob[at, :] = do
        both = do.astype(F32) * ob_ref[at, :].astype(F32)
        high = both.astype(BF)
        low = (both - high.astype(F32)).astype(BF)
        center_t[:, at] = mm_t(of_head, high) + mm_t(of_head, low)
        lse_t[:, at] = lse_ref[at, :].T
        return carry

    lax.fori_loop(0, length // 256, outer, 0)
    dq[...] = jnp.zeros(dq.shape, F32)
    dk[...] = jnp.zeros(dk.shape, F32)
    dv[...] = jnp.zeros(dv.shape, F32)
    lane = iota((1, GROUP), 1)

    def attend(head, carry):
        g, h = head // 4, head % 4
        lanes = pl.ds(pl.multiple_of(g * GROUP, GROUP), GROUP)
        qk_own = jnp.where((lane % 128) // 32 == h, 1.0, 0.0).astype(BF)
        v_own = jnp.where(lane // 64 == h, 1.0, 0.0).astype(BF)
        lse = lse_t[pl.ds(head, 1), :]
        center = center_t[pl.ds(head, 1), :]
        for half in range(length // HALF):
            at = pl.ds(half * HALF, HALF)
            late = pl.ds(half * HALF, length - half * HALF)
            kh = k_ref[at, lanes] * qk_own
            vh = v_ref[at, lanes] * v_own
            q = q_ref[late, lanes] * BF(0.125)
            do = dob[late, lanes]
            s = mm_t(kh, q) - lse[:, half * HALF :]
            if half * HALF + HALF < length:
                s = jnp.concatenate([s[:, :HALF] + bias[half], s[:, HALF:]], axis=1)
            else:
                s = s + bias[half]
            prob = jnp.exp(s)
            dp = mm_t(vh, do)
            ds = (prob * (dp - center[:, half * HALF :])).astype(BF)
            dv[at, lanes] += mm(prob.astype(BF), do * v_own)
            dk[at, lanes] += mm(ds, q * qk_own)
            dq[late, lanes] += t_mm(ds, kh)
        return carry

    lax.fori_loop(0, HEADS, attend, 0)

    def inner(block, carry):
        at = pl.ds(pl.multiple_of(block * 256, 256), 256)
        c, s = cos[at, :], -sin[at, :]
        for g in range(groups):
            lanes = pl.ds(g * GROUP, GROUP)
            dlin[at, lanes] = rope(dq[at, lanes] * 0.125, c, s).astype(BF)
            dlin[at, pl.ds(width + g * GROUP, GROUP)] = rope(dk[at, lanes], c, s).astype(BF)
        dlin[at, pl.ds(2 * width, width)] = dv[at, :].astype(BF)
        d = dlin[at, :]
        u = mm_t(d, up_s[:, pl.ds(0, 3 * width)]).astype(BF)
        dua[at, :] = u
        dx = mm_t(d[:, : 2 * width], wqk[...]) + mm_t(d[:, 2 * width :], wqkv[:, pl.ds(2 * width, width)])
        dx = (dx + mm_t(u, down_ref[0])) * gain_a[...]
        h0 = tok[at, :].astype(F32)
        r = lax.rsqrt(jnp.mean(h0 * h0, axis=1, keepdims=True) + EPS)
        pull = r * dx - h0 * (r * r * r * jnp.mean(dx * h0, axis=1, keepdims=True))
        grad_tok[at, :] = (dh1_ref[at, :] + pull).astype(BF)
        return carry

    lax.fori_loop(0, length // 256, inner, 0)
    order = head_order(True)
    grads = t_mm(dua[...], xa_ref[...]).astype(BF)
    for p in range(3):
        grad_maps[p] = grads[p * RANK : (p + 1) * RANK]
    grad_maps[3] = t_mm(duo[...], ob_ref[...]).astype(BF)[:RANK]
    for p in range(3):
        grads = t_mm(ua_ref[...], dlin[:, pl.ds(p * width, width)]).astype(BF)[p * RANK : (p + 1) * RANK]
        if p < 2:
            grads = jnp.concatenate(
                [mm(grads[:, g * GROUP : (g + 1) * GROUP], order) for g in range(groups)], axis=1
            ).astype(BF)
        grad_maps[4 + p] = grads
    grad_maps[7] = t_mm(uo_ref[...], datt[...]).astype(BF)[:RANK]


def attention_backward(spans, dh1, tok, gain_a, wqkv, wqk, wo, down_s, up_s, xa, q, k, v, ob, ua, uo, lse):
    length, width = tok.shape
    cos, sin = rope_tables(length)
    vmem, smem = pl.BlockSpec(memory_space=pltpu.VMEM), pl.BlockSpec(memory_space=pltpu.SMEM)
    return pl.pallas_call(
        attention_backward_kernel,
        out_shape=[
            jax.ShapeDtypeStruct((length, width), BF),
            jax.ShapeDtypeStruct((8, RANK, width), BF),
        ],
        in_specs=[smem] + [vmem] * 18,
        out_specs=[vmem] * 2,
        scratch_shapes=[
            pltpu.VMEM((length // HALF, HALF, HALF), F32),
            pltpu.VMEM((length, width), BF),
            pltpu.VMEM((length, width), BF),
            pltpu.VMEM((length, 128), BF),
            pltpu.VMEM((128, length), F32),
            pltpu.VMEM((128, length), F32),
            pltpu.VMEM((length, width), F32),
            pltpu.VMEM((length, width), F32),
            pltpu.VMEM((length, width), F32),
            pltpu.VMEM((length, 3 * width), BF),
            pltpu.VMEM((length, 128), BF),
        ],
        compiler_params=pltpu.CompilerParams(vmem_limit_bytes=60 * MIB),
        name="attention_backward",
    )(spans, dh1, tok, gain_a, wqkv, wqk, wo, down_s, up_s, cos, sin, xa, q, k, v, ob, ua, uo, lse)


def split(x):
    high = x.astype(BF)
    return high, (x - high.astype(F32)).astype(BF)


def experts_kernel(
    adapter_ref, xb, h1_ref, lin_ref, cot, routes, carried, gain_m, wr, vectors,
    w_gate, w_up, w_down, gu_down, gu_up, dn_down, dn_up,
    result, dh1_ref, grads,
    count, gates, gates_t, place, place_t, both, x_s, c_s, dy_s, g_s, y_acc, dx_acc, ug_s, ud_acc, dud_s, dug_acc,
    a_gu, b_dn, acc,
):
    e, j = pl.program_id(0), pl.program_id(1)
    experts, tiles = pl.num_programs(0), pl.num_programs(1)
    length, width = xb.shape
    kinds = carried.shape[1]
    numbers = kinds - 4
    tile = w_gate.shape[2]
    hidden = grads.shape[2] - 3 * width
    hidden //= 3
    adapter = adapter_ref[0]
    rows_of = 128

    @pl.when((e == 0) & (j == 0))
    def _():
        lane = iota((1, kinds), 1)
        logits = lin_ref[:, :kinds] + carried[...]
        picks = [lane == routes[:, k : k + 1] for k in range(2)]
        chosen = [jnp.sum(jnp.where(p, logits, 0.0), axis=1, keepdims=True) for p in picks]
        top = jnp.maximum(*chosen)
        parts = [jnp.exp(c - top) for c in chosen]
        total = parts[0] + parts[1]
        gates[...] = jnp.zeros(gates.shape, F32)
        gates[:, :kinds] = jnp.where(picks[0], parts[0] / total, jnp.where(picks[1], parts[1] / total, 0.0))
        wide = iota((1, 128), 1)
        named = [(wide == routes[:, k : k + 1]) & (wide < numbers) for k in range(2)]
        member = one_hot(named[0] | named[1])
        for block in range(length // 256):
            before = one_hot(iota((256, length), 1) < iota((256, length), 0) + block * 256)
            place[pl.ds(block * 256, 256), :] = mm(before, member)
        counts = jnp.sum(member.astype(F32), axis=0, keepdims=True)
        padded = jnp.floor((counts + (rows_of - 1)) * (1.0 / rows_of))
        earlier = one_hot(iota((128, 128), 0) < iota((128, 128), 1))
        starts = rows_of * mm(jnp.broadcast_to(padded, (8, 128)).astype(BF), earlier)[:1]
        own = jnp.where(named[0] | named[1], place[...], -1.0)
        place_t[...] = own.T
        gates_t[...] = gates[...].T
        spots = [
            jnp.sum(jnp.where(n, place[...] + starts + 1.0, 0.0), axis=1, keepdims=True) - 1.0 for n in named
        ]
        place[...] = jnp.where(wide == 0, spots[0], spots[1])
        for i in range(numbers):
            mine = wide == i
            count[0, i] = jnp.sum(jnp.where(mine, padded, 0.0)).astype(jnp.int32)
            count[1, i] = jnp.sum(jnp.where(mine, starts, 0.0)).astype(jnp.int32)
        count[1, numbers] = jnp.sum(jnp.where(wide < numbers, padded, 0.0)).astype(jnp.int32) * rows_of

    blocks = count[0, e]
    first = pl.multiple_of(count[1, e], rows_of)

    @pl.when((j == 0) & (blocks > 0))
    def _():
        a_gu[...] = (mm(gu_down[0, 0], picker(adapter, 0)) + mm(gu_down[0, 1], picker(adapter, 1))).astype(BF)
        b_dn[...] = mm(placer(adapter, 0), dn_up[0]).astype(BF)

    @pl.when((j == 0) & (blocks == 0))
    def _():
        grads[...] = jnp.zeros(grads.shape, BF)

    def work(n):
        rows = pl.ds(0, n)

        @pl.when(j == 0)
        def _():
            own = iota((n, length), 0).astype(F32) == place_t[pl.ds(e, 1), :]
            taken = one_hot(own)
            x = mm(taken, xb[...]).astype(BF)
            c = mm(taken, cot[...]).astype(BF)
            g = jnp.sum(jnp.where(own, gates_t[pl.ds(e, 1), :], 0.0), axis=1, keepdims=True)
            dy = (g * c.astype(F32)).astype(BF)
            x_s[rows, :] = x
            c_s[rows, :] = c
            dy_s[rows, :] = dy
            g_s[rows, :] = jnp.broadcast_to(g, (n, 128))
            ug_s[rows, :] = mm(x, a_gu[...]).astype(BF)
            dud_s[rows, :] = mm_t(dy, b_dn[...]).astype(BF)

        x, dy, ug, dud = x_s[rows, :], dy_s[rows, :], ug_s[rows, :], dud_s[rows, :]
        b_gate = mm(placer(adapter, 0), gu_up[0, 0]).astype(BF)
        b_up = mm(placer(adapter, 1), gu_up[0, 1]).astype(BF)
        a_dn = mm(dn_down[0], picker(adapter, 0)).astype(BF)
        gate = mm(x, w_gate[0]) + mm(ug, b_gate)
        up = mm(x, w_up[0]) + mm(ug, b_up)
        sig = 1.0 / (1.0 + jnp.exp(-gate))
        act = gate * sig
        hid = (act * up).astype(BF)
        dhid = mm_t(dy, w_down[0]) + mm_t(dud, a_dn)
        dup = (dhid * act).astype(BF)
        dgate = (dhid * up * (sig + act * (1.0 - sig))).astype(BF)
        y = mm(hid, w_down[0])
        ud = mm(hid, a_dn)
        dx = mm_t(dgate, w_gate[0]) + mm_t(dup, w_up[0])
        dug = mm_t(dgate, b_gate) + mm_t(dup, b_up)
        at = pl.multiple_of(j * tile, tile)
        ug_t = ug.T
        grads[0, :, pl.ds(2 * width + at, tile)] = mm(ug_t[:RANK], dgate).astype(BF)
        grads[0, :, pl.ds(2 * width + hidden + at, tile)] = mm(ug_t[RANK : 2 * RANK], dup).astype(BF)
        grads[0, :, pl.ds(2 * width + 2 * hidden + at, tile)] = mm(dud.T[:RANK], hid).astype(BF)

        @pl.when(j == 0)
        def _():
            y_acc[rows, :] = y
            dx_acc[rows, :] = dx
            ud_acc[rows, :] = ud
            dug_acc[rows, :] = dug

        @pl.when(j > 0)
        def _():
            y_acc[rows, :] += y
            dx_acc[rows, :] += dx
            ud_acc[rows, :] += ud
            dug_acc[rows, :] += dug

        @pl.when(j == tiles - 1)
        def _():
            ud = ud_acc[rows, :].astype(BF)
            dug = dug_acc[rows, :].astype(BF)
            y = y_acc[rows, :] + mm(ud, b_dn[...])
            g = g_s[rows, :][:, :1]
            dg = jnp.sum(c_s[rows, :].astype(F32) * y.astype(BF).astype(F32), axis=1, keepdims=True)
            high, low = split(dg)
            lane = iota((1, 128), 1)
            to = pl.ds(first, n)
            both[to, :width] = (g * y).astype(BF)
            both[to, width : 2 * width] = (dx_acc[rows, :] + mm_t(dug, a_gu[...])).astype(BF)
            both[to, 2 * width :] = jnp.where(
                lane == e, high.astype(F32), jnp.where(lane == e + 64, low.astype(F32), 0.0)
            ).astype(BF)
            x, dy = x_s[rows, :], dy_s[rows, :]
            to_a = mm(dug.T[: 2 * RANK], x).astype(BF)
            grads[0, :, :width] = to_a[:RANK]
            grads[0, :, width : 2 * width] = to_a[RANK:]
            grads[0, :, 2 * width + 3 * hidden :] = mm(ud.T[:RANK], dy).astype(BF)

    for number in range(1, 512 // rows_of + 1):
        pl.when(blocks == number)(functools.partial(work, number * rows_of))

    @pl.when((e == experts - 1) & (j == tiles - 1))
    def _():
        used = count[1, numbers]
        both[pl.ds(pl.multiple_of(used, rows_of), HALF), :] = jnp.zeros((HALF, both.shape[1]), BF)
        lane = iota((1, 128), 1)

        def combine(block, carry):
            at = pl.ds(pl.multiple_of(block * 256, 256), 256)
            acc[...] = jnp.zeros(acc.shape, F32)
            spots = place[at, :]

            def add(part, carry):
                k0 = pl.multiple_of(part * HALF, HALF)
                slot = (iota((256, HALF), 1) + k0).astype(F32)
                taken = one_hot((slot == spots[:, :1]) | (slot == spots[:, 1:2]))
                acc[...] += mm(taken, both[pl.ds(k0, HALF), :])
                return carry

            lax.fori_loop(0, (used + HALF - 1) // HALF, add, 0)
            h1 = h1_ref[at, :]
            ct = cot[at, :].astype(F32)
            r = lax.rsqrt(jnp.mean(h1 * h1, axis=1, keepdims=True) + EPS)
            gain = gain_m[...]
            n2 = h1 * r * gain
            lin = lin_ref[at, :]
            g = gates[at, :]
            gc = g[:, numbers + 1 : numbers + 2]
            g_fix = [g[:, numbers + 2 + i : numbers + 3 + i] for i in range(2)]
            mixes = []
            for i in range(2):
                a, b = lin[:, kinds + 2 * i : kinds + 2 * i + 1], lin[:, kinds + 2 * i + 1 : kinds + 2 * i + 2]
                top = jnp.maximum(a, b)
                a, b = jnp.exp(a - top), jnp.exp(b - top)
                mixes.append((a / (a + b), b / (a + b)))
            vecs = [vectors[i : i + 1, :] for i in range(2)]
            to_n2 = gc + g_fix[0] * mixes[0][0] + g_fix[1] * mixes[1][0]
            out = h1 + acc[:, :width] + to_n2 * n2
            out = out + (g_fix[0] * mixes[0][1]) * vecs[0] + (g_fix[1] * mixes[1][1]) * vecs[1]
            result[at, :] = out.astype(BF)
            a = jnp.sum(ct * n2, axis=1, keepdims=True)
            bs = [jnp.sum(ct * v, axis=1, keepdims=True) for v in vecs]
            packed = acc[:, 2 * width :]
            dg = jnp.where(lane < numbers, packed + pltpu.roll(packed, 64, 1), 0.0)
            dg = jnp.where(lane == numbers + 1, a, dg)
            for i in range(2):
                dg = jnp.where(lane == numbers + 2 + i, mixes[i][0] * a + mixes[i][1] * bs[i], dg)
            dlin = g * (dg - jnp.sum(g * dg, axis=1, keepdims=True))
            for i in range(2):
                pull = mixes[i][0] * mixes[i][1] * (g_fix[i] * (a - bs[i]))
                dlin = jnp.where(lane == kinds + 2 * i, pull, jnp.where(lane == kinds + 2 * i + 1, -pull, dlin))
            high, low = split(dlin)
            dn2 = acc[:, width : 2 * width] + (mm_t(high, wr[...]) + mm_t(low, wr[...])) + ct * to_n2
            dn2 = dn2 * gain
            back = r * dn2 - h1 * (r * r * r * jnp.mean(dn2 * h1, axis=1, keepdims=True))
            dh1_ref[at, :] = ct + back
            return carry

        lax.fori_loop(0, length // 256, combine, 0)


def experts_both_ways(adapter, xb, h1, lin, cot, routes, carried, gain_m, wr, vectors, w_gu, w_dn, gu_down, gu_up, dn_down, dn_up):
    length, width = xb.shape
    experts, hidden = w_dn.shape[0], w_dn.shape[1]
    tile = hidden // 2
    tiles = hidden // tile
    most = 2 * length + experts * 128
    total = 3 * width + 3 * hidden
    smem = pl.BlockSpec(memory_space=pltpu.SMEM)

    def whole(a):
        return pl.BlockSpec(a.shape, lambda e, j: (0,) * a.ndim, pipeline_mode=pl.Buffered(1))

    resident = (xb, h1, lin, cot, routes, carried, gain_m, wr, vectors)
    return pl.pallas_call(
        experts_kernel,
        grid=(experts, tiles),
        out_shape=[
            jax.ShapeDtypeStruct((length, width), BF),
            jax.ShapeDtypeStruct((length, width), F32),
            jax.ShapeDtypeStruct((experts, RANK, total), BF),
        ],
        in_specs=[smem]
        + [whole(a) for a in resident]
        + [
            pl.BlockSpec((1, width, tile), lambda e, j: (e, 0, j)),
            pl.BlockSpec((1, width, tile), lambda e, j: (e, 0, tiles + j)),
            pl.BlockSpec((1, tile, width), lambda e, j: (e, j, 0)),
            pl.BlockSpec((1, 2, width, 128), lambda e, j: (e, 0, 0, 0)),
            pl.BlockSpec((1, 2, 128, tile), lambda e, j: (e, 0, 0, j)),
            pl.BlockSpec((1, tile, 128), lambda e, j: (e, j, 0)),
            pl.BlockSpec((1, 128, width), lambda e, j: (e, 0, 0)),
        ],
        out_specs=[
            pl.BlockSpec((length, width), lambda e, j: (0, 0), pipeline_mode=pl.Buffered(1)),
            pl.BlockSpec((length, width), lambda e, j: (0, 0), pipeline_mode=pl.Buffered(1)),
            pl.BlockSpec((1, RANK, total), lambda e, j: (e, 0, 0)),
        ],
        scratch_shapes=[
            pltpu.SMEM((2, experts + 1), jnp.int32),
            pltpu.VMEM((length, 128), F32),
            pltpu.VMEM((128, length), F32),
            pltpu.VMEM((length, 128), F32),
            pltpu.VMEM((128, length), F32),
            pltpu.VMEM((most + HALF, 2 * width + 128), BF),
            pltpu.VMEM((512, width), BF),
            pltpu.VMEM((512, width), BF),
            pltpu.VMEM((512, width), BF),
            pltpu.VMEM((512, 128), F32),
            pltpu.VMEM((512, width), F32),
            pltpu.VMEM((512, width), F32),
            pltpu.VMEM((512, 128), BF),
            pltpu.VMEM((512, 128), F32),
            pltpu.VMEM((512, 128), BF),
            pltpu.VMEM((512, 128), F32),
            pltpu.VMEM((width, 128), BF),
            pltpu.VMEM((128, width), BF),
            pltpu.VMEM((256, 2 * width + 128), F32),
        ],
        compiler_params=pltpu.CompilerParams(vmem_limit_bytes=60 * MIB),
        name="experts_both_ways",
    )(adapter, *resident, w_gu, w_gu, w_dn, gu_down, gu_up, dn_down, dn_up)


def gather_experts(arrays):
    return [lax.all_gather(a, "expert", axis=0, tiled=True) for a in arrays]


def sum_expert_maps(compact, senders):
    groups = lax.axis_size("expert")
    mine = compact.reshape(groups, -1, *compact.shape[1:])[:, 0]
    got = lax.all_to_all(mine, "expert", split_axis=0, concat_axis=0, tiled=True)
    rows = got.reshape(groups * RANK, -1)
    to = (senders[:, None] * RANK + jnp.arange(RANK)[None, :]).reshape(-1)
    spread = (jnp.arange(128)[:, None] == to[None, :]).astype(BF)
    return lax.psum(mm(spread, rows).astype(BF), "dp").astype(F32)


def sum_attention_maps(compact, adapter):
    maps, _, width = compact.shape
    dense = lax.dynamic_update_slice(jnp.zeros((maps, 128, width), BF), compact, (0, adapter * RANK, 0))
    return lax.psum(dense, ("dp", "expert")).astype(F32)


def body(
    tokens, cotangent, attention_norm_gain, query_key_value_weight, attention_output_weight,
    adapter_attention_down_maps, adapter_query_key_value_up_maps, adapter_output_up_map,
    experts_norm_gain, router_weight, constant_expert_mixing, constant_expert_vectors,
    expert_gate_up_weight, expert_down_weight, adapter_expert_gate_up_down_maps, adapter_expert_gate_up_up_maps,
    adapter_expert_down_down_maps, adapter_expert_down_up_maps,
    routes, router_logits_carried, picture_span_starts, sequence_adapter_index,
):
    groups = lax.axis_size("expert")
    width = tokens.shape[1]
    hidden = expert_down_weight.shape[1]
    first = lax.axis_index("dp") * groups
    senders = lax.dynamic_slice_in_dim(sequence_adapter_index, first, groups, 0)
    adapter = lax.dynamic_slice_in_dim(senders, lax.axis_index("expert"), 1, 0)
    gain_a, gain_m = attention_norm_gain[None], experts_norm_gain[None]
    spans = picture_span_starts.reshape(-1)
    router = jnp.concatenate([router_weight, constant_expert_mixing], axis=1)
    router = jnp.pad(router, ((0, 0), (0, 128 - router.shape[1])))
    weights = gather_experts([
        expert_gate_up_weight, expert_down_weight, adapter_expert_gate_up_down_maps,
        adapter_expert_gate_up_up_maps, adapter_expert_down_down_maps, adapter_expert_down_up_maps,
    ])
    xa, q, k, v, ob, ua, uo, lse, h1, xb, lin, wqk, down_s, up_s = attention_forward(
        tokens, gain_a, query_key_value_weight, adapter_attention_down_maps, adapter_query_key_value_up_maps,
        attention_output_weight, adapter_output_up_map, gain_m, router, spans, adapter,
    )
    result, dh1, expert_maps = experts_both_ways(
        adapter, xb, h1, lin, cotangent, routes, router_logits_carried, gain_m, router, constant_expert_vectors, *weights
    )
    grad_tokens, attention_maps = attention_backward(
        spans, dh1, tokens, gain_a, query_key_value_weight, wqk, attention_output_weight, down_s, up_s,
        xa, q, k, v, ob, ua, uo, lse,
    )
    of_expert = sum_expert_maps(expert_maps, senders)
    of_attention = sum_attention_maps(attention_maps, adapter[0])
    cuts = [width, 2 * width, 2 * width + hidden, 2 * width + 2 * hidden, 2 * width + 3 * hidden]
    gud0, gud1, guu0, guu1, dnd, dnu = jnp.split(of_expert, cuts, axis=1)
    return (
        result,
        grad_tokens,
        of_attention[:4].transpose(0, 2, 1),
        of_attention[4:7],
        of_attention[7],
        jnp.stack([gud0.T, gud1.T])[None],
        jnp.stack([guu0, guu1])[None],
        dnd.T[None],
        dnu[None],
    )


def solution(mesh):
    tokens, own = P(("dp", "expert"), None), P("expert", None, None)
    own4 = P("expert", None, None, None)
    in_specs = (tokens, tokens) + (P(),) * 10 + (own, own, own4, own4, own, own) + (tokens,) * 3 + (P(),)
    out_specs = (tokens, tokens, P(), P(), P(), own4, own4, own, own)
    return jax.shard_map(body, mesh=mesh, in_specs=in_specs, out_specs=out_specs, check_vma=False)
```

time: 1110 us -> 772 us (0.70)
  matrix products: 418 us -> 2.07 us
  waiting for transfers between devices: 227 us -> 503 us
  local copies, waits for them, and re-layouts: 226 us -> 19.1 us
  Pallas kernels: 0 us -> 206 us
  other arithmetic: 195 us -> 6.12 us
  starting transfers between devices: 19.7 us -> 5.86 us
  blocking collectives: 0 us -> 12.4 us
    dot_general x41 -> x1, matrix products: 418 us -> 2.07 us  [mm(): return jnp.dot(a, b, preferred_element_type=F32)]
    all_gather x0 -> x5, waiting for transfers between devices: none -> 262 us  [gather_experts(): return [lax.all_gather(a, 'expert', axis=0, tiled=True) for a in arrays]]
    pallas_call x0 -> x3, Pallas kernels: none -> 206 us  [the longest x1 108 us: experts_both_ways(): pl.pallas_call(experts_kernel, grid=(experts, tiles), out_shape=[jax.Shap...]
    reduce_sum x13 -> x0, other arithmetic: 120 us -> none  [the longest x1 48.7 us: mix_experts(): return jnp.sum(gates[:, :, None] * (gathered + copied + fixed_out), axis=1)]
    unnamed x200 -> x25, local copies, waits for them, and re-layouts: 41.2 us -> 10.7 us
    convert_element_type x5 -> x0, local copies, waits for them, and re-layouts: 28.3 us -> none  [the longest x1 7.81 us: body(): from_slots(grad_back).astype(jnp.float32)]
    gather x2 -> x0, local copies, waits for them, and re-layouts: 25.3 us -> none  [from_slots(): return padded[places].reshape(length, 2, width)]
    slice x7 -> x1, local copies, waits for them, and re-layouts: 26.4 us -> 2.17 us  [body(): of_attention[4:7]]
  transfers between devices with their start and end apart: 6 -> 8, of which waited for: 3 -> 5; matrix products, arithmetic and copies ran while one was open for 26% -> 2% of each run, Pallas kernels for 0% -> 13%
where the time goes in v1:
time: 772 us; the launch traced here: 769 us
  waiting for transfers between devices  503 us (65%)
  Pallas kernels  206 us (27%)
  local copies, waits for them, and re-layouts  19.1 us (2%)
  between operations  15.2 us (2%)
  blocking collectives  12.4 us (2%)
    all_gather x5, waiting for transfers between devices, gather_experts(): return [lax.all_gather(a, 'expert', axis=0, tiled=True) for a in arrays]  262 us
    psum x1, waiting for transfers between devices, sum_attention_maps(): return lax.psum(dense, ('dp', 'expert')).astype(F32)  141 us
    pallas_call x1, Pallas kernels, experts_both_ways(): pl.pallas_call(experts_kernel, grid=(experts, tiles), out_shape=[jax.Shap...  108 us
    psum x1, waiting for transfers between devices, sum_expert_maps(): return lax.psum(mm(spread, rows).astype(BF), 'dp').astype(F32)  96.6 us
    pallas_call x1, Pallas kernels, attention_backward(): pl.pallas_call(attention_backward_kernel, out_shape=[jax.ShapeDtypeStruct...  52.5 us
    pallas_call x1, Pallas kernels, attention_forward(): pl.pallas_call(attention_forward_kernel, out_shape=[jax.ShapeDtypeStruct(...  44.8 us
  transfers between devices with their start and end apart: 8, of which 5 were waited for; matrix products, arithmetic and copies ran while one was open for 2% of the time, Pallas kernels for 13%

profile of v1, /device:TPU:0, one launch (start us, length us, event | category | flops | bytes accessed | tf_op | source)
XLA Modules:
  0.0 769.3 jit_solution(5425154261556920899)
XLA Ops:
  12.1 1.0 copy.43.routes
  13.1 1.0 copy.44.carried
  15.5 44.8 %attention_forward.1 = (bf16[1024,768]{1,0:T(8,128)(2,1)}, bf16[1024,768]{1,0:T(8,128)(2,1)}, bf16[1024,768]{1,0:T(8,128)(2,1)}, bf16[1024,768]{1,0:T(8,128)(2,1...) custom-call(s32[2]{0:T(128)} %bitcast.31, ...), custom_call_target="tpu_custom_call" | custom-call | tf_op jit(solution)/shard_map/attention_forward/pallas_call | solution.py:200
  60.3 12.4 %all_gather.23.dn_up = bf16[4,128,768]{2,1,0:T(8,128)(2,1)} all-gather(bf16[1,128,768]{2,1,0:T(8,128)(2,1)S(1)} %copy-done.2), channel_id=1, replica_groups=mesh['dp'=8,'expert'=4] {'expert'}, dimensions={0}, use_global_device_ids=true | all-gather | bytes 983040 | tf_op jit(solution)/shard_map/all_gather | solution.py:609
  72.6 21.1 %all-gather.12.cloned.1.call-done.gu_up = bf16[4,2,128,2048]{3,2,1,0:T(8,128)(2,1)} async-done(((bf16[1,2,128,2048]{3,2,1,0:T(8,128)(2,1)}), bf16[4,2,128,2048]{3,2,1,0:T(8,128)(2,1)}) %all-gather.12.cloned.1.call-update) | async-done | bytes 4194320 | tf_op jit(solution)/shard_map/all_gather | solution.py:609
  93.8 84.4 %all-gather.8.cloned.1.call-done.w_down = bf16[4,2048,768]{2,1,0:T(8,128)(2,1)} async-done(((bf16[1,2048,768]{2,1,0:T(8,128)(2,1)}), bf16[4,2048,768]{2,1,0:T(8,128)(2,1)}) %all-gather.8.cloned.1.call-update) | async-done | bytes 12582928 | tf_op jit(solution)/shard_map/all_gather | solution.py:609
  178.2 156.3 %all-gather.6.cloned.1.call-done.w_gate.w_up = bf16[4,768,4096]{2,1,0:T(8,128)(2,1)} async-done(((bf16[1,768,4096]{2,1,0:T(8,128)(2,1)}), bf16[4,768,4096]{2,1,0:T(8,128)(2,1)}) %all-gather.6.cloned.1.call-update) | async-done | bytes 25165840 | tf_op jit(solution)/shard_map/all_gather | solution.py:609
  334.4 108.5 %experts_both_ways.1 = (bf16[1024,768]{1,0:T(8,128)(2,1)}, f32[1024,768]{1,0:T(8,128)}, bf16[4,16,8448]{2,1,0:T(8,128)(2,1)}) custom-call(s32[1]{0:T(128)} %dynamic_slice.9.adapter_ref, bf16[1024,768]{1,0:T(8,128)(2,1)} %get-tuple-element.28.xb, f32[1024,768]{1,0:T(8,128)} %get-tuple-element.29.h1_ref, f32[1024,128]{1,0:T(8,128)} %get-tuple-element.30.lin_ref, ...), custom_call_target="tpu_custom_call" | custom-call | tf_op jit(solution)/shard_map/experts_both_ways/pallas_call | solution.py:558
  442.9 5.6 all-to-all-start
  449.3 52.5 %attention_backward.1 = (bf16[1024,768]{1,0:T(8,128)(2,1)}, bf16[8,16,768]{2,1,0:T(8,128)(2,1)}) custom-call(s32[2]{0:T(128)} %bitcast.32, f32[1024,768]{1,0:T(8,128)} %get-tuple-element.32.dh1_ref, bf16[1024,768]{1,0:T(8,128)(2,1)} %tok.3, f32[1,768]{1,0:T(1,128)} %broadcast_in_dim.24.gain_a, bf16[768,2304]{1,0:T(8,128)(2,1)} %wqkv.3, ...), custom_call_target="tpu_custom_call" | custom-call | tf_op jit(solution)/shard_map/attention_backward/pallas_call | solution.py:312
  502.7 1.1 copy-done
  504.2 2.1 convolution_convert_fusion
  506.2 141.4 %all-reduce.4.cloned.1.call-done = bf16[8,128,768]{2,1,0:T(8,128)(2,1)} async-done(((bf16[8,128,768]{2,1,0:T(8,128)(2,1)}), bf16[8,128,768]{2,1,0:T(8,128)(2,1)}) %all-reduce.4.cloned.1.call-update) | async-done | bytes 1572880 | tf_op jit(solution)/shard_map/psum | solution.py:625
  647.6 1.7 convert_element_type.12
  649.3 1.3 slice_bitcast_fusion
  650.6 3.0 copy.45
  653.6 2.2 slice.13
  656.6 96.6 %all-reduce.6.cloned.1.call-done = bf16[128,8448]{1,0:T(8,128)(2,1)} async-done(((bf16[128,8448]{1,0:T(8,128)(2,1)}), bf16[128,8448]{1,0:T(8,128)(2,1)}) %all-reduce.6.cloned.1.call-update) | async-done | bytes 2162704 | tf_op jit(solution)/shard_map/psum | solution.py:619
  753.1 1.9 convert_element_type.14
  755.4 0.8 slice_bitcast_fusion.4
  756.3 0.9 maximum_bitcast_fusion.1
  757.2 2.3 copy.46
  759.5 1.3 copy.47
  760.8 1.5 maximum_bitcast_fusion
  (49 shorter events, 8.5 us)
Async XLA Ops:
  7.2 65.5 %all-gather.10.cloned.1.call-start = ((), (), s32[]{:S(2)}) async-start(), calls=%async_computation.3 | async-start | bytes 1966080 | tf_op jit(solution)/shard_map/all_gather | solution.py:609
  7.9 64.7 %all-gather.14.cloned.1.call-start = ((), (), s32[]{:S(2)}) async-start(), calls=%async_computation.5 | async-start | bytes 2621440 | tf_op jit(solution)/shard_map/all_gather | solution.py:609
  8.7 85.1 %all-gather.12.cloned.1.call-start = ((), (), s32[]{:S(2)}) async-start(), calls=%async_computation.4 | async-start | bytes 5242880 | tf_op jit(solution)/shard_map/all_gather | solution.py:609
  9.4 168.8 %all-gather.8.cloned.1.call-start = ((), (), s32[]{:S(2)}) async-start(), calls=%async_computation.2 | async-start | bytes 15728640 | tf_op jit(solution)/shard_map/all_gather | solution.py:609
  10.0 0.7 copy-start.4
  10.0 0.7 copy-start.6
  10.0 0.9 copy-start.7
  10.0 1.5 copy-start.8
  10.0 2.1 copy-start.5
  10.0 3.1 copy-start.3
  10.0 4.1 copy-start.9
  10.0 324.4 %all-gather.6.cloned.1.call-start = ((), (), s32[]{:S(2)}) async-start(), calls=%async_computation.1 | async-start | bytes 31457280 | tf_op jit(solution)/shard_map/all_gather | solution.py:609
  15.5 44.8 %copy-start.2 = (bf16[1,128,768]{2,1,0:T(8,128)(2,1)S(1)}, bf16[1,128,768]{2,1,0:T(8,128)(2,1)}, u32[]{:S(2)}) copy-start(bf16[1,128,768]{2,1,0:T(8,128)(2,1)} %param.43) | copy-start | bytes 589828
  442.9 61.2 %all-to-all-start = ((bf16[4,16,8448]{2,1,0:T(8,128)(2,1)}), bf16[4,16,8448]{2,1,0:T(8,128)(2,1)S(1)}, u32[]{:S(2)}, u32[]{:S(2)}) async-start(bf16[4,16,8448]{2,1,0:T(8,128)(2,1)} %get-tuple-element.46), calls=%async_computation | async-start | bytes 2162688 | tf_op jit(solution)/shard_map/all_to_all | solution.py:615
  448.6 199.1 %all-reduce.4.cloned.1.call-start = ((), (), s32[]{:S(2)}) async-start(), calls=%async_computation.6 | async-start | bytes 3145728 | tf_op jit(solution)/shard_map/psum | solution.py:625
  501.7 0.9 copy-start.1
  502.7 1.1 copy-start
  503.9 249.3 %all-reduce.6.cloned.1.call-start = ((), (), s32[]{:S(2)}) async-start(), calls=%async_computation.7 | async-start | bytes 4325376 | tf_op jit(solution)/shard_map/psum | solution.py:619
Sparse Core Ops, SparseCore 0:
  9.6 22.3 all-gather.9
  33.5 22.5 all-gather.13
  57.7 36.0 all-gather.11
  95.2 82.9 all-gather.7
  179.6 154.8 all-gather.5
  504.0 143.6 all-reduce.3
  651.2 101.8 all-reduce.5

commit v2 on v1

--- a/solution.py
+++ b/solution.py
@@ -76,15 +76,187 @@
     return jnp.where((key <= query) | inside, 0.0, NEG)
 
 
-def attention_forward_kernel(
-    spans, adapter_ref, tok, gain_a, wqkv, down, up, wo, up_out, gain_m, wr, cos, sin,
-    xa_ref, q_ref, k_ref, v_ref, ob_ref, ua_ref, uo_ref, lse_ref, h1_ref, xb_ref, lin_ref, wqk_ref,
-    down_ref, up_s,
-    bias,
-):
+UNITS = 32
+CHUNKS = ((0, 1), (1, 2), (3, 1), (4, 2))
+EXTRA = ((0, 2), (2, 2))
+MESH = pl.DeviceIdType.MESH
+
+
+def other(index, step):
+    return index + step - 2 * step * ((index // step) % 2)
+
+
+def sending_steps(own, outs, scratch):
+    senders, w_gu, w_dn, gu_down, gu_up, dn_down, dn_up = own
+    all_gu, all_dn, all_maps = outs
+    bounce_gu, bounce_dn, compact, send, recv, local = scratch
+    sources, targets, bounce = (w_gu, w_dn), (all_gu, all_dn), (bounce_gu, bounce_dn)
+    dp, ex = lax.axis_index("dp"), lax.axis_index("expert")
+    sibling, far = other(ex, 1), other(ex, 2)
+    peers = {
+        "x": (other(dp, 1), ex), "z": (other(dp, 2), ex), "y": (dp, far), "s": (dp, sibling), "d": (dp, other(far, 1)),
+    }
+    x, z = dp % 2, (dp // 2) % 2
+    quarter = {"y": z * 2 + x, "x": z * 2 + 1 - x, "z": (1 - z) * 2 + x, "d": (1 - z) * 2 + 1 - x}
+    kind = (x + z) % 2
+    slots = {}
+    for name in ("y", "x", "z", "d"):
+        for chunk in CHUNKS:
+            slots[name, chunk] = len(slots)
+    for name in ("e", "o"):
+        for chunk in EXTRA:
+            slots[name, chunk] = len(slots)
+    count = len(slots)
+    started = []
+
+    def views(refs, expert, key):
+        name, (first, number) = key
+        if name in quarter:
+            first = quarter[name] * 6 + first
+        else:
+            first = 24 + 4 * (kind if name == "e" else 1 - kind) + first
+        columns, rows = refs[0].shape[-1] // UNITS, refs[1].shape[-2] // UNITS
+        return (
+            refs[0].at[expert, :, pl.ds(pl.multiple_of(first * columns, columns), number * columns)],
+            refs[1].at[expert, pl.ds(pl.multiple_of(first * rows, rows), number * rows), :],
+        )
+
+    def copies(source, target, peer, slot):
+        for i in range(len(source())):
+            number = len(started)
+
+            def made(i=i, number=number):
+                return pltpu.make_async_remote_copy(
+                    src_ref=source()[i], dst_ref=target()[i], send_sem=send.at[number], recv_sem=recv.at[slot, i],
+                    device_id=peers[peer], device_id_type=MESH,
+                )
+
+            made().start()
+            started.append(made)
+
+    def arrived(view, slot, i):
+        pltpu.make_async_remote_copy(
+            src_ref=view, dst_ref=view, send_sem=send.at[0], recv_sem=recv.at[slot, i],
+            device_id=peers["s"], device_id_type=MESH,
+        ).wait_recv()
+
+    def begin():
+        barrier = pltpu.get_barrier_semaphore()
+        for peer in peers.values():
+            pl.semaphore_signal(barrier, inc=1, device_id=peer, device_id_type=MESH)
+        pl.semaphore_wait(barrier, len(peers))
+        for name, chunks in (("y", CHUNKS), ("e", EXTRA)):
+            for chunk in chunks:
+                key = name, chunk
+                copies(
+                    functools.partial(views, sources, 0, key), functools.partial(views, targets, ex, key), "y", slots[key]
+                )
+        copies(lambda: [s.at[0] for s in sources], lambda: [t.at[ex] for t in targets], "s", 2 * count)
+        for i in range(2):
+            pltpu.make_async_copy(sources[i].at[0], bounce[i], local.at[i]).start()
+
+    def select():
+        row, column = iota((64, 128), 0), iota((64, 128), 1)
+        first = sum(jnp.where(row // RANK == i, senders[i], 0) for i in range(4))
+        rows = one_hot(column == first * RANK + row % RANK)
+        width, hidden = gu_down.shape[2], dn_down.shape[1]
+        parts = [
+            (0, mm_t(rows, gu_down[0, 0])),
+            (width, mm_t(rows, gu_down[0, 1])),
+            (2 * width, mm(rows, gu_up[0, 0])),
+            (2 * width + hidden, mm(rows, gu_up[0, 1])),
+            (2 * width + 2 * hidden, mm_t(rows, dn_down[0])),
+            (2 * width + 3 * hidden, mm(rows, dn_up[0])),
+        ]
+        for at, part in parts:
+            for i in range(4):
+                compact[i, :, pl.ds(at, part.shape[1])] = part[i * RANK : (i + 1) * RANK].astype(BF)
+        for i, (peer, to) in enumerate((("s", sibling), ("y", far), ("d", other(far, 1)))):
+            copies(lambda to=to: [compact.at[to]], lambda: [all_maps.at[ex]], peer, 2 * count + 1 + i)
+        pltpu.make_async_copy(compact.at[ex], all_maps.at[ex], local.at[2]).start()
+
+    def turn():
+        for i in range(2):
+            pltpu.make_async_copy(sources[i].at[0], bounce[i], local.at[i]).wait()
+            pltpu.make_async_copy(bounce[i], targets[i].at[ex], local.at[i]).start()
+
+    along_x = (CHUNKS[0], CHUNKS[3])
+
+    def got(name, chunk):
+        key = name, chunk
+        to = []
+        if name == "y":
+            to = [("x", slots["x", chunk]), ("z", slots["z", chunk])]
+        if name == "x" and chunk not in along_x:
+            to = [("z", slots["d", chunk])]
+        if name == "z" and chunk in along_x:
+            to = [("x", slots["d", chunk])]
+        if name == "e":
+            to = [("x" if chunk == EXTRA[0] else "z", slots["o", chunk])]
+
+        def step():
+            mine = functools.partial(views, targets, far, key)
+            for i in range(2):
+                arrived(mine()[i], slots[key], i)
+            for peer, slot in to:
+                copies(mine, mine, peer, slot)
+            copies(mine, mine, "s", count + slots[key])
+
+        return step
+
+    def end():
+        for made in started:
+            made().wait_send()
+        for i in range(2):
+            pltpu.make_async_copy(bounce[i], targets[i].at[ex], local.at[i]).wait()
+            arrived(targets[i].at[sibling], 2 * count, i)
+        pltpu.make_async_copy(compact.at[ex], all_maps.at[ex], local.at[2]).wait()
+        for i, source in enumerate((sibling, far, other(far, 1))):
+            arrived(all_maps.at[source], 2 * count + 1 + i, 0)
+        for key, slot in slots.items():
+            view = views(targets, other(far, 1), key)
+            for i in range(2):
+                arrived(view[i], count + slot, i)
+
+    c, e = CHUNKS, EXTRA
+    return {
+        "begin": [begin, select],
+        "ready": [turn],
+        "projected": [got("y", c[0])],
+        2: [got("x", c[0]), got("z", c[0])],
+        4: [got("y", c[1])],
+        6: [got("y", c[2]), got("d", c[0])],
+        9: [got("x", c[1]), got("z", c[1])],
+        "end": [
+            got("y", c[3]), got("x", c[2]), got("z", c[2]), got("e", e[0]), got("x", c[3]), got("z", c[3]), got("e", e[1]),
+            got("d", c[1]), got("d", c[2]), got("o", e[0]), got("d", c[3]), got("o", e[1]), end,
+        ],
+    }
+
+
+def attention_forward_kernel(exchange, *refs):
+    spans, adapter_ref, tok, gain_a, wqkv, down, up, wo, up_out, gain_m, wr, cos, sin = refs[:13]
+    refs = refs[13:]
+    own = ()
+    if exchange:
+        own, refs = refs[:7], refs[7:]
+    xa_ref, q_ref, k_ref, v_ref, ob_ref, ua_ref, uo_ref, lse_ref, h1_ref, xb_ref, lin_ref, wqk_ref, down_ref, up_s = refs[:14]
+    refs = refs[14:]
+    steps = {}
+    if exchange:
+        steps = sending_steps(own, refs[:3], refs[4:])
+        bias = refs[3]
+    else:
+        (bias,) = refs
     length, width = tok.shape
     groups = width // GROUP
     adapter = adapter_ref[0]
+
+    def run(point):
+        for step in steps.get(point, ()):
+            step()
+
+    run("begin")
     order = head_order(False)
     down_s = sum(mm(down[p], picker(adapter, p)) for p in range(3)).astype(BF)
     down_o = mm(down[3], picker(adapter, 0)).astype(BF)
@@ -104,6 +276,7 @@
         wqk_ref[:, at] = mm(wqkv[:, at], order).astype(BF)
     for half in range(length // HALF):
         bias[half] = span_bias(spans[half] - half * HALF, False)
+    run("ready")
 
     def project(block, carry):
         at = pl.ds(pl.multiple_of(block * 256, 256), 256)
@@ -124,6 +297,7 @@
         return carry
 
     lax.fori_loop(0, length // 256, project, 0)
+    run("projected")
 
     lane = iota((1, GROUP), 1)
     lse_ref[...] = jnp.zeros(lse_ref.shape, F32)
@@ -157,6 +331,9 @@
             lse_ref[at, :] = jnp.where(iota((1, 128), 1) == head, lse, lse_ref[at, :])
             old = jnp.where(v_own > 0.5, 0.0, ob_f[at, lanes].astype(F32))
             ob_f[at, lanes] = jnp.where(v_own > 0.5, o, old).astype(BF)
+        for point in steps:
+            if isinstance(point, int):
+                pl.when(head == point)(functools.partial(run, point))
         return carry
 
     lax.fori_loop(0, HEADS, attend, 0)
@@ -175,9 +352,10 @@
         return carry
 
     lax.fori_loop(0, length // 256, finish, 0)
-
-
-def attention_forward(tok, gain_a, wqkv, down, up, wo, up_out, gain_m, wr, spans, adapter):
+    run("end")
+
+
+def attention_forward(tok, gain_a, wqkv, down, up, wo, up_out, gain_m, wr, spans, adapter, own=(), senders=None):
     length, width = tok.shape
     cos, sin = rope_tables(length)
     shapes = [
@@ -197,15 +375,36 @@
         ((128, 4 * width), BF),
     ]
     vmem, smem = pl.BlockSpec(memory_space=pltpu.VMEM), pl.BlockSpec(memory_space=pltpu.SMEM)
+    anys = pl.BlockSpec(memory_space=pl.ANY)
+    in_specs, out_specs = [smem, smem] + [vmem] * 11, [vmem] * len(shapes)
+    scratch = [pltpu.VMEM((length // HALF, HALF, HALF), F32)]
+    params = dict(vmem_limit_bytes=60 * MIB)
+    args = (spans, adapter, tok, gain_a, wqkv, down, up, wo, up_out, gain_m, wr, cos, sin)
+    if own:
+        w_gu, w_dn = own[:2]
+        columns = 3 * width + 3 * w_dn.shape[1]
+        in_specs += [smem, anys, anys] + [vmem] * 4
+        args += (senders, *own)
+        shapes += [((4, *w_gu.shape[1:]), BF), ((4, *w_dn.shape[1:]), BF), ((4, RANK, columns), BF)]
+        out_specs += [anys] * 3
+        scratch += [
+            pltpu.VMEM(w_gu.shape[1:], BF),
+            pltpu.VMEM(w_dn.shape[1:], BF),
+            pltpu.VMEM((4, RANK, columns), BF),
+            pltpu.SemaphoreType.DMA((96,)),
+            pltpu.SemaphoreType.DMA((48, 2)),
+            pltpu.SemaphoreType.DMA((3,)),
+        ]
+        params.update(collective_id=0, has_side_effects=True)
     return pl.pallas_call(
-        attention_forward_kernel,
+        functools.partial(attention_forward_kernel, bool(own)),
         out_shape=[jax.ShapeDtypeStruct(s, t) for s, t in shapes],
-        in_specs=[smem, smem] + [vmem] * 11,
-        out_specs=[vmem] * len(shapes),
-        scratch_shapes=[pltpu.VMEM((length // HALF, HALF, HALF), F32)],
-        compiler_params=pltpu.CompilerParams(vmem_limit_bytes=56 * MIB),
+        in_specs=in_specs,
+        out_specs=out_specs,
+        scratch_shapes=scratch,
+        compiler_params=pltpu.CompilerParams(**params),
         name="attention_forward",
-    )(spans, adapter, tok, gain_a, wqkv, down, up, wo, up_out, gain_m, wr, cos, sin)
+    )(*args)
 
 
 def attention_backward_kernel(
@@ -341,8 +540,8 @@
 
 
 def experts_kernel(
-    adapter_ref, xb, h1_ref, lin_ref, cot, routes, carried, gain_m, wr, vectors,
-    w_gate, w_up, w_down, gu_down, gu_up, dn_down, dn_up,
+    xb, h1_ref, lin_ref, cot, routes, carried, gain_m, wr, vectors,
+    w_gate, w_up, w_down, maps,
     result, dh1_ref, grads,
     count, gates, gates_t, place, place_t, both, x_s, c_s, dy_s, g_s, y_acc, dx_acc, ug_s, ud_acc, dud_s, dug_acc,
     a_gu, b_dn, acc,
@@ -353,10 +552,13 @@
     kinds = carried.shape[1]
     numbers = kinds - 4
     tile = w_gate.shape[2]
-    hidden = grads.shape[2] - 3 * width
-    hidden //= 3
-    adapter = adapter_ref[0]
+    hidden = (grads.shape[2] - 3 * width) // 3
     rows_of = 128
+
+    def padded_rows(start, number, before=0):
+        part = maps[0, :, pl.ds(start, number)]
+        parts = [jnp.zeros((before, number), BF), part, jnp.zeros((128 - RANK - before, number), BF)]
+        return jnp.concatenate(parts if before else parts[1:], axis=0)
 
     @pl.when((e == 0) & (j == 0))
     def _():
@@ -397,8 +599,8 @@
 
     @pl.when((j == 0) & (blocks > 0))
     def _():
-        a_gu[...] = (mm(gu_down[0, 0], picker(adapter, 0)) + mm(gu_down[0, 1], picker(adapter, 1))).astype(BF)
-        b_dn[...] = mm(placer(adapter, 0), dn_up[0]).astype(BF)
+        a_gu[...] = padded_rows(0, width) + padded_rows(width, width, RANK)
+        b_dn[...] = padded_rows(2 * width + 3 * hidden, width)
 
     @pl.when((j == 0) & (blocks == 0))
     def _():
@@ -419,26 +621,26 @@
             c_s[rows, :] = c
             dy_s[rows, :] = dy
             g_s[rows, :] = jnp.broadcast_to(g, (n, 128))
-            ug_s[rows, :] = mm(x, a_gu[...]).astype(BF)
+            ug_s[rows, :] = mm_t(x, a_gu[...]).astype(BF)
             dud_s[rows, :] = mm_t(dy, b_dn[...]).astype(BF)
 
         x, dy, ug, dud = x_s[rows, :], dy_s[rows, :], ug_s[rows, :], dud_s[rows, :]
-        b_gate = mm(placer(adapter, 0), gu_up[0, 0]).astype(BF)
-        b_up = mm(placer(adapter, 1), gu_up[0, 1]).astype(BF)
-        a_dn = mm(dn_down[0], picker(adapter, 0)).astype(BF)
+        at = pl.multiple_of(j * tile, tile)
+        b_gate = padded_rows(2 * width + at, tile)
+        b_up = padded_rows(2 * width + hidden + at, tile, RANK)
+        a_dn = padded_rows(2 * width + 2 * hidden + at, tile)
         gate = mm(x, w_gate[0]) + mm(ug, b_gate)
         up = mm(x, w_up[0]) + mm(ug, b_up)
         sig = 1.0 / (1.0 + jnp.exp(-gate))
         act = gate * sig
         hid = (act * up).astype(BF)
-        dhid = mm_t(dy, w_down[0]) + mm_t(dud, a_dn)
+        dhid = mm_t(dy, w_down[0]) + mm(dud, a_dn)
         dup = (dhid * act).astype(BF)
         dgate = (dhid * up * (sig + act * (1.0 - sig))).astype(BF)
         y = mm(hid, w_down[0])
-        ud = mm(hid, a_dn)
+        ud = mm_t(hid, a_dn)
         dx = mm_t(dgate, w_gate[0]) + mm_t(dup, w_up[0])
         dug = mm_t(dgate, b_gate) + mm_t(dup, b_up)
-        at = pl.multiple_of(j * tile, tile)
         ug_t = ug.T
         grads[0, :, pl.ds(2 * width + at, tile)] = mm(ug_t[:RANK], dgate).astype(BF)
         grads[0, :, pl.ds(2 * width + hidden + at, tile)] = mm(ug_t[RANK : 2 * RANK], dup).astype(BF)
@@ -469,7 +671,7 @@
             lane = iota((1, 128), 1)
             to = pl.ds(first, n)
             both[to, :width] = (g * y).astype(BF)
-            both[to, width : 2 * width] = (dx_acc[rows, :] + mm_t(dug, a_gu[...])).astype(BF)
+            both[to, width : 2 * width] = (dx_acc[rows, :] + mm(dug, a_gu[...])).astype(BF)
             both[to, 2 * width :] = jnp.where(
                 lane == e, high.astype(F32), jnp.where(lane == e + 64, low.astype(F32), 0.0)
             ).astype(BF)
@@ -542,14 +744,13 @@
         lax.fori_loop(0, length // 256, combine, 0)
 
 
-def experts_both_ways(adapter, xb, h1, lin, cot, routes, carried, gain_m, wr, vectors, w_gu, w_dn, gu_down, gu_up, dn_down, dn_up):
+def experts_both_ways(xb, h1, lin, cot, routes, carried, gain_m, wr, vectors, w_gu, w_dn, maps):
     length, width = xb.shape
     experts, hidden = w_dn.shape[0], w_dn.shape[1]
     tile = hidden // 2
     tiles = hidden // tile
     most = 2 * length + experts * 128
     total = 3 * width + 3 * hidden
-    smem = pl.BlockSpec(memory_space=pltpu.SMEM)
 
     def whole(a):
         return pl.BlockSpec(a.shape, lambda e, j: (0,) * a.ndim, pipeline_mode=pl.Buffered(1))
@@ -563,16 +764,12 @@
             jax.ShapeDtypeStruct((length, width), F32),
             jax.ShapeDtypeStruct((experts, RANK, total), BF),
         ],
-        in_specs=[smem]
-        + [whole(a) for a in resident]
+        in_specs=[whole(a) for a in resident]
         + [
             pl.BlockSpec((1, width, tile), lambda e, j: (e, 0, j)),
             pl.BlockSpec((1, width, tile), lambda e, j: (e, 0, tiles + j)),
             pl.BlockSpec((1, tile, width), lambda e, j: (e, j, 0)),
-            pl.BlockSpec((1, 2, width, 128), lambda e, j: (e, 0, 0, 0)),
-            pl.BlockSpec((1, 2, 128, tile), lambda e, j: (e, 0, 0, j)),
-            pl.BlockSpec((1, tile, 128), lambda e, j: (e, j, 0)),
-            pl.BlockSpec((1, 128, width), lambda e, j: (e, 0, 0)),
+            pl.BlockSpec((1, RANK, total), lambda e, j: (e, 0, 0)),
         ],
         out_specs=[
             pl.BlockSpec((length, width), lambda e, j: (0, 0), pipeline_mode=pl.Buffered(1)),
@@ -596,36 +793,57 @@
             pltpu.VMEM((512, 128), F32),
             pltpu.VMEM((512, 128), BF),
             pltpu.VMEM((512, 128), F32),
-            pltpu.VMEM((width, 128), BF),
+            pltpu.VMEM((128, width), BF),
             pltpu.VMEM((128, width), BF),
             pltpu.VMEM((256, 2 * width + 128), F32),
         ],
         compiler_params=pltpu.CompilerParams(vmem_limit_bytes=60 * MIB),
         name="experts_both_ways",
-    )(adapter, *resident, w_gu, w_gu, w_dn, gu_down, gu_up, dn_down, dn_up)
-
-
-def gather_experts(arrays):
-    return [lax.all_gather(a, "expert", axis=0, tiled=True) for a in arrays]
-
-
-def sum_expert_maps(compact, senders):
-    groups = lax.axis_size("expert")
-    mine = compact.reshape(groups, -1, *compact.shape[1:])[:, 0]
-    got = lax.all_to_all(mine, "expert", split_axis=0, concat_axis=0, tiled=True)
-    rows = got.reshape(groups * RANK, -1)
+    )(*resident, w_gu, w_gu, w_dn, maps)
+
+
+def gather_experts(weights, senders):
+    w_gu, w_dn, gu_down, gu_up, dn_down, dn_up = weights
+    maps = jnp.concatenate(
+        [gu_down[0, 0].T, gu_down[0, 1].T, gu_up[0, 0], gu_up[0, 1], dn_down[0].T, dn_up[0]], axis=1
+    )
     to = (senders[:, None] * RANK + jnp.arange(RANK)[None, :]).reshape(-1)
-    spread = (jnp.arange(128)[:, None] == to[None, :]).astype(BF)
-    return lax.psum(mm(spread, rows).astype(BF), "dp").astype(F32)
-
-
-def sum_attention_maps(compact, adapter):
-    maps, _, width = compact.shape
-    dense = lax.dynamic_update_slice(jnp.zeros((maps, 128, width), BF), compact, (0, adapter * RANK, 0))
-    return lax.psum(dense, ("dp", "expert")).astype(F32)
+    rows = mm((to[:, None] == jnp.arange(128)[None, :]).astype(BF), maps).astype(BF)
+    rows = rows.reshape(senders.shape[0], RANK, -1)
+    return (
+        lax.all_gather(w_gu, "expert", axis=0, tiled=True),
+        lax.all_gather(w_dn, "expert", axis=0, tiled=True),
+        lax.all_to_all(rows, "expert", split_axis=0, concat_axis=0, tiled=True),
+    )
+
+
+BOTH = ("dp", "expert")
+
+
+def sum_expert_maps(compact, spread):
+    copies = lax.axis_size("dp")
+    experts, rank, columns = compact.shape
+    each = -(-columns // (copies * 128)) * 128
+    parts = jnp.pad(compact, ((0, 0), (0, 0), (0, copies * each - columns)))
+    parts = parts.reshape(experts, rank, copies, each).transpose(2, 0, 1, 3).reshape(copies * experts, rank, each)
+    got = lax.all_to_all(parts, BOTH, split_axis=0, concat_axis=0, tiled=True)
+    own = mm(spread, got.reshape(-1, each)).astype(BF)
+    return lax.all_gather(own, "dp", axis=1, tiled=True)
+
+
+def sum_attention_maps(compact, spread):
+    devices = lax.axis_size("dp") * lax.axis_size("expert")
+    maps, rank, width = compact.shape
+    cuts = devices // maps
+    parts = compact.reshape(maps, rank, cuts, width // cuts).transpose(0, 2, 1, 3).reshape(devices, rank, width // cuts)
+    got = lax.all_to_all(parts, BOTH, split_axis=0, concat_axis=0, tiled=True)
+    own = mm(spread, got.reshape(devices * rank, width // cuts)).astype(BF)
+    whole = lax.all_gather(own[None], BOTH, axis=0, tiled=True)
+    return whole.reshape(maps, cuts, 128, width // cuts).transpose(0, 2, 1, 3).reshape(maps, 128, width).astype(F32)
 
 
 def body(
+    exchange,
     tokens, cotangent, attention_norm_gain, query_key_value_weight, attention_output_weight,
     adapter_attention_down_maps, adapter_query_key_value_up_maps, adapter_output_up_map,
     experts_norm_gain, router_weight, constant_expert_mixing, constant_expert_vectors,
@@ -643,23 +861,28 @@
     spans = picture_span_starts.reshape(-1)
     router = jnp.concatenate([router_weight, constant_expert_mixing], axis=1)
     router = jnp.pad(router, ((0, 0), (0, 128 - router.shape[1])))
-    weights = gather_experts([
+    own = (
         expert_gate_up_weight, expert_down_weight, adapter_expert_gate_up_down_maps,
         adapter_expert_gate_up_up_maps, adapter_expert_down_down_maps, adapter_expert_down_up_maps,
-    ])
-    xa, q, k, v, ob, ua, uo, lse, h1, xb, lin, wqk, down_s, up_s = attention_forward(
+    )
+    outs = attention_forward(
         tokens, gain_a, query_key_value_weight, adapter_attention_down_maps, adapter_query_key_value_up_maps,
         attention_output_weight, adapter_output_up_map, gain_m, router, spans, adapter,
+        *((own, senders) if exchange else ()),
     )
+    xa, q, k, v, ob, ua, uo, lse, h1, xb, lin, wqk, down_s, up_s = outs[:14]
+    weights = outs[14:] if exchange else gather_experts(own, senders)
     result, dh1, expert_maps = experts_both_ways(
-        adapter, xb, h1, lin, cotangent, routes, router_logits_carried, gain_m, router, constant_expert_vectors, *weights
+        xb, h1, lin, cotangent, routes, router_logits_carried, gain_m, router, constant_expert_vectors, *weights
     )
     grad_tokens, attention_maps = attention_backward(
         spans, dh1, tokens, gain_a, query_key_value_weight, wqk, attention_output_weight, down_s, up_s,
         xa, q, k, v, ob, ua, uo, lse,
     )
-    of_expert = sum_expert_maps(expert_maps, senders)
-    of_attention = sum_attention_maps(attention_maps, adapter[0])
+    to = (sequence_adapter_index[:, None] * RANK + jnp.arange(RANK)[None, :]).reshape(-1)
+    spread = (jnp.arange(128)[:, None] == to[None, :]).astype(BF)
+    of_expert = sum_expert_maps(expert_maps, spread)[:, : expert_maps.shape[2]].astype(F32)
+    of_attention = sum_attention_maps(attention_maps, spread)
     cuts = [width, 2 * width, 2 * width + hidden, 2 * width + 2 * hidden, 2 * width + 3 * hidden]
     gud0, gud1, guu0, guu1, dnd, dnu = jnp.split(of_expert, cuts, axis=1)
     return (
@@ -680,4 +903,5 @@
     own4 = P("expert", None, None, None)
     in_specs = (tokens, tokens) + (P(),) * 10 + (own, own, own4, own4, own, own) + (tokens,) * 3 + (P(),)
     out_specs = (tokens, tokens, P(), P(), P(), own4, own4, own, own)
-    return jax.shard_map(body, mesh=mesh, in_specs=in_specs, out_specs=out_specs, check_vma=False)
+    exchange = dict(mesh.shape) == {"dp": 8, "expert": 4}
+    return jax.shard_map(functools.partial(body, exchange), mesh=mesh, in_specs=in_specs, out_specs=out_specs, check_vma=False)

time: 772 us -> 431 us (0.56)
  waiting for transfers between devices: 503 us -> 72 us
  Pallas kernels: 206 us -> 256 us
  blocking collectives: 12.4 us -> 36.3 us
    psum x2 -> x0, waiting for transfers between devices: 238 us -> none  [the longest x1 141 us: sum_attention_maps(): return lax.psum(dense, ('dp', 'expert')).astype(F32)]
    all_gather x5 -> x2, waiting for transfers between devices: 262 us -> 61.6 us  [the longest x1 44.7 us: sum_expert_maps(): return lax.all_gather(own, 'dp', axis=1, tiled=True)]
    pallas_call x1, Pallas kernels: 44.8 us -> 108 us  [attention_forward(): pl.pallas_call(functools.partial(attention_forward_kernel, bool(own)), ou...]
    all_to_all x0 -> x1, blocking collectives: none -> 36.3 us  [sum_expert_maps(): got = lax.all_to_all(parts, BOTH, split_axis=0, concat_axis=0, tiled=True)]
    pallas_call x1, Pallas kernels: 108 us -> 95.6 us  [experts_both_ways(): pl.pallas_call(experts_kernel, grid=(experts, tiles), out_shape=[jax.Shap...]
    all_gather x1 -> x0, blocking collectives: 12.4 us -> none  [gather_experts(): return [lax.all_gather(a, 'expert', axis=0, tiled=True) for a in arrays]]
    all_to_all x1, waiting for transfers between devices: 0.01 us -> 10.4 us  [sum_attention_maps(): got = lax.all_to_all(parts, BOTH, split_axis=0, concat_axis=0, tiled=True)]
  transfers between devices with their start and end apart: 8 -> 3, of which waited for: 5 -> 3; matrix products, arithmetic and copies ran while one was open for 2% -> 3% of each run, Pallas kernels for 13% -> 0%
where the time goes in v2:
time: 431 us; the launch traced here: 424 us
  Pallas kernels  256 us (59%)
  waiting for transfers between devices  72 us (17%)
  blocking collectives  36.3 us (8%)
  local copies, waits for them, and re-layouts  25 us (6%)
  between operations  14.4 us (3%)
  starting transfers between devices  12.6 us (3%)
  other arithmetic  5.83 us (1%)
    pallas_call x1, Pallas kernels, attention_forward(): pl.pallas_call(functools.partial(attention_forward_kernel, bool(own)), ou...  108 us
    pallas_call x1, Pallas kernels, experts_both_ways(): pl.pallas_call(experts_kernel, grid=(experts, tiles), out_shape=[jax.Shap...  95.6 us
    pallas_call x1, Pallas kernels, attention_backward(): pl.pallas_call(attention_backward_kernel, out_shape=[jax.ShapeDtypeStruct...  52.4 us
    all_gather x1, waiting for transfers between devices, sum_expert_maps(): return lax.all_gather(own, 'dp', axis=1, tiled=True)  44.7 us
    all_to_all x1, blocking collectives, sum_expert_maps(): got = lax.all_to_all(parts, BOTH, split_axis=0, concat_axis=0, tiled=True)  36.3 us
    all_gather x1, waiting for transfers between devices, sum_attention_maps(): whole = lax.all_gather(own[None], BOTH, axis=0, tiled=True)  16.9 us
    all_to_all x1, starting transfers between devices, sum_attention_maps(): got = lax.all_to_all(parts, BOTH, split_axis=0, concat_axis=0, tiled=True)  12.5 us
    all_to_all x1, waiting for transfers between devices, sum_attention_maps(): got = lax.all_to_all(parts, BOTH, split_axis=0, concat_axis=0, tiled=True)  10.4 us
  transfers between devices with their start and end apart: 3, of which 3 were waited for; matrix products, arithmetic and copies ran while one was open for 3% of the time, Pallas kernels for 0%

profile of v2, /device:TPU:0, one launch (start us, length us, event | category | flops | bytes accessed | tf_op | source)
XLA Modules:
  0.0 423.8 jit_solution(12620645177291182743)
XLA Ops:
  7.2 1.2 dynamic_slice.10.refs_13_
  8.4 1.2 dynamic_slice.9.refs_1_
  10.6 1.3 broadcast_in_dim.24.refs_3_.gain_a
  11.8 1.3 broadcast_in_dim.25.refs_9_.gain_m
  13.1 1.7 copy.55.routes
  14.8 1.8 copy.56.carried
  17.3 107.8 %attention_forward.1 = (bf16[1024,768]{1,0:T(8,128)(2,1)}, bf16[1024,768]{1,0:T(8,128)(2,1)}, bf16[1024,768]{1,0:T(8,128)(2,1)}, bf16[1024,768]{1,0:T(8,128)(2,1...) custom-call(s32[2]{0:T(128)} %bitcast.55, ...), custom_call_target="tpu_custom_call" | custom-call | tf_op jit(solution)/shard_map/attention_forward/pallas_call | solution.py:399
  125.1 95.6 %experts_both_ways.1 = (bf16[1024,768]{1,0:T(8,128)(2,1)}, f32[1024,768]{1,0:T(8,128)}, bf16[4,16,8448]{2,1,0:T(8,128)(2,1)}) custom-call(bf16[1024,768]{1,0:T(8,128)(2,1)} %get-tuple-element.31.xb, f32[1024,768]{1,0:T(8,128)} %get-tuple-element.32.h1_ref, f32[1024,128]{1,0:T(8,128)} %get-tuple-element.33.lin_ref, bf16[1024,768]{1,0:T(8,128)(2,1)} %cot.1, ...), custom_call_target="tpu_custom_call" | custom-call | tf_op jit(solution)/shard_map/experts_both_ways/pallas_call | solution.py:759
  220.7 52.4 %attention_backward.1 = (bf16[1024,768]{1,0:T(8,128)(2,1)}, bf16[8,16,768]{2,1,0:T(8,128)(2,1)}) custom-call(s32[2]{0:T(128)} %bitcast.56, f32[1024,768]{1,0:T(8,128)} %get-tuple-element.38.dh1_ref, bf16[1024,768]{1,0:T(8,128)(2,1)} %tok.1, f32[1,768]{1,0:T(1,128)} %broadcast_in_dim.24.refs_3_.gain_a, bf16[768,2304]{1,0:T(8,128)(2,1)} %wqkv.1, ...), custom_call_target="tpu_custom_call" | custom-call | tf_op jit(solution)/shard_map/attention_backward/pallas_call | solution.py:511
  273.1 1.2 fusion.2
  275.0 12.5 %all-to-all-start = ((bf16[32,16,192]{2,1,0:T(8,128)(2,1)}), bf16[32,16,192]{2,1,0:T(8,128)(2,1)S(1)}, u32[]{:S(2)}, u32[]{:S(2)}) async-start(bf16[32,16,192]{2,1,0:T(8,128)(2,1)} %bitcast.1), calls=%async_computation | async-start | bytes 524288 | tf_op jit(solution)/shard_map/all_to_all | solution.py:839
  287.8 10.4 %all-to-all-done = bf16[32,16,192]{2,1,0:T(8,128)(2,1)S(1)} async-done(((bf16[32,16,192]{2,1,0:T(8,128)(2,1)}), bf16[32,16,192]{2,1,0:T(8,128)(2,1)S(1)}, u32[]{:S(2)}, u32[]{:S(2)}) %all-to-all-start) | async-done | bytes 196640 | tf_op jit(solution)/shard_map/all_to_all | solution.py:839
  299.3 36.3 %all_to_all.10 = bf16[32,16,1152]{2,1,0:T(8,128)(2,1)S(1)} all-to-all(bf16[32,16,1152]{2,1,0:T(8,128)(2,1)S(1)} %bitcast.51), channel_id=1, replica_groups=mesh['dp'=8,'expert'=4] {'dp','expert'}, dimensions={0} | all-to-all | bytes 2359296 | tf_op jit(solution)/shard_map/all_to_all | solution.py:829
  335.6 1.1 convolution_convert_fusion
  336.7 16.9 %all-gather.6.cloned.1.call-done = bf16[4096,192]{0,1:T(8,128)(2,1)} async-done(((bf16[128,192]{0,1:T(8,128)(2,1)}), bf16[4096,192]{0,1:T(8,128)(2,1)}) %all-gather.6.cloned.1.call-update) | async-done | bytes 1572880 | tf_op jit(solution)/shard_map/all_gather | solution.py:841
  353.6 3.8 reshape.68
  357.5 1.8 copy.66
  359.4 1.3 slice.41
  360.7 1.4 copy.59
  363.0 44.7 %all-gather.4.cloned.1.call-done = bf16[128,9216]{1,0:T(8,128)(2,1)} async-done(((bf16[128,1152]{1,0:T(8,128)(2,1)}), bf16[128,9216]{1,0:T(8,128)(2,1)}) %all-gather.4.cloned.1.call-update) | async-done | bytes 2359312 | tf_op jit(solution)/shard_map/all_gather | solution.py:831
  407.7 1.9 slice_convert_fusion
  411.7 2.3 copy.61
  414.0 1.3 copy.62
  415.3 1.5 maximum_bitcast_fusion
  (24 shorter events, 6.9 us)
Async XLA Ops:
  273.1 14.5 %copy-start.1 = (s32[32]{0:T(128)S(1)}, s32[32]{0:T(128)}, u32[]{:S(2)}) copy-start(s32[32]{0:T(128)} %param.47) | copy-start | bytes 388
  273.1 26.0 %copy-start = (bf16[4,16,8448]{2,1,0:T(8,128)(2,1)S(1)}, bf16[4,16,8448]{2,1,0:T(8,128)(2,1)}, u32[]{:S(2)}) copy-start(bf16[4,16,8448]{2,1,0:T(8,128)(2,1)} %get-tuple-element.52) | copy-start | bytes 3244036
  275.0 23.1 %all-to-all-start = ((bf16[32,16,192]{2,1,0:T(8,128)(2,1)}), bf16[32,16,192]{2,1,0:T(8,128)(2,1)S(1)}, u32[]{:S(2)}, u32[]{:S(2)}) async-start(bf16[32,16,192]{2,1,0:T(8,128)(2,1)} %bitcast.1), calls=%async_computation | async-start | bytes 524288 | tf_op jit(solution)/shard_map/all_to_all | solution.py:839
  287.6 66.1 %all-gather.6.cloned.1.call-start = ((), (), s32[]{:S(2)}) async-start(), calls=%async_computation.3 | async-start | bytes 1622016 | tf_op jit(solution)/shard_map/all_gather | solution.py:841
  299.1 108.6 %all-gather.4.cloned.1.call-start = ((), (), s32[]{:S(2)}) async-start(), calls=%async_computation.2 | async-start | bytes 2654208 | tf_op jit(solution)/shard_map/all_gather | solution.py:831
Sparse Core Ops, SparseCore 0:
  299.2 54.3 all-gather.5
  356.4 51.1 all-gather.3

commit v3 on v2

--- a/solution.py
+++ b/solution.py
@@ -407,14 +407,197 @@
     )(*args)
 
 
-def attention_backward_kernel(
-    spans, dh1_ref, tok, gain_a, wqkv, wqk, wo, down_ref, up_s, cos, sin,
-    xa_ref, q_ref, k_ref, v_ref, ob_ref, ua_ref, uo_ref, lse_ref,
-    grad_tok, grad_maps,
-    bias, dob, datt, duo, lse_t, center_t, dq, dk, dv, dlin, dua,
-):
+class Mail:
+    def __init__(self, send, recv):
+        self.send, self.recv, self.started = send, recv, []
+
+    def post(self, source, target, peer, slot):
+        number = len(self.started)
+
+        def made():
+            return pltpu.make_async_remote_copy(
+                src_ref=source(), dst_ref=target(), send_sem=self.send.at[number], recv_sem=self.recv.at[slot],
+                device_id=peer, device_id_type=MESH,
+            )
+
+        made().start()
+        self.started.append(made)
+
+    def arrived(self, view, slot, peer):
+        pltpu.make_async_remote_copy(
+            src_ref=view, dst_ref=view, send_sem=self.send.at[0], recv_sem=self.recv.at[slot],
+            device_id=peer, device_id_type=MESH,
+        ).wait_recv()
+
+    def finish(self):
+        for made in self.started:
+            made().wait_send()
+
+
+def meet(peers):
+    barrier = pltpu.get_barrier_semaphore()
+    for peer in peers:
+        pl.semaphore_signal(barrier, inc=1, device_id=peer, device_id_type=MESH)
+    pl.semaphore_wait(barrier, len(peers))
+
+
+def summing_steps(refs, grad_maps):
+    maps_in, takers, all_e, all_a, e_got, e_two, e_own, a_in, a_part, a_z, a_own, send, recv, local = refs
+    mail = Mail(send, recv)
+    dp, ex = lax.axis_index("dp"), lax.axis_index("expert")
+    x, z = dp % 2, dp // 2
+    share = e_two.shape[3]
+    group = {k: (ex + k) % 4 for k in range(1, 4)}
+    later = {k: (z + k) % 4 for k in range(1, 4)}
+    along = {k: (dp + k) % 8 for k in range(1, 8)}
+    along_z = {k: ((z + k) % 4) * 2 + x for k in range(1, 4)}
+    plane = {(a, k): (other(dp, 1) if a else dp, (ex + k) % 4) for a in range(2) for k in range(4) if (a, k) != (0, 0)}
+    x_peer, y_peer, s_peer = (other(dp, 1), ex), (dp, other(ex, 2)), (dp, other(ex, 1))
+    free = [0]
+
+    def slots(n):
+        free[0] += n
+        return free[0] - n
+
+    first = {n: slots(c) for n, c in dict(e1=4, e2=8, e3=4, e4=4, a1=8, a2=4, a3=4, ay=1, ax=2, a_s=4).items()}
+
+    def begin():
+        meet([(dp, group[k]) for k in group] + [(along[k], ex) for k in along] + [plane[1, k] for k in range(1, 4)])
+        for k, to in group.items():
+            mail.post(lambda to=to: maps_in.at[to], lambda: e_got.at[ex], (dp, to), first["e1"] + k)
+        pltpu.make_async_copy(maps_in.at[ex], e_got.at[ex], local.at[0]).start()
+
+    def spread_out():
+        for k in group:
+            source = (ex + 4 - k) % 4
+            mail.arrived(e_got.at[source], first["e1"] + k, (dp, source))
+        pltpu.make_async_copy(maps_in.at[ex], e_got.at[ex], local.at[0]).wait()
+
+        def columns(to):
+            return e_got.at[:, :, pl.ds(pl.multiple_of(to * share, 128), share)]
+
+        for k, to in along.items():
+            mail.post(lambda to=to: columns(to), lambda: e_two.at[dp], (to, ex), first["e2"] + k)
+        e_two[dp] = e_got[:, :, pl.ds(pl.multiple_of(dp * share, 128), share)]
+
+    def placed(sender, columns):
+        row, column = iota((128, columns), 0), iota((128, columns), 1)
+        return one_hot(row - sender * RANK == column % RANK)
+
+    def add_up():
+        for k in along:
+            source = (dp + 8 - k) % 8
+            mail.arrived(e_two.at[source], first["e2"] + k, (source, ex))
+        rows = e_two[...].reshape(-1, share)
+        e_own[...] = mm(placed(takers[...], rows.shape[0]), rows).astype(BF)
+        for k, to in along_z.items():
+            mail.post(lambda: e_own, lambda: all_e.at[dp], (to, ex), first["e3"] + k)
+        mail.post(lambda: e_own, lambda: all_e.at[dp], x_peer, first["e4"])
+        pltpu.make_async_copy(e_own, all_e.at[dp], local.at[1]).start()
+
+    def e_forward():
+        for k in along_z:
+            source = ((z + 4 - k) % 4) * 2 + x
+            mail.arrived(all_e.at[source], first["e3"] + k, (source, ex))
+            here = functools.partial(lambda source: all_e.at[source], source)
+            mail.post(here, here, x_peer, first["e4"] + k)
+
+    def a_share():
+        for (a, k), to in plane.items():
+            number = 2 * to[1] + to[0] % 2
+            mail.post(
+                lambda number=number: grad_maps.at[number], lambda: a_in.at[x * 4 + ex], to, first["a1"] + a * 4 + k
+            )
+        a_in[x * 4 + ex] = grad_maps[2 * ex + x]
+
+    def a_partial():
+        for a, k in plane:
+            source = (other(dp, 1) if a else dp, (ex + 4 - k) % 4)
+            at = (source[0] % 2) * 4 + source[1]
+            mail.arrived(a_in.at[at], first["a1"] + a * 4 + k, source)
+        rows = a_in[...].reshape(128, -1)
+        senders = takers[:, pl.ds(pl.multiple_of(z * 128, 128), 128)]
+        a_part[...] = mm(placed(senders, 128), rows).astype(BF)
+        for k, to in later.items():
+            mail.post(
+                lambda to=to: a_part.at[pl.ds(pl.multiple_of(to * 32, 32), 32)], lambda: a_z.at[z],
+                (along_z[k], ex), first["a2"] + k,
+            )
+        a_z[z] = a_part[pl.ds(pl.multiple_of(z * 32, 32), 32), :]
+
+    def piece(number, place):
+        return all_a.at[number, pl.ds(pl.multiple_of(place * 32, 32), 32)]
+
+    mine = 2 * ex + x
+
+    def a_total():
+        for k in range(1, 4):
+            source = (z + 4 - k) % 4
+            mail.arrived(a_z.at[source], first["a2"] + k, (source * 2 + x, ex))
+        a_own[...] = sum(a_z[i].astype(F32) for i in range(4)).astype(BF)
+        for k in range(1, 4):
+            mail.post(lambda: a_own, lambda: piece(mine, z), (along_z[k], ex), first["a3"] + k)
+        pltpu.make_async_copy(a_own, piece(mine, z), local.at[2]).start()
+
+    def a_gather():
+        pltpu.make_async_copy(a_own, piece(mine, z), local.at[2]).wait()
+        for k in range(1, 4):
+            source = (z + 4 - k) % 4
+            mail.arrived(piece(mine, source), first["a3"] + k, (source * 2 + x, ex))
+
+        def send(number, peer, slot):
+            here = functools.partial(lambda number: all_a.at[number], number)
+            mail.post(here, here, peer, slot)
+
+        of_y, of_x = 2 * other(ex, 2) + x, 2 * ex + 1 - x
+        of_xy = 2 * other(ex, 2) + 1 - x
+        send(mine, y_peer, first["ay"])
+        send(mine, x_peer, first["ax"])
+        send(mine, s_peer, first["a_s"])
+        mail.arrived(all_a.at[of_y], first["ay"], y_peer)
+        send(of_y, x_peer, first["ax"] + 1)
+        send(of_y, s_peer, first["a_s"] + 1)
+        mail.arrived(all_a.at[of_x], first["ax"], x_peer)
+        send(of_x, s_peer, first["a_s"] + 2)
+        mail.arrived(all_a.at[of_xy], first["ax"] + 1, x_peer)
+        send(of_xy, s_peer, first["a_s"] + 3)
+
+    def end():
+        sib = other(ex, 1)
+        numbers = (2 * sib + x, 2 * other(sib, 2) + x, 2 * sib + 1 - x, 2 * other(sib, 2) + 1 - x)
+        for i, number in enumerate(numbers):
+            mail.arrived(all_a.at[number], first["a_s"] + i, s_peer)
+        for k in range(4):
+            source = ((z + 4 - k) % 4) * 2 + 1 - x
+            mail.arrived(all_e.at[source], first["e4"] + k, x_peer)
+        pltpu.make_async_copy(e_own, all_e.at[dp], local.at[1]).wait()
+        mail.finish()
+
+    return {
+        "begin": [begin], 1: [spread_out], 10: [add_up], "maps": [a_share, e_forward], "half": [a_partial],
+        "end": [a_total, a_gather, end],
+    }
+
+
+def attention_backward_kernel(exchange, *refs):
+    spans, dh1_ref, tok, gain_a, wqkv, wqk, wo, down_ref, up_s, cos, sin = refs[:11]
+    xa_ref, q_ref, k_ref, v_ref, ob_ref, ua_ref, uo_ref, lse_ref = refs[11:19]
+    steps = {}
+    if exchange:
+        grad_tok, grad_maps, own = refs[21], refs[24], refs[36:]
+        steps = summing_steps((*refs[19:21], *refs[22:24], *own), grad_maps)
+        bias, dob, datt, duo, lse_t, center_t, dq, dk, dv, dlin, dua = refs[25:36]
+    else:
+        grad_tok, grad_maps = refs[19:21]
+        bias, dob, datt, duo, lse_t, center_t, dq, dk, dv, dlin, dua = refs[21:]
     length, width = tok.shape
     groups = width // GROUP
+
+    def run(point):
+        for step in steps.get(point, ()):
+            step()
+
+    run("begin")
     for half in range(length // HALF):
         bias[half] = span_bias(spans[half] - half * HALF, True)
     of_head = one_hot(iota((128, width), 1) // HD == iota((128, width), 0))
@@ -465,11 +648,14 @@
             dv[at, lanes] += mm(prob.astype(BF), do * v_own)
             dk[at, lanes] += mm(ds, q * qk_own)
             dq[late, lanes] += t_mm(ds, kh)
+        for point in steps:
+            if isinstance(point, int):
+                pl.when(head == point)(functools.partial(run, point))
         return carry
 
     lax.fori_loop(0, HEADS, attend, 0)
 
-    def inner(block, carry):
+    def turn_back(block, carry):
         at = pl.ds(pl.multiple_of(block * 256, 256), 256)
         c, s = cos[at, :], -sin[at, :]
         for g in range(groups):
@@ -477,18 +663,10 @@
             dlin[at, lanes] = rope(dq[at, lanes] * 0.125, c, s).astype(BF)
             dlin[at, pl.ds(width + g * GROUP, GROUP)] = rope(dk[at, lanes], c, s).astype(BF)
         dlin[at, pl.ds(2 * width, width)] = dv[at, :].astype(BF)
-        d = dlin[at, :]
-        u = mm_t(d, up_s[:, pl.ds(0, 3 * width)]).astype(BF)
-        dua[at, :] = u
-        dx = mm_t(d[:, : 2 * width], wqk[...]) + mm_t(d[:, 2 * width :], wqkv[:, pl.ds(2 * width, width)])
-        dx = (dx + mm_t(u, down_ref[0])) * gain_a[...]
-        h0 = tok[at, :].astype(F32)
-        r = lax.rsqrt(jnp.mean(h0 * h0, axis=1, keepdims=True) + EPS)
-        pull = r * dx - h0 * (r * r * r * jnp.mean(dx * h0, axis=1, keepdims=True))
-        grad_tok[at, :] = (dh1_ref[at, :] + pull).astype(BF)
+        dua[at, :] = mm_t(dlin[at, :], up_s[:, pl.ds(0, 3 * width)]).astype(BF)
         return carry
 
-    lax.fori_loop(0, length // 256, inner, 0)
+    lax.fori_loop(0, length // 256, turn_back, 0)
     order = head_order(True)
     grads = t_mm(dua[...], xa_ref[...]).astype(BF)
     for p in range(3):
@@ -502,36 +680,125 @@
             ).astype(BF)
         grad_maps[4 + p] = grads
     grad_maps[7] = t_mm(uo_ref[...], datt[...]).astype(BF)[:RANK]
-
-
-def attention_backward(spans, dh1, tok, gain_a, wqkv, wqk, wo, down_s, up_s, xa, q, k, v, ob, ua, uo, lse):
+    run("maps")
+
+    def inner(block, carry):
+        at = pl.ds(pl.multiple_of(block * 256, 256), 256)
+        d, u = dlin[at, :], dua[at, :]
+        dx = mm_t(d[:, : 2 * width], wqk[...]) + mm_t(d[:, 2 * width :], wqkv[:, pl.ds(2 * width, width)])
+        dx = (dx + mm_t(u, down_ref[0])) * gain_a[...]
+        h0 = tok[at, :].astype(F32)
+        r = lax.rsqrt(jnp.mean(h0 * h0, axis=1, keepdims=True) + EPS)
+        pull = r * dx - h0 * (r * r * r * jnp.mean(dx * h0, axis=1, keepdims=True))
+        grad_tok[at, :] = (dh1_ref[at, :] + pull).astype(BF)
+        if "half" in steps:
+            pl.when(block == 1)(functools.partial(run, "half"))
+        return carry
+
+    lax.fori_loop(0, length // 256, inner, 0)
+    run("end")
+
+
+def attention_backward(
+    spans, dh1, tok, gain_a, wqkv, wqk, wo, down_s, up_s, xa, q, k, v, ob, ua, uo, lse, maps=None, takers=None
+):
     length, width = tok.shape
     cos, sin = rope_tables(length)
     vmem, smem = pl.BlockSpec(memory_space=pltpu.VMEM), pl.BlockSpec(memory_space=pltpu.SMEM)
+    anys = pl.BlockSpec(memory_space=pl.ANY)
+    args = (spans, dh1, tok, gain_a, wqkv, wqk, wo, down_s, up_s, cos, sin, xa, q, k, v, ob, ua, uo, lse)
+    in_specs = [smem] + [vmem] * 18
+    compact = ((8, RANK, width), BF)
+    shapes, out_specs, scratch = [((length, width), BF)], [vmem], []
+    if maps is None:
+        shapes.append(compact)
+        out_specs.append(vmem)
+    else:
+        share = maps.shape[2] // 8
+        in_specs += [anys, vmem]
+        args += (maps, takers)
+        shapes += [((8, 128, share), BF), ((8, 128, width), BF)]
+        out_specs += [anys] * 2
+        scratch.append(compact)
+    scratch += [
+        ((length // HALF, HALF, HALF), F32),
+        ((length, width), BF),
+        ((length, width), BF),
+        ((length, 128), BF),
+        ((128, length), F32),
+        ((128, length), F32),
+        ((length, width), F32),
+        ((length, width), F32),
+        ((length, width), F32),
+        ((length, 3 * width), BF),
+        ((length, 128), BF),
+    ]
+    params = dict(vmem_limit_bytes=62 * MIB)
+    semaphores = []
+    if maps is not None:
+        scratch += [
+            (maps.shape, BF),
+            ((8, 4, RANK, share), BF),
+            ((128, share), BF),
+            ((8, RANK, width), BF),
+            ((128, width), BF),
+            ((4, 32, width), BF),
+            ((32, width), BF),
+        ]
+        semaphores = [pltpu.SemaphoreType.DMA((48,)), pltpu.SemaphoreType.DMA((48,)), pltpu.SemaphoreType.DMA((3,))]
+        params.update(collective_id=1, has_side_effects=True)
     return pl.pallas_call(
-        attention_backward_kernel,
-        out_shape=[
-            jax.ShapeDtypeStruct((length, width), BF),
-            jax.ShapeDtypeStruct((8, RANK, width), BF),
-        ],
-        in_specs=[smem] + [vmem] * 18,
-        out_specs=[vmem] * 2,
-        scratch_shapes=[
-            pltpu.VMEM((length // HALF, HALF, HALF), F32),
-            pltpu.VMEM((length, width), BF),
-            pltpu.VMEM((length, width), BF),
-            pltpu.VMEM((length, 128), BF),
-            pltpu.VMEM((128, length), F32),
-            pltpu.VMEM((128, length), F32),
-            pltpu.VMEM((length, width), F32),
-            pltpu.VMEM((length, width), F32),
-            pltpu.VMEM((length, width), F32),
-            pltpu.VMEM((length, 3 * width), BF),
-            pltpu.VMEM((length, 128), BF),
-        ],
-        compiler_params=pltpu.CompilerParams(vmem_limit_bytes=60 * MIB),
+        functools.partial(attention_backward_kernel, maps is not None),
+        out_shape=[jax.ShapeDtypeStruct(s, t) for s, t in shapes],
+        in_specs=in_specs,
+        out_specs=out_specs,
+        scratch_shapes=[pltpu.VMEM(s, t) for s, t in scratch] + semaphores,
+        compiler_params=pltpu.CompilerParams(**params),
         name="attention_backward",
-    )(spans, dh1, tok, gain_a, wqkv, wqk, wo, down_s, up_s, cos, sin, xa, q, k, v, ob, ua, uo, lse)
+    )(*args)
+
+
+def unpack_kernel(all_e, all_a, a_attention, b_qkv, b_out, a_gate_up, b_gate_up, a_down, b_down):
+    width, hidden, share = b_out.shape[1], a_down.shape[1], all_e.shape[2]
+    for p in range(4):
+        a_attention[p] = all_a[p].astype(F32).T
+    for p in range(3):
+        b_qkv[p] = all_a[4 + p].astype(F32)
+    b_out[...] = all_a[7].astype(F32)
+
+    def pieces(start, number):
+        at = start
+        while at < start + number:
+            stop = min(start + number, (at // share + 1) * share)
+            part = all_e[at // share, :, at % share : at % share + stop - at]
+            yield at - start, part.astype(F32)
+            at = stop
+
+    for p in range(2):
+        for at, part in pieces(p * width, width):
+            a_gate_up[0, p, pl.ds(at, part.shape[1]), :] = part.T
+        for at, part in pieces(2 * width + p * hidden, hidden):
+            b_gate_up[0, p, :, pl.ds(at, part.shape[1])] = part
+    for at, part in pieces(2 * width + 2 * hidden, hidden):
+        a_down[0, pl.ds(at, part.shape[1]), :] = part.T
+    for at, part in pieces(2 * width + 3 * hidden, width):
+        b_down[0, :, pl.ds(at, part.shape[1])] = part
+
+
+def unpack(all_e, all_a, hidden):
+    width = all_a.shape[2]
+    shapes = [
+        (4, width, 128), (3, 128, width), (128, width),
+        (1, 2, width, 128), (1, 2, 128, hidden), (1, hidden, 128), (1, 128, width),
+    ]
+    return pl.pallas_call(
+        unpack_kernel,
+        out_shape=[jax.ShapeDtypeStruct(s, F32) for s in shapes],
+        in_specs=[pl.BlockSpec(memory_space=pltpu.VMEM)] * 2,
+        out_specs=[pl.BlockSpec(memory_space=pltpu.VMEM)] * 7,
+        compiler_params=pltpu.CompilerParams(vmem_limit_bytes=40 * MIB),
+        name="unpack",
+    )(all_e, all_a)
 
 
 def split(x):
@@ -552,7 +819,7 @@
     kinds = carried.shape[1]
     numbers = kinds - 4
     tile = w_gate.shape[2]
-    hidden = (grads.shape[2] - 3 * width) // 3
+    hidden = (maps.shape[2] - 3 * width) // 3
     rows_of = 128
 
     def padded_rows(start, number, before=0):
@@ -606,6 +873,9 @@
     def _():
         grads[...] = jnp.zeros(grads.shape, BF)
 
+    if grads.shape[2] > maps.shape[2]:
+        grads[0, :, maps.shape[2] :] = jnp.zeros((RANK, grads.shape[2] - maps.shape[2]), BF)
+
     def work(n):
         rows = pl.ds(0, n)
 
@@ -679,7 +949,7 @@
             to_a = mm(dug.T[: 2 * RANK], x).astype(BF)
             grads[0, :, :width] = to_a[:RANK]
             grads[0, :, width : 2 * width] = to_a[RANK:]
-            grads[0, :, 2 * width + 3 * hidden :] = mm(ud.T[:RANK], dy).astype(BF)
+            grads[0, :, 2 * width + 3 * hidden : 3 * width + 3 * hidden] = mm(ud.T[:RANK], dy).astype(BF)
 
     for number in range(1, 512 // rows_of + 1):
         pl.when(blocks == number)(functools.partial(work, number * rows_of))
@@ -744,13 +1014,14 @@
         lax.fori_loop(0, length // 256, combine, 0)
 
 
-def experts_both_ways(xb, h1, lin, cot, routes, carried, gain_m, wr, vectors, w_gu, w_dn, maps):
+def experts_both_ways(xb, h1, lin, cot, routes, carried, gain_m, wr, vectors, w_gu, w_dn, maps, copies):
     length, width = xb.shape
     experts, hidden = w_dn.shape[0], w_dn.shape[1]
     tile = hidden // 2
     tiles = hidden // tile
     most = 2 * length + experts * 128
     total = 3 * width + 3 * hidden
+    padded = -(-total // (copies * 128)) * copies * 128
 
     def whole(a):
         return pl.BlockSpec(a.shape, lambda e, j: (0,) * a.ndim, pipeline_mode=pl.Buffered(1))
@@ -762,7 +1033,7 @@
         out_shape=[
             jax.ShapeDtypeStruct((length, width), BF),
             jax.ShapeDtypeStruct((length, width), F32),
-            jax.ShapeDtypeStruct((experts, RANK, total), BF),
+            jax.ShapeDtypeStruct((experts, RANK, padded), BF),
         ],
         in_specs=[whole(a) for a in resident]
         + [
@@ -774,7 +1045,7 @@
         out_specs=[
             pl.BlockSpec((length, width), lambda e, j: (0, 0), pipeline_mode=pl.Buffered(1)),
             pl.BlockSpec((length, width), lambda e, j: (0, 0), pipeline_mode=pl.Buffered(1)),
-            pl.BlockSpec((1, RANK, total), lambda e, j: (e, 0, 0)),
+            pl.BlockSpec((1, RANK, padded), lambda e, j: (e, 0, 0)),
         ],
         scratch_shapes=[
             pltpu.SMEM((2, experts + 1), jnp.int32),
@@ -823,9 +1094,8 @@
 def sum_expert_maps(compact, spread):
     copies = lax.axis_size("dp")
     experts, rank, columns = compact.shape
-    each = -(-columns // (copies * 128)) * 128
-    parts = jnp.pad(compact, ((0, 0), (0, 0), (0, copies * each - columns)))
-    parts = parts.reshape(experts, rank, copies, each).transpose(2, 0, 1, 3).reshape(copies * experts, rank, each)
+    each = columns // copies
+    parts = compact.reshape(experts, rank, copies, each).transpose(2, 0, 1, 3).reshape(copies * experts, rank, each)
     got = lax.all_to_all(parts, BOTH, split_axis=0, concat_axis=0, tiled=True)
     own = mm(spread, got.reshape(-1, each)).astype(BF)
     return lax.all_gather(own, "dp", axis=1, tiled=True)
@@ -873,18 +1143,24 @@
     xa, q, k, v, ob, ua, uo, lse, h1, xb, lin, wqk, down_s, up_s = outs[:14]
     weights = outs[14:] if exchange else gather_experts(own, senders)
     result, dh1, expert_maps = experts_both_ways(
-        xb, h1, lin, cotangent, routes, router_logits_carried, gain_m, router, constant_expert_vectors, *weights
+        xb, h1, lin, cotangent, routes, router_logits_carried, gain_m, router, constant_expert_vectors, *weights,
+        lax.axis_size("dp"),
     )
-    grad_tokens, attention_maps = attention_backward(
-        spans, dh1, tokens, gain_a, query_key_value_weight, wqk, attention_output_weight, down_s, up_s,
+    backward = functools.partial(
+        attention_backward, spans, dh1, tokens, gain_a, query_key_value_weight, wqk, attention_output_weight, down_s, up_s,
         xa, q, k, v, ob, ua, uo, lse,
     )
+    if exchange:
+        takers = jnp.repeat(sequence_adapter_index, RANK)[None]
+        grad_tokens, all_e, all_a = backward(expert_maps, takers)
+        return (result, grad_tokens, *unpack(all_e, all_a, hidden))
+    grad_tokens, attention_maps = backward()
     to = (sequence_adapter_index[:, None] * RANK + jnp.arange(RANK)[None, :]).reshape(-1)
     spread = (jnp.arange(128)[:, None] == to[None, :]).astype(BF)
-    of_expert = sum_expert_maps(expert_maps, spread)[:, : expert_maps.shape[2]].astype(F32)
+    of_expert = sum_expert_maps(expert_maps, spread).astype(F32)
     of_attention = sum_attention_maps(attention_maps, spread)
-    cuts = [width, 2 * width, 2 * width + hidden, 2 * width + 2 * hidden, 2 * width + 3 * hidden]
-    gud0, gud1, guu0, guu1, dnd, dnu = jnp.split(of_expert, cuts, axis=1)
+    ends = [0, width, 2 * width, 2 * width + hidden, 2 * width + 2 * hidden, 2 * width + 3 * hidden, 3 * width + 3 * hidden]
+    gud0, gud1, guu0, guu1, dnd, dnu = (of_expert[:, a:b] for a, b in zip(ends, ends[1:]))
     return (
         result,
         grad_tokens,

time: 431 us -> 352 us (0.82); the launches traced: 424 us -> 352 us
  Pallas kernels: 256 us -> 337 us
  waiting for transfers between devices: 72 us -> 0 us
  blocking collectives: 36.3 us -> 0 us
  between operations: 14.4 us -> 0.9 us
  starting transfers between devices: 12.6 us -> 0 us
  local copies, waits for them, and re-layouts: 25 us -> 12.9 us
  other arithmetic: 5.83 us -> 0.73 us
    pallas_call x1 -> x2, Pallas kernels: 52.4 us -> 127 us  [the longest x1 124 us: attention_backward(): pl.pallas_call(functools.partial(attention_backward_kernel, maps is not N...]
    all_gather x2 -> x0, waiting for transfers between devices: 61.6 us -> none  [the longest x1 44.7 us: sum_expert_maps(): return lax.all_gather(own, 'dp', axis=1, tiled=True)]
    all_to_all x1 -> x0, blocking collectives: 36.3 us -> none  [sum_expert_maps(): got = lax.all_to_all(parts, BOTH, split_axis=0, concat_axis=0, tiled=True)]
    all_to_all x1 -> x0, starting transfers between devices: 12.5 us -> none  [sum_attention_maps(): got = lax.all_to_all(parts, BOTH, split_axis=0, concat_axis=0, tiled=True)]
    all_to_all x1 -> x0, waiting for transfers between devices: 10.4 us -> none  [sum_attention_maps(): got = lax.all_to_all(parts, BOTH, split_axis=0, concat_axis=0, tiled=True)]
    pallas_call x1, Pallas kernels: 95.6 us -> 102 us  [experts_both_ways(): pl.pallas_call(experts_kernel, grid=(experts, tiles), out_shape=[jax.Shap...]
    convert_element_type x2 -> x0, local copies, waits for them, and re-layouts: 5.65 us -> none  [sum_attention_maps(): whole.reshape(maps, cuts, 128, width // cuts).transpose(0, 2, 1, 3)]
    unnamed x10 -> x15, local copies, waits for them, and re-layouts: 9.36 us -> 6.25 us
  transfers between devices with their start and end apart: 3 -> 0, of which waited for: 3 -> 0; matrix products, arithmetic and copies ran while one was open for 3% -> 0% of each run, Pallas kernels for 0% -> 0%
where the time goes in v3:
time: 352 us
  Pallas kernels  337 us (96%)
  local copies, waits for them, and re-layouts  12.9 us (4%)
    pallas_call x1, Pallas kernels, attention_backward(): pl.pallas_call(functools.partial(attention_backward_kernel, maps is not N...  124 us
    pallas_call x1, Pallas kernels, attention_forward(): pl.pallas_call(functools.partial(attention_forward_kernel, bool(own)), ou...  108 us
    pallas_call x1, Pallas kernels, experts_both_ways(): pl.pallas_call(experts_kernel, grid=(experts, tiles), out_shape=[jax.Shap...  102 us

profile of v3, /device:TPU:0, one launch (start us, length us, event | category | flops | bytes accessed | tf_op | source)
XLA Modules:
  0.0 351.8 jit_solution(17184281030547523043)
XLA Ops:
  0.7 1.2 dynamic_slice.9.refs_1_
  1.9 1.2 dynamic_slice.10.refs_13_
  3.1 0.7 pad_maximum_fusion
  3.9 0.2 copy.43
  4.0 0.7 pad.4.refs_10_.wr
  4.8 1.3 broadcast_in_dim.10.refs_9_.gain_m
  6.0 1.3 broadcast_in_dim.9.refs_3_
  7.3 0.0 copy-start.3
  7.3 107.9 %attention_forward.1 = (bf16[1024,768]{1,0:T(8,128)(2,1)}, bf16[1024,768]{1,0:T(8,128)(2,1)}, bf16[1024,768]{1,0:T(8,128)(2,1)}, bf16[1024,768]{1,0:T(8,128)(2,1...) custom-call(s32[2]{0:T(128)} %bitcast.1, ...), custom_call_target="tpu_custom_call" | custom-call | tf_op jit(solution)/shard_map/attention_forward/pallas_call | solution.py:399
  115.2 0.0 copy-done.4
  115.2 1.0 copy.44.routes
  116.2 0.0 copy-done.3
  116.2 1.0 copy.45.carried
  117.2 102.3 %experts_both_ways.1 = (bf16[1024,768]{1,0:T(8,128)(2,1)}, f32[1024,768]{1,0:T(8,128)}, bf16[4,16,9216]{2,1,0:T(8,128)(2,1)}) custom-call(bf16[1024,768]{1,0:T(8,128)(2,1)} %get-tuple-element.39.xb, f32[1024,768]{1,0:T(8,128)} %get-tuple-element.40.h1_ref, f32[1024,128]{1,0:T(8,128)} %get-tuple-element.41.lin_ref, bf16[1024,768]{1,0:T(8,128)(2,1)} %cot.1, ...), custom_call_target="tpu_custom_call" | custom-call | tf_op jit(solution)/shard_map/experts_both_ways/pallas_call | solution.py:1030
  219.6 0.0 copy-done.5
  219.6 0.1 broadcast_in_dim.11
  219.7 0.7 broadcast_in_dim_reshape.3.refs_20_
  220.3 123.8 %attention_backward.1 = (bf16[1024,768]{1,0:T(8,128)(2,1)}, bf16[8,128,1152]{2,1,0:T(8,128)(2,1)}, bf16[8,128,768]{2,1,0:T(8,128)(2,1)}) custom-call(s32[2]{0:T(128)} %bitcast.2, f32[1024,768]{1,0:T(8,128)} %get-tuple-element.46.refs_1_, bf16[1024,768]{1,0:T(8,128)(2,1)} %refs_2_.3, f32[1,768]{1,0:T(1,128)} %broadcast_in_dim.9.refs_3_, ...), custom_call_target="tpu_custom_call" | custom-call | tf_op jit(solution)/shard_map/attention_backward/pallas_call | solution.py:750
  344.2 0.0 copy-start
  344.2 1.7 copy-done
  345.8 1.4 copy-done.1
  347.2 3.3 unpack.1
  350.5 0.0 copy-done.2
  350.5 1.1 copy.47
  (4 shorter events, 0.0 us)
Async XLA Ops:
  7.3 107.9 %copy-start.4 = (s32[1024,2]{0,1:T(2,128)S(1)}, s32[1024,2]{0,1:T(2,128)}, u32[]{:S(2)}) copy-start(s32[1024,2]{0,1:T(2,128)} %param.44) | copy-start | bytes 24580
  7.3 108.9 %copy-start.3 = (f32[1024,8]{0,1:T(8,128)S(1)}, f32[1024,8]{0,1:T(8,128)}, u32[]{:S(2)}) copy-start(f32[1024,8]{0,1:T(8,128)} %param.45) | copy-start | bytes 98308
  117.2 102.3 %copy-start.5 = (s32[32]{0:T(128)S(1)}, s32[32]{0:T(128)}, u32[]{:S(2)}) copy-start(s32[32]{0:T(128)} %param.47) | copy-start | bytes 388
  344.2 1.7 copy-start
  345.8 1.4 copy-start.1
  347.2 3.3 copy-start.2

commit v4 on v3

--- a/solution.py
+++ b/solution.py
@@ -87,7 +87,7 @@
 
 
 def sending_steps(own, outs, scratch):
-    senders, w_gu, w_dn, gu_down, gu_up, dn_down, dn_up = own
+    adapters, w_gu, w_dn, gu_down, gu_up, dn_down, dn_up = own
     all_gu, all_dn, all_maps = outs
     bounce_gu, bounce_dn, compact, send, recv, local = scratch
     sources, targets, bounce = (w_gu, w_dn), (all_gu, all_dn), (bounce_gu, bounce_dn)
@@ -157,7 +157,7 @@
 
     def select():
         row, column = iota((64, 128), 0), iota((64, 128), 1)
-        first = sum(jnp.where(row // RANK == i, senders[i], 0) for i in range(4))
+        first = sum(jnp.where(row // RANK == i, adapters[dp * 4 + i], 0) for i in range(4))
         rows = one_hot(column == first * RANK + row % RANK)
         width, hidden = gu_down.shape[2], dn_down.shape[1]
         parts = [
@@ -220,47 +220,70 @@
 
     c, e = CHUNKS, EXTRA
     return {
-        "begin": [begin, select],
-        "ready": [turn],
-        "projected": [got("y", c[0])],
-        2: [got("x", c[0]), got("z", c[0])],
-        4: [got("y", c[1])],
-        6: [got("y", c[2]), got("d", c[0])],
-        9: [got("x", c[1]), got("z", c[1])],
-        "end": [
-            got("y", c[3]), got("x", c[2]), got("z", c[2]), got("e", e[0]), got("x", c[3]), got("z", c[3]), got("e", e[1]),
-            got("d", c[1]), got("d", c[2]), got("o", e[0]), got("d", c[3]), got("o", e[1]), end,
-        ],
+        "begin": [begin],
+        "loaded": [select],
+        "ready": [turn, got("y", c[0])],
+        "projected": [got("x", c[0]), got("z", c[0]), got("y", c[1])],
+        3: [got("y", c[2])],
+        6: [got("z", c[1]), got("x", c[1])],
+        8: [got("y", c[3]), got("d", c[0])],
+        10: [got("x", c[2]), got("z", c[2])],
+        "finished": [got("z", c[3]), got("e", e[0])],
+        200: [got("x", c[3])],
+        201: [got("e", e[1])],
+        202: [got("d", c[1])],
+        203: [got("d", c[2])],
+        "end": [got("o", e[0]), got("d", c[3]), got("o", e[1]), end],
     }
 
 
 def attention_forward_kernel(exchange, *refs):
-    spans, adapter_ref, tok, gain_a, wqkv, down, up, wo, up_out, gain_m, wr, cos, sin = refs[:13]
-    refs = refs[13:]
+    spans, adapters, tok, gain_a, wqkv, down, up, wo, up_out, gain_m, router, mixing, cos, sin = refs[:14]
+    refs = refs[14:]
     own = ()
     if exchange:
-        own, refs = refs[:7], refs[7:]
-    xa_ref, q_ref, k_ref, v_ref, ob_ref, ua_ref, uo_ref, lse_ref, h1_ref, xb_ref, lin_ref, wqk_ref, down_ref, up_s = refs[:14]
-    refs = refs[14:]
+        own, refs = (adapters, *refs[:9]), refs[9:]
+    xa_ref, q_ref, k_ref, v_ref, ob_ref, ua_ref, uo_ref, lse_ref, h1_ref, xb_ref, lin_ref, wqk_ref, down_ref, up_s, wr = refs[:15]
+    refs = refs[15:]
     steps = {}
     if exchange:
-        steps = sending_steps(own, refs[:3], refs[4:])
-        bias = refs[3]
+        cot, routes, carried = own[-3:]
+        own_outs, semaphores = refs[:3], refs[6:12]
+        own_both, own_grads, bias = refs[3:6]
+        bounce_gu, bounce_dn, compact = refs[6:9]
+        info_t, place_t, x_s, c_s, dy_s, y_acc, ud_acc, dx_acc, dug_acc = refs[12:21]
+        held, refs = refs[21:], ()
+        loads = (tok, down, up, up_out, *own[3:7], wqkv, cos, sin, wo, cot)
+        load = Staged(list(zip(loads, held)), held[-2])
+        tok, down, up, up_out, *maps, wqkv, cos, sin, wo, cot = held[: len(loads)]
+        outs = (xa_ref, q_ref, k_ref, v_ref, ob_ref, ua_ref, uo_ref, lse_ref, h1_ref, xb_ref, lin_ref, wqk_ref, down_ref, up_s, wr)
+        kept_outs = held[len(loads) : len(loads) + len(outs)]
+        store = Staged(list(zip(kept_outs, outs)), held[-1])
+        xa_ref, q_ref, k_ref, v_ref, ob_ref, ua_ref, uo_ref, lse_ref, h1_ref, xb_ref, lin_ref, wqk_ref, down_ref, up_s, wr = kept_outs
+        steps = sending_steps((*own[:3], *maps), own_outs, semaphores)
     else:
         (bias,) = refs
     length, width = tok.shape
     groups = width // GROUP
-    adapter = adapter_ref[0]
+    adapter = adapters[lax.axis_index("dp") * lax.axis_size("expert") + lax.axis_index("expert")]
 
     def run(point):
         for step in steps.get(point, ()):
             step()
 
     run("begin")
+    if exchange:
+        load.start()
+        load.wait()
+        run("loaded")
     order = head_order(False)
     down_s = sum(mm(down[p], picker(adapter, p)) for p in range(3)).astype(BF)
     down_o = mm(down[3], picker(adapter, 0)).astype(BF)
     up_o = mm(placer(adapter, 0), up_out[...]).astype(BF)
+    row, column = iota((128, router.shape[0]), 0), iota((128, router.shape[0]), 1)
+    wr[...] = mm(one_hot(row == column), router[...]).astype(BF)
+    row, column = iota((128, mixing.shape[0]), 0), iota((128, mixing.shape[0]), 1)
+    wr[...] += mm(one_hot(row == column + router.shape[0]), mixing[...]).astype(BF)
     down_ref[0] = down_s
     down_ref[1] = down_o
     up_s[:, pl.ds(3 * width, width)] = up_o
@@ -281,7 +304,7 @@
     def project(block, carry):
         at = pl.ds(pl.multiple_of(block * 256, 256), 256)
         h0 = tok[at, :].astype(F32)
-        x = h0 * lax.rsqrt(jnp.mean(h0 * h0, axis=1, keepdims=True) + EPS) * gain_a[...]
+        x = h0 * lax.rsqrt(jnp.mean(h0 * h0, axis=1, keepdims=True) + EPS) * gain_a[...][None]
         x = x.astype(BF)
         xa_ref[at, :] = x
         u = mm(x, down_s).astype(BF)
@@ -332,7 +355,7 @@
             old = jnp.where(v_own > 0.5, 0.0, ob_f[at, lanes].astype(F32))
             ob_f[at, lanes] = jnp.where(v_own > 0.5, o, old).astype(BF)
         for point in steps:
-            if isinstance(point, int):
+            if isinstance(point, int) and point < 100:
                 pl.when(head == point)(functools.partial(run, point))
         return carry
 
@@ -345,17 +368,60 @@
         uo_ref[at, :] = u
         h1 = tok[at, :].astype(F32) + (mm(o, wo[...]) + mm(u, up_o))
         h1_ref[at, :] = h1
-        x = h1 * lax.rsqrt(jnp.mean(h1 * h1, axis=1, keepdims=True) + EPS) * gain_m[...]
+        x = h1 * lax.rsqrt(jnp.mean(h1 * h1, axis=1, keepdims=True) + EPS) * gain_m[...][None]
         x = x.astype(BF)
         xb_ref[at, :] = x
-        lin_ref[at, :] = mm(x, wr[...])
+        lin_ref[at, :] = mm_t(x, wr[...])
         return carry
 
     lax.fori_loop(0, length // 256, finish, 0)
+    if exchange:
+        store.start()
+        run("finished")
+        ex = lax.axis_index("expert")
+        hidden = bounce_dn.shape[0]
+        own_grads[:, 3 * width + 3 * hidden :] = jnp.zeros((RANK, own_grads.shape[1] - 3 * width - 3 * hidden), BF)
+        route(lin_ref, carried, routes, carried.shape[0] - 4, info_t, place_t)
+        x, c, g, dy = take_rows(x_s.shape[0], place_t[pl.ds(ex, 1), :], info_t[pl.ds(ex, 1), :], xb_ref, cot)
+        x_s[...], c_s[...], dy_s[...] = x, c, dy
+        a_gu = padded_rows(compact[ex, :, :width]) + padded_rows(compact[ex, :, width : 2 * width], RANK)
+        b_dn = padded_rows(compact[ex, :, 2 * width + 3 * hidden :])
+        ug, dud = mm_t(x, a_gu).astype(BF), mm_t(dy, b_dn).astype(BF)
+        kept = (y_acc, ud_acc, dx_acc, dug_acc)
+        for ref in kept:
+            ref[...] = jnp.zeros(ref.shape, F32)
+        run(200)
+        tile = 512
+
+        def one_tile(j, carry):
+            at = pl.multiple_of(j * tile, tile)
+            starts = [2 * width + i * hidden + at for i in range(3)]
+            sums, parts = hidden_tile(
+                x_s[...], dy_s[...], ug, dud,
+                bounce_gu[:, pl.ds(at, tile)], bounce_gu[:, pl.ds(hidden + at, tile)], bounce_dn[pl.ds(at, tile), :],
+                padded_rows(compact[ex, :, pl.ds(starts[0], tile)]),
+                padded_rows(compact[ex, :, pl.ds(starts[1], tile)], RANK),
+                padded_rows(compact[ex, :, pl.ds(starts[2], tile)]),
+            )
+            for start, part in zip(starts, parts):
+                own_grads[:, pl.ds(start, tile)] = part
+            for ref, value in zip(kept, sums):
+                ref[...] += value
+            for point in steps:
+                if isinstance(point, int) and point > 200:
+                    pl.when(j == point - 201)(functools.partial(run, point))
+            return carry
+
+        lax.fori_loop(0, hidden // tile, one_tile, 0)
+        out, parts = close_rows(ex, [ref[...] for ref in kept], x_s[...], c_s[...], g, dy_s[...], a_gu, b_dn)
+        own_both[:, :width], own_both[:, width : 2 * width], own_both[:, 2 * width :] = out
+        own_grads[:, :width], own_grads[:, width : 2 * width] = parts[:2]
+        own_grads[:, 2 * width + 3 * hidden : 3 * width + 3 * hidden] = parts[2]
+        store.wait()
     run("end")
 
 
-def attention_forward(tok, gain_a, wqkv, down, up, wo, up_out, gain_m, wr, spans, adapter, own=(), senders=None):
+def attention_forward(tok, gain_a, wqkv, down, up, wo, up_out, gain_m, router, mixing, spans, adapters, own=()):
     length, width = tok.shape
     cos, sin = rope_tables(length)
     shapes = [
@@ -373,20 +439,31 @@
         ((width, 2 * width), BF),
         ((2, width, 128), BF),
         ((128, 4 * width), BF),
+        ((128, width), BF),
     ]
     vmem, smem = pl.BlockSpec(memory_space=pltpu.VMEM), pl.BlockSpec(memory_space=pltpu.SMEM)
     anys = pl.BlockSpec(memory_space=pl.ANY)
-    in_specs, out_specs = [smem, smem] + [vmem] * 11, [vmem] * len(shapes)
+    in_specs, out_specs = [smem, smem] + [vmem] * 12, [vmem] * len(shapes)
     scratch = [pltpu.VMEM((length // HALF, HALF, HALF), F32)]
     params = dict(vmem_limit_bytes=60 * MIB)
-    args = (spans, adapter, tok, gain_a, wqkv, down, up, wo, up_out, gain_m, wr, cos, sin)
+    args = (spans, adapters, tok, gain_a, wqkv, down, up, wo, up_out, gain_m, router, mixing, cos, sin)
     if own:
         w_gu, w_dn = own[:2]
         columns = 3 * width + 3 * w_dn.shape[1]
-        in_specs += [smem, anys, anys] + [vmem] * 4
-        args += (senders, *own)
-        shapes += [((4, *w_gu.shape[1:]), BF), ((4, *w_dn.shape[1:]), BF), ((4, RANK, columns), BF)]
-        out_specs += [anys] * 3
+        in_specs = [smem, smem] + [vmem if i in (1, 7, 8, 9) else anys for i in range(12)]
+        in_specs += [anys] * 7 + [vmem] * 2
+        args += own
+        held = [args[i] for i in (2, 5, 6, 8, 16, 17, 18, 19, 4, 12, 13, 7, 20)]
+        held = [pltpu.VMEM(a.shape, a.dtype) for a in held] + [pltpu.VMEM(a, t) for a, t in shapes]
+        padded = -(-columns // 1024) * 1024
+        shapes += [
+            ((4, *w_gu.shape[1:]), BF),
+            ((4, *w_dn.shape[1:]), BF),
+            ((4, RANK, columns), BF),
+            ((HALF, 2 * width + 128), BF),
+            ((RANK, padded), BF),
+        ]
+        out_specs = [anys] * (len(out_specs) + 3) + [vmem] * 2
         scratch += [
             pltpu.VMEM(w_gu.shape[1:], BF),
             pltpu.VMEM(w_dn.shape[1:], BF),
@@ -394,7 +471,17 @@
             pltpu.SemaphoreType.DMA((96,)),
             pltpu.SemaphoreType.DMA((48, 2)),
             pltpu.SemaphoreType.DMA((3,)),
+            pltpu.VMEM((128, length), F32),
+            pltpu.VMEM((128, length), F32),
+            pltpu.VMEM((HALF, width), BF),
+            pltpu.VMEM((HALF, width), BF),
+            pltpu.VMEM((HALF, width), BF),
+            pltpu.VMEM((HALF, width), F32),
+            pltpu.VMEM((HALF, 128), F32),
+            pltpu.VMEM((HALF, width), F32),
+            pltpu.VMEM((HALF, 128), F32),
         ]
+        scratch += held + [pltpu.SemaphoreType.DMA((16,)), pltpu.SemaphoreType.DMA((16,))]
         params.update(collective_id=0, has_side_effects=True)
     return pl.pallas_call(
         functools.partial(attention_forward_kernel, bool(own)),
@@ -407,21 +494,44 @@
     )(*args)
 
 
+class Staged:
+    def __init__(self, pairs, sems):
+        self.pairs, self.sems = pairs, sems
+
+    def copy(self, i):
+        return pltpu.make_async_copy(self.pairs[i][0], self.pairs[i][1], self.sems.at[i])
+
+    def start(self, numbers=None):
+        for i in range(len(self.pairs)) if numbers is None else numbers:
+            self.copy(i).start()
+
+    def wait(self, numbers=None):
+        for i in range(len(self.pairs)) if numbers is None else numbers:
+            self.copy(i).wait()
+
+
 class Mail:
     def __init__(self, send, recv):
         self.send, self.recv, self.started = send, recv, []
 
-    def post(self, source, target, peer, slot):
+    def post(self, source, target, peer, slot, when=None):
         number = len(self.started)
 
         def made():
             return pltpu.make_async_remote_copy(
-                src_ref=source(), dst_ref=target(), send_sem=self.send.at[number], recv_sem=self.recv.at[slot],
+                src_ref=source(), dst_ref=target(), send_sem=self.send.at[number],
+                recv_sem=self.recv.at[slot() if callable(slot) else slot],
                 device_id=peer, device_id_type=MESH,
             )
 
-        made().start()
-        self.started.append(made)
+        self.only(when, lambda: made().start())
+        self.started.append((made, when))
+
+    def only(self, when, do):
+        if when is None:
+            do()
+        else:
+            pl.when(when())(do)
 
     def arrived(self, view, slot, peer):
         pltpu.make_async_remote_copy(
@@ -430,8 +540,8 @@
         ).wait_recv()
 
     def finish(self):
-        for made in self.started:
-            made().wait_send()
+        for made, when in self.started:
+            self.only(when, lambda made=made: made().wait_send())
 
 
 def meet(peers):
@@ -442,7 +552,7 @@
 
 
 def summing_steps(refs, grad_maps):
-    maps_in, takers, all_e, all_a, e_got, e_two, e_own, a_in, a_part, a_z, a_own, send, recv, local = refs
+    maps_in, own_maps, takers, all_e, all_a, e_got, e_two, e_own, a_in, a_part, a_z, a_own, send, recv, local = refs
     mail = Mail(send, recv)
     dp, ex = lax.axis_index("dp"), lax.axis_index("expert")
     x, z = dp % 2, dp // 2
@@ -453,32 +563,45 @@
     along_z = {k: ((z + k) % 4) * 2 + x for k in range(1, 4)}
     plane = {(a, k): (other(dp, 1) if a else dp, (ex + k) % 4) for a in range(2) for k in range(4) if (a, k) != (0, 0)}
     x_peer, y_peer, s_peer = (other(dp, 1), ex), (dp, other(ex, 2)), (dp, other(ex, 1))
+    others = (other(ex, 1), other(ex, 2), other(other(ex, 1), 2))
+    spots = {(up, k): ((z + 4 - k) if up else (z + k)) % 4 for up in (True, False) for k in range(1, 4)}
+    reach = {(up, k): (z >= k) if up else (z + k < 4) for up in (True, False) for k in range(1, 4)}
+    above, below = (((z + 1) % 4) * 2 + x, ex), (((z + 3) % 4) * 2 + x, ex)
+    near = 2 * (ex // 2)
+    away = 2 - near
     free = [0]
 
     def slots(n):
         free[0] += n
         return free[0] - n
 
-    first = {n: slots(c) for n, c in dict(e1=4, e2=8, e3=4, e4=4, a1=8, a2=4, a3=4, ay=1, ax=2, a_s=4).items()}
+    first = {n: slots(c) for n, c in dict(e1=4, e2=8, e5=8, e3=4, e4=4, a1=8, a2=4, a3=4, ay=2, ax=1, a_s=4).items()}
 
     def begin():
         meet([(dp, group[k]) for k in group] + [(along[k], ex) for k in along] + [plane[1, k] for k in range(1, 4)])
-        for k, to in group.items():
-            mail.post(lambda to=to: maps_in.at[to], lambda: e_got.at[ex], (dp, to), first["e1"] + k)
-        pltpu.make_async_copy(maps_in.at[ex], e_got.at[ex], local.at[0]).start()
-
-    def spread_out():
-        for k in group:
-            source = (ex + 4 - k) % 4
-            mail.arrived(e_got.at[source], first["e1"] + k, (dp, source))
-        pltpu.make_async_copy(maps_in.at[ex], e_got.at[ex], local.at[0]).wait()
-
-        def columns(to):
-            return e_got.at[:, :, pl.ds(pl.multiple_of(to * share, 128), share)]
-
+        for i, to in enumerate(others):
+            mail.post(lambda to=to: maps_in.at[to], lambda: e_got.at[ex], (dp, to), first["e1"] + i)
+        pltpu.make_async_copy(own_maps, e_got.at[ex], local.at[0]).start()
+
+    def columns(refs, pair, to):
+        return refs.at[pl.ds(pair, 2), :, pl.ds(pl.multiple_of(to * share, 128), share)]
+
+    def spread_out(pair, slot):
         for k, to in along.items():
-            mail.post(lambda to=to: columns(to), lambda: e_two.at[dp], (to, ex), first["e2"] + k)
-        e_two[dp] = e_got[:, :, pl.ds(pl.multiple_of(dp * share, 128), share)]
+            mail.post(
+                lambda to=to: columns(e_got, pair, to), lambda: e_two.at[dp, pl.ds(pair, 2)], (to, ex), first[slot] + k
+            )
+        e_two[dp, pl.ds(pair, 2)] = e_got[pl.ds(pair, 2), :, pl.ds(pl.multiple_of(dp * share, 128), share)]
+
+    def spread_near():
+        mail.arrived(e_got.at[others[0]], first["e1"], s_peer)
+        pltpu.make_async_copy(own_maps, e_got.at[ex], local.at[0]).wait()
+        spread_out(near, "e2")
+
+    def spread_far():
+        for i in (1, 2):
+            mail.arrived(e_got.at[others[i]], first["e1"] + i, (dp, others[i]))
+        spread_out(away, "e5")
 
     def placed(sender, columns):
         row, column = iota((128, columns), 0), iota((128, columns), 1)
@@ -487,20 +610,36 @@
     def add_up():
         for k in along:
             source = (dp + 8 - k) % 8
-            mail.arrived(e_two.at[source], first["e2"] + k, (source, ex))
+            mail.arrived(e_two.at[source, pl.ds(near, 2)], first["e2"] + k, (source, ex))
+            mail.arrived(e_two.at[source, pl.ds(away, 2)], first["e5"] + k, (source, ex))
         rows = e_two[...].reshape(-1, share)
         e_own[...] = mm(placed(takers[...], rows.shape[0]), rows).astype(BF)
-        for k, to in along_z.items():
-            mail.post(lambda: e_own, lambda: all_e.at[dp], (to, ex), first["e3"] + k)
-        mail.post(lambda: e_own, lambda: all_e.at[dp], x_peer, first["e4"])
+        mail.post(lambda: e_own, lambda: all_e.at[dp], above, lambda: first["e3"] + z, lambda: z < 3)
+        mail.post(lambda: e_own, lambda: all_e.at[dp], below, lambda: first["e3"] + z, lambda: z > 0)
+        mail.post(lambda: e_own, lambda: all_e.at[dp], x_peer, lambda: first["e4"] + z)
         pltpu.make_async_copy(e_own, all_e.at[dp], local.at[1]).start()
 
-    def e_forward():
-        for k in along_z:
-            source = ((z + 4 - k) % 4) * 2 + x
-            mail.arrived(all_e.at[source], first["e3"] + k, (source, ex))
-            here = functools.partial(lambda source: all_e.at[source], source)
-            mail.post(here, here, x_peer, first["e4"] + k)
+    def e_forward(k):
+        for up in (True, False):
+            here = reach[up, k]
+            place = spots[up, k]
+
+            def take(place=place):
+                mail.arrived(all_e.at[place * 2 + x], first["e3"] + place, (place * 2 + x, ex))
+
+            def view(place=place):
+                return all_e.at[place * 2 + x]
+
+            mail.only(lambda here=here: here, take)
+            if up:
+                mail.post(
+                    view, view, above, lambda place=place: first["e3"] + place, lambda here=here: here & (z < 3)
+                )
+            else:
+                mail.post(
+                    view, view, below, lambda place=place: first["e3"] + place, lambda here=here: here & (z > 0)
+                )
+            mail.post(view, view, x_peer, lambda place=place: first["e4"] + place, lambda here=here: here)
 
     def a_share():
         for (a, k), to in plane.items():
@@ -551,31 +690,31 @@
 
         of_y, of_x = 2 * other(ex, 2) + x, 2 * ex + 1 - x
         of_xy = 2 * other(ex, 2) + 1 - x
+        send(mine, x_peer, first["ax"])
         send(mine, y_peer, first["ay"])
-        send(mine, x_peer, first["ax"])
         send(mine, s_peer, first["a_s"])
+        mail.arrived(all_a.at[of_x], first["ax"], x_peer)
+        send(of_x, y_peer, first["ay"] + 1)
+        send(of_x, s_peer, first["a_s"] + 1)
         mail.arrived(all_a.at[of_y], first["ay"], y_peer)
-        send(of_y, x_peer, first["ax"] + 1)
-        send(of_y, s_peer, first["a_s"] + 1)
-        mail.arrived(all_a.at[of_x], first["ax"], x_peer)
-        send(of_x, s_peer, first["a_s"] + 2)
-        mail.arrived(all_a.at[of_xy], first["ax"] + 1, x_peer)
+        send(of_y, s_peer, first["a_s"] + 2)
+        mail.arrived(all_a.at[of_xy], first["ay"] + 1, y_peer)
         send(of_xy, s_peer, first["a_s"] + 3)
 
     def end():
         sib = other(ex, 1)
-        numbers = (2 * sib + x, 2 * other(sib, 2) + x, 2 * sib + 1 - x, 2 * other(sib, 2) + 1 - x)
+        numbers = (2 * sib + x, 2 * sib + 1 - x, 2 * other(sib, 2) + x, 2 * other(sib, 2) + 1 - x)
         for i, number in enumerate(numbers):
             mail.arrived(all_a.at[number], first["a_s"] + i, s_peer)
         for k in range(4):
-            source = ((z + 4 - k) % 4) * 2 + 1 - x
-            mail.arrived(all_e.at[source], first["e4"] + k, x_peer)
+            mail.arrived(all_e.at[2 * k + 1 - x], first["e4"] + k, x_peer)
         pltpu.make_async_copy(e_own, all_e.at[dp], local.at[1]).wait()
         mail.finish()
 
     return {
-        "begin": [begin], 1: [spread_out], 10: [add_up], "maps": [a_share, e_forward], "half": [a_partial],
-        "end": [a_total, a_gather, end],
+        "begin": [begin], "outer": [spread_near], 1: [spread_far], 6: [add_up], 9: [functools.partial(e_forward, 1)],
+        "maps": [a_share], 101: [functools.partial(e_forward, 2)], 102: [a_partial],
+        "end": [a_total, functools.partial(e_forward, 3), a_gather, end],
     }
 
 
@@ -584,11 +723,25 @@
     xa_ref, q_ref, k_ref, v_ref, ob_ref, ua_ref, uo_ref, lse_ref = refs[11:19]
     steps = {}
     if exchange:
-        grad_tok, grad_maps, own = refs[21], refs[24], refs[36:]
-        steps = summing_steps((*refs[19:21], *refs[22:24], *own), grad_maps)
-        bias, dob, datt, duo, lse_t, center_t, dq, dk, dv, dlin, dua = refs[25:36]
+        grad_tok, grad_maps, own = refs[22], refs[25], refs[37:]
+        sums = (*refs[19:22], *refs[23:25])
+        bias, dob, datt, duo, lse_t, center_t, dq, dk, dv, dlin, dua = refs[26:37]
+        own, held = own[:10], own[10:]
+        width = wo.shape[0]
+        loads = (
+            dh1_ref, up_s, wo, down_ref, ob_ref, lse_ref, q_ref, k_ref, v_ref, cos, sin, ua_ref, xa_ref, uo_ref,
+            wqk, wqkv.at[:, pl.ds(2 * width, width)], tok,
+        )
+        load = Staged([*zip(loads, held), (held[17], grad_tok)], held[18])
+        (
+            dh1_ref, up_s, wo, down_ref, ob_ref, lse_ref, q_ref, k_ref, v_ref, cos, sin, ua_ref, xa_ref, uo_ref,
+            wqk, wv, tok,
+        ) = held[:17]
+        grad_tok = held[17]
+        steps = summing_steps((*sums, *own), grad_maps)
     else:
         grad_tok, grad_maps = refs[19:21]
+        wv = wqkv.at[:, pl.ds(2 * wo.shape[0], wo.shape[0])]
         bias, dob, datt, duo, lse_t, center_t, dq, dk, dv, dlin, dua = refs[21:]
     length, width = tok.shape
     groups = width // GROUP
@@ -598,8 +751,12 @@
             step()
 
     run("begin")
+    if exchange:
+        load.start(range(17))
     for half in range(length // HALF):
         bias[half] = span_bias(spans[half] - half * HALF, True)
+    if exchange:
+        load.wait(range(6))
     of_head = one_hot(iota((128, width), 1) // HD == iota((128, width), 0))
 
     def outer(block, carry):
@@ -615,9 +772,13 @@
         low = (both - high.astype(F32)).astype(BF)
         center_t[:, at] = mm_t(of_head, high) + mm_t(of_head, low)
         lse_t[:, at] = lse_ref[at, :].T
+        if steps:
+            pl.when(block == 0)(functools.partial(run, "outer"))
         return carry
 
     lax.fori_loop(0, length // 256, outer, 0)
+    if exchange:
+        load.wait(range(6, 9))
     dq[...] = jnp.zeros(dq.shape, F32)
     dk[...] = jnp.zeros(dk.shape, F32)
     dv[...] = jnp.zeros(dv.shape, F32)
@@ -649,11 +810,13 @@
             dk[at, lanes] += mm(ds, q * qk_own)
             dq[late, lanes] += t_mm(ds, kh)
         for point in steps:
-            if isinstance(point, int):
+            if isinstance(point, int) and point < 100:
                 pl.when(head == point)(functools.partial(run, point))
         return carry
 
     lax.fori_loop(0, HEADS, attend, 0)
+    if exchange:
+        load.wait(range(9, 17))
 
     def turn_back(block, carry):
         at = pl.ds(pl.multiple_of(block * 256, 256), 256)
@@ -685,22 +848,27 @@
     def inner(block, carry):
         at = pl.ds(pl.multiple_of(block * 256, 256), 256)
         d, u = dlin[at, :], dua[at, :]
-        dx = mm_t(d[:, : 2 * width], wqk[...]) + mm_t(d[:, 2 * width :], wqkv[:, pl.ds(2 * width, width)])
-        dx = (dx + mm_t(u, down_ref[0])) * gain_a[...]
+        dx = mm_t(d[:, : 2 * width], wqk[...]) + mm_t(d[:, 2 * width :], wv[...])
+        dx = (dx + mm_t(u, down_ref[0])) * gain_a[...][None]
         h0 = tok[at, :].astype(F32)
         r = lax.rsqrt(jnp.mean(h0 * h0, axis=1, keepdims=True) + EPS)
         pull = r * dx - h0 * (r * r * r * jnp.mean(dx * h0, axis=1, keepdims=True))
         grad_tok[at, :] = (dh1_ref[at, :] + pull).astype(BF)
-        if "half" in steps:
-            pl.when(block == 1)(functools.partial(run, "half"))
+        for point in steps:
+            if isinstance(point, int) and point >= 100:
+                pl.when(block == point - 100)(functools.partial(run, point))
         return carry
 
     lax.fori_loop(0, length // 256, inner, 0)
+    if exchange:
+        load.start([17])
     run("end")
+    if exchange:
+        load.wait([17])
 
 
 def attention_backward(
-    spans, dh1, tok, gain_a, wqkv, wqk, wo, down_s, up_s, xa, q, k, v, ob, ua, uo, lse, maps=None, takers=None
+    spans, dh1, tok, gain_a, wqkv, wqk, wo, down_s, up_s, xa, q, k, v, ob, ua, uo, lse, maps=None, own_maps=None, takers=None
 ):
     length, width = tok.shape
     cos, sin = rope_tables(length)
@@ -715,8 +883,11 @@
         out_specs.append(vmem)
     else:
         share = maps.shape[2] // 8
-        in_specs += [anys, vmem]
-        args += (maps, takers)
+        in_specs = [smem] + [vmem if a.ndim == 1 else anys for a in args[1:]] + [anys, anys, vmem]
+        held = [dh1, up_s, wo, down_s, ob, lse, q, k, v, cos, sin, ua, xa, uo, wqk, wo, tok, tok]
+        held = [pltpu.VMEM(a.shape, a.dtype) for a in held]
+        args += (maps, own_maps, takers)
+        out_specs = [anys]
         shapes += [((8, 128, share), BF), ((8, 128, width), BF)]
         out_specs += [anys] * 2
         scratch.append(compact)
@@ -745,7 +916,8 @@
             ((4, 32, width), BF),
             ((32, width), BF),
         ]
-        semaphores = [pltpu.SemaphoreType.DMA((48,)), pltpu.SemaphoreType.DMA((48,)), pltpu.SemaphoreType.DMA((3,))]
+        semaphores = [pltpu.SemaphoreType.DMA((64,)), pltpu.SemaphoreType.DMA((64,)), pltpu.SemaphoreType.DMA((3,))]
+        semaphores += [*held, pltpu.SemaphoreType.DMA((18,))]
         params.update(collective_id=1, has_side_effects=True)
     return pl.pallas_call(
         functools.partial(attention_backward_kernel, maps is not None),
@@ -806,87 +978,137 @@
     return high, (x - high.astype(F32)).astype(BF)
 
 
+def route(lin_ref, carried, routes, numbers, info_t, place_t):
+    kinds, length = carried.shape
+    target = iota((kinds, length), 0)
+    logits = lin_ref[...].T[:kinds] + carried[...]
+    picks = [target == routes[k : k + 1, :] for k in range(2)]
+    chosen = [jnp.sum(jnp.where(p, logits, 0.0), axis=0, keepdims=True) for p in picks]
+    top = jnp.maximum(*chosen)
+    parts = [jnp.exp(c - top) for c in chosen]
+    total = parts[0] + parts[1]
+    info_t[...] = jnp.zeros(info_t.shape, F32)
+    info_t[:kinds, :] = jnp.where(picks[0], parts[0] / total, jnp.where(picks[1], parts[1] / total, 0.0))
+    wide = iota((128, length), 0)
+    named = [(wide == routes[k : k + 1, :]) & (wide < numbers) for k in range(2)]
+    member = one_hot(named[0] | named[1])
+    for block in range(length // 256):
+        before = one_hot(iota((256, length), 1) < iota((256, length), 0) + block * 256)
+        place_t[:, pl.ds(block * 256, 256)] = mm_t(member, before)
+    place_t[...] = jnp.where(named[0] | named[1], place_t[...], -1.0)
+    return named, member
+
+
+def padded_rows(part, before=0):
+    columns = part.shape[1]
+    parts = [jnp.zeros((before, columns), BF), part, jnp.zeros((128 - RANK - before, columns), BF)]
+    return jnp.concatenate(parts if before else parts[1:], axis=0)
+
+
+def take_rows(n, places, gates, xb, cot):
+    own = iota((n, xb.shape[0]), 0).astype(F32) == places
+    taken = one_hot(own)
+    x = mm(taken, xb[...]).astype(BF)
+    c = mm(taken, cot[...]).astype(BF)
+    g = jnp.sum(jnp.where(own, gates, 0.0), axis=1, keepdims=True)
+    return x, c, g, (g * c.astype(F32)).astype(BF)
+
+
+def hidden_tile(x, dy, ug, dud, w_gate, w_up, w_down, b_gate, b_up, a_dn):
+    gate = mm(x, w_gate) + mm(ug, b_gate)
+    up = mm(x, w_up) + mm(ug, b_up)
+    sig = 1.0 / (1.0 + jnp.exp(-gate))
+    act = gate * sig
+    hid = (act * up).astype(BF)
+    dhid = mm_t(dy, w_down) + mm(dud, a_dn)
+    dup = (dhid * act).astype(BF)
+    dgate = (dhid * up * (sig + act * (1.0 - sig))).astype(BF)
+    y = mm(hid, w_down)
+    ud = mm_t(hid, a_dn)
+    dx = mm_t(dgate, w_gate) + mm_t(dup, w_up)
+    dug = mm_t(dgate, b_gate) + mm_t(dup, b_up)
+    ug_t = ug.T
+    grads = mm(ug_t[:RANK], dgate), mm(ug_t[RANK : 2 * RANK], dup), mm(dud.T[:RANK], hid)
+    return (y, ud, dx, dug), [g.astype(BF) for g in grads]
+
+
+def close_rows(expert, sums, x, c, g, dy, a_gu, b_dn):
+    y, ud, dx, dug = sums
+    ud, dug = ud.astype(BF), dug.astype(BF)
+    y = y + mm(ud, b_dn)
+    high, low = split(jnp.sum(c.astype(F32) * y.astype(BF).astype(F32), axis=1, keepdims=True))
+    lane = iota((1, 128), 1)
+    high, low = high.astype(F32), low.astype(F32)
+    both = (
+        (g * y).astype(BF),
+        (dx + mm(dug, a_gu)).astype(BF),
+        jnp.where(lane == expert, high, jnp.where(lane == expert + 64, low, 0.0)).astype(BF),
+    )
+    to_a = mm(dug.T[: 2 * RANK], x).astype(BF)
+    return both, (to_a[:RANK], to_a[RANK:], mm(ud.T[:RANK], dy).astype(BF))
+
+
 def experts_kernel(
-    xb, h1_ref, lin_ref, cot, routes, carried, gain_m, wr, vectors,
+    own_first, order, xb, h1_ref, lin_ref, cot, routes, carried, gain_m, wr, vectors, own_both,
     w_gate, w_up, w_down, maps,
     result, dh1_ref, grads,
-    count, gates, gates_t, place, place_t, both, x_s, c_s, dy_s, g_s, y_acc, dx_acc, ug_s, ud_acc, dud_s, dug_acc,
-    a_gu, b_dn, acc,
+    count, info, info_t, place_t, both, x_s, c_s, dy_s, g_s, y_acc, dx_acc, ug_s, ud_acc, dud_s, dug_acc, a_gu, b_dn, acc,
 ):
-    e, j = pl.program_id(0), pl.program_id(1)
-    experts, tiles = pl.num_programs(0), pl.num_programs(1)
+    step, j = pl.program_id(0), pl.program_id(1)
+    steps, tiles = pl.num_programs(0), pl.num_programs(1)
+    e = order[step]
     length, width = xb.shape
-    kinds = carried.shape[1]
+    kinds = carried.shape[0]
     numbers = kinds - 4
     tile = w_gate.shape[2]
     hidden = (maps.shape[2] - 3 * width) // 3
     rows_of = 128
-
-    def padded_rows(start, number, before=0):
-        part = maps[0, :, pl.ds(start, number)]
-        parts = [jnp.zeros((before, number), BF), part, jnp.zeros((128 - RANK - before, number), BF)]
-        return jnp.concatenate(parts if before else parts[1:], axis=0)
-
-    @pl.when((e == 0) & (j == 0))
+    skip = HALF if own_first else 0
+
+    if grads.shape[2] > maps.shape[2]:
+        grads[0, :, maps.shape[2] :] = jnp.zeros((RANK, grads.shape[2] - maps.shape[2]), BF)
+
+    @pl.when((step == 0) & (j == 0))
     def _():
-        lane = iota((1, kinds), 1)
-        logits = lin_ref[:, :kinds] + carried[...]
-        picks = [lane == routes[:, k : k + 1] for k in range(2)]
-        chosen = [jnp.sum(jnp.where(p, logits, 0.0), axis=1, keepdims=True) for p in picks]
-        top = jnp.maximum(*chosen)
-        parts = [jnp.exp(c - top) for c in chosen]
-        total = parts[0] + parts[1]
-        gates[...] = jnp.zeros(gates.shape, F32)
-        gates[:, :kinds] = jnp.where(picks[0], parts[0] / total, jnp.where(picks[1], parts[1] / total, 0.0))
-        wide = iota((1, 128), 1)
-        named = [(wide == routes[:, k : k + 1]) & (wide < numbers) for k in range(2)]
-        member = one_hot(named[0] | named[1])
-        for block in range(length // 256):
-            before = one_hot(iota((256, length), 1) < iota((256, length), 0) + block * 256)
-            place[pl.ds(block * 256, 256), :] = mm(before, member)
-        counts = jnp.sum(member.astype(F32), axis=0, keepdims=True)
+        named, member = route(lin_ref, carried, routes, numbers, info_t, place_t)
+        number = iota((128, 1), 0)
+        counts = jnp.sum(member.astype(F32), axis=1, keepdims=True)
         padded = jnp.floor((counts + (rows_of - 1)) * (1.0 / rows_of))
-        earlier = one_hot(iota((128, 128), 0) < iota((128, 128), 1))
-        starts = rows_of * mm(jnp.broadcast_to(padded, (8, 128)).astype(BF), earlier)[:1]
-        own = jnp.where(named[0] | named[1], place[...], -1.0)
-        place_t[...] = own.T
-        gates_t[...] = gates[...].T
-        spots = [
-            jnp.sum(jnp.where(n, place[...] + starts + 1.0, 0.0), axis=1, keepdims=True) - 1.0 for n in named
-        ]
-        place[...] = jnp.where(wide == 0, spots[0], spots[1])
+        if own_first:
+            padded = jnp.where(number == lax.axis_index("expert"), 0.0, padded)
+        earlier = one_hot(iota((128, 128), 1) < iota((128, 128), 0))
+        starts = rows_of * mm(earlier, jnp.broadcast_to(padded, (128, 128)).astype(BF))[:, :1]
+        slots = starts + skip
+        if own_first:
+            slots = jnp.where(number == lax.axis_index("expert"), 0.0, slots)
+        at_slot = place_t[...] + slots
+        for k in range(2):
+            spot = jnp.sum(jnp.where(named[k], at_slot + 1.0, 0.0), axis=0, keepdims=True) - 1.0
+            info_t[pl.ds(64 + k, 1), :] = spot
+        info[...] = info_t[...].T
         for i in range(numbers):
-            mine = wide == i
-            count[0, i] = jnp.sum(jnp.where(mine, padded, 0.0)).astype(jnp.int32)
-            count[1, i] = jnp.sum(jnp.where(mine, starts, 0.0)).astype(jnp.int32)
-        count[1, numbers] = jnp.sum(jnp.where(wide < numbers, padded, 0.0)).astype(jnp.int32) * rows_of
+            count[0, i] = jnp.sum(jnp.where(number == i, padded, 0.0)).astype(jnp.int32)
+            count[1, i] = jnp.sum(jnp.where(number == i, starts, 0.0)).astype(jnp.int32)
+        count[1, numbers] = jnp.sum(jnp.where(number < numbers, padded, 0.0)).astype(jnp.int32) * rows_of
 
     blocks = count[0, e]
     first = pl.multiple_of(count[1, e], rows_of)
 
     @pl.when((j == 0) & (blocks > 0))
     def _():
-        a_gu[...] = padded_rows(0, width) + padded_rows(width, width, RANK)
-        b_dn[...] = padded_rows(2 * width + 3 * hidden, width)
+        a_gu[...] = padded_rows(maps[0, :, :width]) + padded_rows(maps[0, :, width : 2 * width], RANK)
+        b_dn[...] = padded_rows(maps[0, :, 2 * width + 3 * hidden :])
 
     @pl.when((j == 0) & (blocks == 0))
     def _():
         grads[...] = jnp.zeros(grads.shape, BF)
 
-    if grads.shape[2] > maps.shape[2]:
-        grads[0, :, maps.shape[2] :] = jnp.zeros((RANK, grads.shape[2] - maps.shape[2]), BF)
-
     def work(n):
         rows = pl.ds(0, n)
 
         @pl.when(j == 0)
         def _():
-            own = iota((n, length), 0).astype(F32) == place_t[pl.ds(e, 1), :]
-            taken = one_hot(own)
-            x = mm(taken, xb[...]).astype(BF)
-            c = mm(taken, cot[...]).astype(BF)
-            g = jnp.sum(jnp.where(own, gates_t[pl.ds(e, 1), :], 0.0), axis=1, keepdims=True)
-            dy = (g * c.astype(F32)).astype(BF)
+            x, c, g, dy = take_rows(n, place_t[pl.ds(e, 1), :], info_t[pl.ds(e, 1), :], xb, cot)
             x_s[rows, :] = x
             c_s[rows, :] = c
             dy_s[rows, :] = dy
@@ -894,67 +1116,43 @@
             ug_s[rows, :] = mm_t(x, a_gu[...]).astype(BF)
             dud_s[rows, :] = mm_t(dy, b_dn[...]).astype(BF)
 
-        x, dy, ug, dud = x_s[rows, :], dy_s[rows, :], ug_s[rows, :], dud_s[rows, :]
         at = pl.multiple_of(j * tile, tile)
-        b_gate = padded_rows(2 * width + at, tile)
-        b_up = padded_rows(2 * width + hidden + at, tile, RANK)
-        a_dn = padded_rows(2 * width + 2 * hidden + at, tile)
-        gate = mm(x, w_gate[0]) + mm(ug, b_gate)
-        up = mm(x, w_up[0]) + mm(ug, b_up)
-        sig = 1.0 / (1.0 + jnp.exp(-gate))
-        act = gate * sig
-        hid = (act * up).astype(BF)
-        dhid = mm_t(dy, w_down[0]) + mm(dud, a_dn)
-        dup = (dhid * act).astype(BF)
-        dgate = (dhid * up * (sig + act * (1.0 - sig))).astype(BF)
-        y = mm(hid, w_down[0])
-        ud = mm_t(hid, a_dn)
-        dx = mm_t(dgate, w_gate[0]) + mm_t(dup, w_up[0])
-        dug = mm_t(dgate, b_gate) + mm_t(dup, b_up)
-        ug_t = ug.T
-        grads[0, :, pl.ds(2 * width + at, tile)] = mm(ug_t[:RANK], dgate).astype(BF)
-        grads[0, :, pl.ds(2 * width + hidden + at, tile)] = mm(ug_t[RANK : 2 * RANK], dup).astype(BF)
-        grads[0, :, pl.ds(2 * width + 2 * hidden + at, tile)] = mm(dud.T[:RANK], hid).astype(BF)
+        starts = [2 * width + i * hidden + at for i in range(3)]
+        sums, parts = hidden_tile(
+            x_s[rows, :], dy_s[rows, :], ug_s[rows, :], dud_s[rows, :], w_gate[0], w_up[0], w_down[0],
+            padded_rows(maps[0, :, pl.ds(starts[0], tile)]),
+            padded_rows(maps[0, :, pl.ds(starts[1], tile)], RANK),
+            padded_rows(maps[0, :, pl.ds(starts[2], tile)]),
+        )
+        for start, part in zip(starts, parts):
+            grads[0, :, pl.ds(start, tile)] = part
+        kept = (y_acc, ud_acc, dx_acc, dug_acc)
 
         @pl.when(j == 0)
         def _():
-            y_acc[rows, :] = y
-            dx_acc[rows, :] = dx
-            ud_acc[rows, :] = ud
-            dug_acc[rows, :] = dug
+            for ref, value in zip(kept, sums):
+                ref[rows, :] = value
 
         @pl.when(j > 0)
         def _():
-            y_acc[rows, :] += y
-            dx_acc[rows, :] += dx
-            ud_acc[rows, :] += ud
-            dug_acc[rows, :] += dug
+            for ref, value in zip(kept, sums):
+                ref[rows, :] += value
 
         @pl.when(j == tiles - 1)
         def _():
-            ud = ud_acc[rows, :].astype(BF)
-            dug = dug_acc[rows, :].astype(BF)
-            y = y_acc[rows, :] + mm(ud, b_dn[...])
-            g = g_s[rows, :][:, :1]
-            dg = jnp.sum(c_s[rows, :].astype(F32) * y.astype(BF).astype(F32), axis=1, keepdims=True)
-            high, low = split(dg)
-            lane = iota((1, 128), 1)
+            out, parts = close_rows(
+                e, [ref[rows, :] for ref in kept], x_s[rows, :], c_s[rows, :], g_s[rows, :][:, :1], dy_s[rows, :],
+                a_gu[...], b_dn[...],
+            )
             to = pl.ds(first, n)
-            both[to, :width] = (g * y).astype(BF)
-            both[to, width : 2 * width] = (dx_acc[rows, :] + mm(dug, a_gu[...])).astype(BF)
-            both[to, 2 * width :] = jnp.where(
-                lane == e, high.astype(F32), jnp.where(lane == e + 64, low.astype(F32), 0.0)
-            ).astype(BF)
-            x, dy = x_s[rows, :], dy_s[rows, :]
-            to_a = mm(dug.T[: 2 * RANK], x).astype(BF)
-            grads[0, :, :width] = to_a[:RANK]
-            grads[0, :, width : 2 * width] = to_a[RANK:]
-            grads[0, :, 2 * width + 3 * hidden : 3 * width + 3 * hidden] = mm(ud.T[:RANK], dy).astype(BF)
+            both[to, :width], both[to, width : 2 * width], both[to, 2 * width :] = out
+            grads[0, :, :width], grads[0, :, width : 2 * width] = parts[:2]
+            grads[0, :, 2 * width + 3 * hidden : 3 * width + 3 * hidden] = parts[2]
 
     for number in range(1, 512 // rows_of + 1):
         pl.when(blocks == number)(functools.partial(work, number * rows_of))
 
-    @pl.when((e == experts - 1) & (j == tiles - 1))
+    @pl.when((step == steps - 1) & (j == tiles - 1))
     def _():
         used = count[1, numbers]
         both[pl.ds(pl.multiple_of(used, rows_of), HALF), :] = jnp.zeros((HALF, both.shape[1]), BF)
@@ -962,24 +1160,30 @@
 
         def combine(block, carry):
             at = pl.ds(pl.multiple_of(block * 256, 256), 256)
-            acc[...] = jnp.zeros(acc.shape, F32)
-            spots = place[at, :]
+            g = info[at, :]
+            spots = g[:, 64:66]
+
+            def taken(start):
+                slot = (iota((256, HALF), 1) + start).astype(F32)
+                return one_hot((slot == spots[:, :1]) | (slot == spots[:, 1:2]))
+
+            if own_first:
+                acc[...] = mm(taken(0), own_both[...])
+            else:
+                acc[...] = jnp.zeros(acc.shape, F32)
 
             def add(part, carry):
                 k0 = pl.multiple_of(part * HALF, HALF)
-                slot = (iota((256, HALF), 1) + k0).astype(F32)
-                taken = one_hot((slot == spots[:, :1]) | (slot == spots[:, 1:2]))
-                acc[...] += mm(taken, both[pl.ds(k0, HALF), :])
+                acc[...] += mm(taken(k0 + skip), both[pl.ds(k0, HALF), :])
                 return carry
 
             lax.fori_loop(0, (used + HALF - 1) // HALF, add, 0)
             h1 = h1_ref[at, :]
             ct = cot[at, :].astype(F32)
             r = lax.rsqrt(jnp.mean(h1 * h1, axis=1, keepdims=True) + EPS)
-            gain = gain_m[...]
+            gain = gain_m[...][None]
             n2 = h1 * r * gain
             lin = lin_ref[at, :]
-            g = gates[at, :]
             gc = g[:, numbers + 1 : numbers + 2]
             g_fix = [g[:, numbers + 2 + i : numbers + 3 + i] for i in range(2)]
             mixes = []
@@ -1000,12 +1204,13 @@
             dg = jnp.where(lane == numbers + 1, a, dg)
             for i in range(2):
                 dg = jnp.where(lane == numbers + 2 + i, mixes[i][0] * a + mixes[i][1] * bs[i], dg)
+            g = jnp.where(lane < kinds, g, 0.0)
             dlin = g * (dg - jnp.sum(g * dg, axis=1, keepdims=True))
             for i in range(2):
                 pull = mixes[i][0] * mixes[i][1] * (g_fix[i] * (a - bs[i]))
                 dlin = jnp.where(lane == kinds + 2 * i, pull, jnp.where(lane == kinds + 2 * i + 1, -pull, dlin))
             high, low = split(dlin)
-            dn2 = acc[:, width : 2 * width] + (mm_t(high, wr[...]) + mm_t(low, wr[...])) + ct * to_n2
+            dn2 = acc[:, width : 2 * width] + (mm(high, wr[...]) + mm(low, wr[...])) + ct * to_n2
             dn2 = dn2 * gain
             back = r * dn2 - h1 * (r * r * r * jnp.mean(dn2 * h1, axis=1, keepdims=True))
             dh1_ref[at, :] = ct + back
@@ -1014,7 +1219,7 @@
         lax.fori_loop(0, length // 256, combine, 0)
 
 
-def experts_both_ways(xb, h1, lin, cot, routes, carried, gain_m, wr, vectors, w_gu, w_dn, maps, copies):
+def experts_both_ways(xb, h1, lin, cot, routes, carried, gain_m, wr, vectors, w_gu, w_dn, maps, copies, own_both=None):
     length, width = xb.shape
     experts, hidden = w_dn.shape[0], w_dn.shape[1]
     tile = hidden // 2
@@ -1024,34 +1229,41 @@
     padded = -(-total // (copies * 128)) * copies * 128
 
     def whole(a):
-        return pl.BlockSpec(a.shape, lambda e, j: (0,) * a.ndim, pipeline_mode=pl.Buffered(1))
-
-    resident = (xb, h1, lin, cot, routes, carried, gain_m, wr, vectors)
+        return pl.BlockSpec(a.shape, lambda e, j, order: (0,) * a.ndim, pipeline_mode=pl.Buffered(1))
+
+    own_first = own_both is not None
+    if own_first:
+        order = (lax.axis_index("expert") + jnp.arange(1, experts, dtype=jnp.int32)) % experts
+    else:
+        order = jnp.arange(experts, dtype=jnp.int32)
+        own_both = jnp.zeros((16, 128), BF)
+    resident = (xb, h1, lin, cot, routes, carried, gain_m, wr, vectors, own_both)
     return pl.pallas_call(
-        experts_kernel,
-        grid=(experts, tiles),
+        functools.partial(experts_kernel, own_first),
         out_shape=[
             jax.ShapeDtypeStruct((length, width), BF),
             jax.ShapeDtypeStruct((length, width), F32),
             jax.ShapeDtypeStruct((experts, RANK, padded), BF),
         ],
-        in_specs=[whole(a) for a in resident]
-        + [
-            pl.BlockSpec((1, width, tile), lambda e, j: (e, 0, j)),
-            pl.BlockSpec((1, width, tile), lambda e, j: (e, 0, tiles + j)),
-            pl.BlockSpec((1, tile, width), lambda e, j: (e, j, 0)),
-            pl.BlockSpec((1, RANK, total), lambda e, j: (e, 0, 0)),
-        ],
-        out_specs=[
-            pl.BlockSpec((length, width), lambda e, j: (0, 0), pipeline_mode=pl.Buffered(1)),
-            pl.BlockSpec((length, width), lambda e, j: (0, 0), pipeline_mode=pl.Buffered(1)),
-            pl.BlockSpec((1, RANK, padded), lambda e, j: (e, 0, 0)),
-        ],
-        scratch_shapes=[
+        grid_spec=pltpu.PrefetchScalarGridSpec(
+            num_scalar_prefetch=1,
+            grid=(order.shape[0], tiles),
+            in_specs=[whole(a) for a in resident]
+            + [
+                pl.BlockSpec((1, width, tile), lambda e, j, order: (order[e], 0, j)),
+                pl.BlockSpec((1, width, tile), lambda e, j, order: (order[e], 0, tiles + j)),
+                pl.BlockSpec((1, tile, width), lambda e, j, order: (order[e], j, 0)),
+                pl.BlockSpec((1, RANK, total), lambda e, j, order: (order[e], 0, 0)),
+            ],
+            out_specs=[
+                pl.BlockSpec((length, width), lambda e, j, order: (0, 0), pipeline_mode=pl.Buffered(1)),
+                pl.BlockSpec((length, width), lambda e, j, order: (0, 0), pipeline_mode=pl.Buffered(1)),
+                pl.BlockSpec((1, RANK, padded), lambda e, j, order: (order[e], 0, 0)),
+            ],
+            scratch_shapes=[
             pltpu.SMEM((2, experts + 1), jnp.int32),
             pltpu.VMEM((length, 128), F32),
             pltpu.VMEM((128, length), F32),
-            pltpu.VMEM((length, 128), F32),
             pltpu.VMEM((128, length), F32),
             pltpu.VMEM((most + HALF, 2 * width + 128), BF),
             pltpu.VMEM((512, width), BF),
@@ -1068,9 +1280,10 @@
             pltpu.VMEM((128, width), BF),
             pltpu.VMEM((256, 2 * width + 128), F32),
         ],
+        ),
         compiler_params=pltpu.CompilerParams(vmem_limit_bytes=60 * MIB),
         name="experts_both_ways",
-    )(*resident, w_gu, w_gu, w_dn, maps)
+    )(order, *resident, w_gu, w_gu, w_dn, maps)
 
 
 def gather_experts(weights, senders):
@@ -1126,33 +1339,30 @@
     hidden = expert_down_weight.shape[1]
     first = lax.axis_index("dp") * groups
     senders = lax.dynamic_slice_in_dim(sequence_adapter_index, first, groups, 0)
-    adapter = lax.dynamic_slice_in_dim(senders, lax.axis_index("expert"), 1, 0)
-    gain_a, gain_m = attention_norm_gain[None], experts_norm_gain[None]
     spans = picture_span_starts.reshape(-1)
-    router = jnp.concatenate([router_weight, constant_expert_mixing], axis=1)
-    router = jnp.pad(router, ((0, 0), (0, 128 - router.shape[1])))
     own = (
         expert_gate_up_weight, expert_down_weight, adapter_expert_gate_up_down_maps,
         adapter_expert_gate_up_up_maps, adapter_expert_down_down_maps, adapter_expert_down_up_maps,
     )
     outs = attention_forward(
-        tokens, gain_a, query_key_value_weight, adapter_attention_down_maps, adapter_query_key_value_up_maps,
-        attention_output_weight, adapter_output_up_map, gain_m, router, spans, adapter,
-        *((own, senders) if exchange else ()),
+        tokens, attention_norm_gain, query_key_value_weight, adapter_attention_down_maps, adapter_query_key_value_up_maps,
+        attention_output_weight, adapter_output_up_map, experts_norm_gain, router_weight.T, constant_expert_mixing.T,
+        spans, sequence_adapter_index,
+        (*own, cotangent, routes.T, router_logits_carried.T) if exchange else (),
     )
-    xa, q, k, v, ob, ua, uo, lse, h1, xb, lin, wqk, down_s, up_s = outs[:14]
-    weights = outs[14:] if exchange else gather_experts(own, senders)
+    xa, q, k, v, ob, ua, uo, lse, h1, xb, lin, wqk, down_s, up_s, wr = outs[:15]
+    weights = outs[15:18] if exchange else gather_experts(own, senders)
     result, dh1, expert_maps = experts_both_ways(
-        xb, h1, lin, cotangent, routes, router_logits_carried, gain_m, router, constant_expert_vectors, *weights,
-        lax.axis_size("dp"),
+        xb, h1, lin, cotangent, routes.T, router_logits_carried.T, experts_norm_gain, wr, constant_expert_vectors, *weights,
+        lax.axis_size("dp"), outs[18] if exchange else None,
     )
     backward = functools.partial(
-        attention_backward, spans, dh1, tokens, gain_a, query_key_value_weight, wqk, attention_output_weight, down_s, up_s,
+        attention_backward, spans, dh1, tokens, attention_norm_gain, query_key_value_weight, wqk, attention_output_weight, down_s, up_s,
         xa, q, k, v, ob, ua, uo, lse,
     )
     if exchange:
         takers = jnp.repeat(sequence_adapter_index, RANK)[None]
-        grad_tokens, all_e, all_a = backward(expert_maps, takers)
+        grad_tokens, all_e, all_a = backward(expert_maps, outs[19], takers)
         return (result, grad_tokens, *unpack(all_e, all_a, hidden))
     grad_tokens, attention_maps = backward()
     to = (sequence_adapter_index[:, None] * RANK + jnp.arange(RANK)[None, :]).reshape(-1)

time: 352 us -> 299 us (0.85)
  Pallas kernels: 337 us -> 290 us
  local copies, waits for them, and re-layouts: 12.9 us -> 4.95 us
    pallas_call x1, Pallas kernels: 124 us -> 97.2 us  [attention_backward(): pl.pallas_call(functools.partial(attention_backward_kernel, maps is not N...]
    pallas_call x1, Pallas kernels: 102 us -> 84.5 us  [experts_both_ways(): pl.pallas_call(functools.partial(experts_kernel, own_first), out_shape=[j...]
where the time goes in v4:
time: 299 us; the launch traced here: 296 us
  Pallas kernels  290 us (97%)
  local copies, waits for them, and re-layouts  4.95 us (2%)
    pallas_call x1, Pallas kernels, attention_forward(): pl.pallas_call(functools.partial(attention_forward_kernel, bool(own)), ou...  105 us
    pallas_call x1, Pallas kernels, attention_backward(): pl.pallas_call(functools.partial(attention_backward_kernel, maps is not N...  97.2 us
    pallas_call x1, Pallas kernels, experts_both_ways(): pl.pallas_call(functools.partial(experts_kernel, own_first), out_shape=[j...  84.5 us

profile of v4, /device:TPU:0, one launch (start us, length us, event | category | flops | bytes accessed | tf_op | source)
XLA Modules:
  0.0 296.3 jit_solution(264630795232812509)
XLA Ops:
  0.6 104.8 %attention_forward.1 = (bf16[1024,768]{1,0:T(8,128)(2,1)}, bf16[1024,768]{1,0:T(8,128)(2,1)}, bf16[1024,768]{1,0:T(8,128)(2,1)}, bf16[1024,768]{1,0:T(8,128)(2,1...) custom-call(s32[2]{0:T(128)} %bitcast.11, ...), custom_call_target="tpu_custom_call" | custom-call | tf_op jit(solution)/shard_map/attention_forward/pallas_call | solution.py:486
  105.4 0.5 and_select_fusion.order
  105.9 0.0 copy-start.3
  106.0 84.5 %experts_both_ways.1 = (bf16[1024,768]{1,0:T(8,128)(2,1)}, f32[1024,768]{1,0:T(8,128)}, bf16[4,16,9216]{2,1,0:T(8,128)(2,1)}) custom-call(s32[3]{0:T(128)} %and_select_fusion.order, bf16[1024,768]{1,0:T(8,128)(2,1)} %get-tuple-element.42.xb, f32[1024,768]{1,0:T(8,128)} %get-tuple-element.43.h1_ref, f32[1024,128]{1,0:T(8,128)} %get-tuple-element.44.lin_ref, ...), custom_call_target="tpu_custom_call" | custom-call | tf_op jit(solution)/shard_map/experts_both_ways/pallas_call | solution.py:1241
  190.5 0.0 copy-done.3
  190.5 0.1 broadcast_in_dim.3
  190.6 0.7 broadcast_in_dim_reshape.3.refs_21_
  191.2 97.2 %attention_backward.1 = (bf16[1024,768]{1,0:T(8,128)(2,1)}, bf16[8,128,1152]{2,1,0:T(8,128)(2,1)}, bf16[8,128,768]{2,1,0:T(8,128)(2,1)}) custom-call(s32[2]{0:T(128)} %bitcast.12, f32[1024,768]{1,0:T(8,128)} %get-tuple-element.51.refs_1_, bf16[1024,768]{1,0:T(8,128)(2,1)} %refs_2_.3, f32[768]{0:T(1024)} %refs_3_.3, bf16[768,2304]{1,0:T(8,128)(2,1)} %refs_4_.3, ...), custom_call_target="tpu_custom_call" | custom-call | tf_op jit(solution)/shard_map/attention_backward/pallas_call | solution.py:922
  288.5 0.0 copy-start
  288.5 1.7 copy-done
  290.1 0.0 copy-start.1
  290.1 1.4 copy-done.1
  291.5 0.0 copy-start.2
  291.5 3.3 %unpack.1 = (f32[4,768,128]{2,1,0:T(8,128)}, f32[3,128,768]{2,1,0:T(8,128)}, f32[128,768]{1,0:T(8,128)}, f32[1,2,768,128]{3,2,1,0:T(8,128)}, f32[1,2,128,2048]{3...) custom-call(bf16[8,128,1152]{2,1,0:T(8,128)(2,1)S(1)} %copy-done, bf16[8,128,768]{2,1,0:T(8,128)(2,1)S(1)} %copy-done.1), custom_call_target="tpu_custom_call" | custom-call | tf_op jit(solution)/shard_map/unpack/pallas_call | solution.py:966
  294.8 0.0 copy-done.2
  294.8 1.1 copy.36
Async XLA Ops:
  105.9 84.5 %copy-start.3 = (s32[32]{0:T(128)S(1)}, s32[32]{0:T(128)}, u32[]{:S(2)}) copy-start(s32[32]{0:T(128)} %refs_1_.1) | copy-start | bytes 388
  288.5 1.7 copy-start
  290.1 1.4 copy-start.1
  291.5 3.3 %copy-start.2 = (bf16[1024,768]{1,0:T(8,128)(2,1)S(1)}, bf16[1024,768]{1,0:T(8,128)(2,1)}, u32[]{:S(2)}) copy-start(bf16[1024,768]{1,0:T(8,128)(2,1)} %get-tuple-element.85) | copy-start | bytes 4718596

commit v5 on v4

--- a/solution.py
+++ b/solution.py
@@ -171,6 +171,8 @@
         for at, part in parts:
             for i in range(4):
                 compact[i, :, pl.ds(at, part.shape[1])] = part[i * RANK : (i + 1) * RANK].astype(BF)
+
+    def send_maps():
         for i, (peer, to) in enumerate((("s", sibling), ("y", far), ("d", other(far, 1)))):
             copies(lambda to=to: [compact.at[to]], lambda: [all_maps.at[ex]], peer, 2 * count + 1 + i)
         pltpu.make_async_copy(compact.at[ex], all_maps.at[ex], local.at[2]).start()
@@ -204,15 +206,25 @@
 
         return step
 
+    def change():
+        for i in range(2):
+            pltpu.make_async_copy(bounce[i], targets[i].at[ex], local.at[i]).wait()
+            arrived(targets[i].at[sibling], 2 * count, i)
+            pltpu.make_async_copy(targets[i].at[sibling], bounce[i], local.at[i]).start()
+        pltpu.make_async_copy(compact.at[ex], all_maps.at[ex], local.at[2]).wait()
+        arrived(all_maps.at[sibling], 2 * count + 1, 0)
+        pltpu.make_async_copy(all_maps.at[sibling], compact.at[ex], local.at[2]).start()
+
+    def changed():
+        for i in range(2):
+            pltpu.make_async_copy(targets[i].at[sibling], bounce[i], local.at[i]).wait()
+        pltpu.make_async_copy(all_maps.at[sibling], compact.at[ex], local.at[2]).wait()
+
     def end():
         for made in started:
             made().wait_send()
-        for i in range(2):
-            pltpu.make_async_copy(bounce[i], targets[i].at[ex], local.at[i]).wait()
-            arrived(targets[i].at[sibling], 2 * count, i)
-        pltpu.make_async_copy(compact.at[ex], all_maps.at[ex], local.at[2]).wait()
-        for i, source in enumerate((sibling, far, other(far, 1))):
-            arrived(all_maps.at[source], 2 * count + 1 + i, 0)
+        for i, source in enumerate((far, other(far, 1))):
+            arrived(all_maps.at[source], 2 * count + 2 + i, 0)
         for key, slot in slots.items():
             view = views(targets, other(far, 1), key)
             for i in range(2):
@@ -228,11 +240,11 @@
         6: [got("z", c[1]), got("x", c[1])],
         8: [got("y", c[3]), got("d", c[0])],
         10: [got("x", c[2]), got("z", c[2])],
-        "finished": [got("z", c[3]), got("e", e[0])],
+        "finished": [send_maps, got("z", c[3]), got("e", e[0])],
         200: [got("x", c[3])],
-        201: [got("e", e[1])],
-        202: [got("d", c[1])],
-        203: [got("d", c[2])],
+        "change": [change],
+        "changed": [got("e", e[1]), got("d", c[1]), changed],
+        212: [got("d", c[2])],
         "end": [got("o", e[0]), got("d", c[3]), got("o", e[1]), end],
     }
 
@@ -248,17 +260,19 @@
     steps = {}
     if exchange:
         cot, routes, carried = own[-3:]
-        own_outs, semaphores = refs[:3], refs[6:12]
+        own_outs, routing, refs = refs[:3], refs[5:7], refs[:5] + refs[7:]
+        semaphores = refs[6:12]
         own_both, own_grads, bias = refs[3:6]
         bounce_gu, bounce_dn, compact = refs[6:9]
-        info_t, place_t, x_s, c_s, dy_s, y_acc, ud_acc, dx_acc, dug_acc = refs[12:21]
-        held, refs = refs[21:], ()
+        x_s, c_s, dy_s, y_acc, ud_acc, dx_acc, dug_acc = refs[12:19]
+        held, refs = refs[19:], ()
         loads = (tok, down, up, up_out, *own[3:7], wqkv, cos, sin, wo, cot)
         load = Staged(list(zip(loads, held)), held[-2])
         tok, down, up, up_out, *maps, wqkv, cos, sin, wo, cot = held[: len(loads)]
         outs = (xa_ref, q_ref, k_ref, v_ref, ob_ref, ua_ref, uo_ref, lse_ref, h1_ref, xb_ref, lin_ref, wqk_ref, down_ref, up_s, wr)
         kept_outs = held[len(loads) : len(loads) + len(outs)]
-        store = Staged(list(zip(kept_outs, outs)), held[-1])
+        info_t, place_t = held[len(loads) + len(outs) : len(loads) + len(outs) + 2]
+        store = Staged(list(zip((*kept_outs, info_t, place_t), (*outs, *routing))), held[-1])
         xa_ref, q_ref, k_ref, v_ref, ob_ref, ua_ref, uo_ref, lse_ref, h1_ref, xb_ref, lin_ref, wqk_ref, down_ref, up_s, wr = kept_outs
         steps = sending_steps((*own[:3], *maps), own_outs, semaphores)
     else:
@@ -376,47 +390,55 @@
 
     lax.fori_loop(0, length // 256, finish, 0)
     if exchange:
-        store.start()
+        store.start(range(15))
         run("finished")
         ex = lax.axis_index("expert")
         hidden = bounce_dn.shape[0]
-        own_grads[:, 3 * width + 3 * hidden :] = jnp.zeros((RANK, own_grads.shape[1] - 3 * width - 3 * hidden), BF)
+        rest = own_grads.shape[2] - 3 * width - 3 * hidden
+        own_grads[:, :, 3 * width + 3 * hidden :] = jnp.zeros((2, RANK, rest), BF)
         route(lin_ref, carried, routes, carried.shape[0] - 4, info_t, place_t)
-        x, c, g, dy = take_rows(x_s.shape[0], place_t[pl.ds(ex, 1), :], info_t[pl.ds(ex, 1), :], xb_ref, cot)
-        x_s[...], c_s[...], dy_s[...] = x, c, dy
-        a_gu = padded_rows(compact[ex, :, :width]) + padded_rows(compact[ex, :, width : 2 * width], RANK)
-        b_dn = padded_rows(compact[ex, :, 2 * width + 3 * hidden :])
-        ug, dud = mm_t(x, a_gu).astype(BF), mm_t(dy, b_dn).astype(BF)
-        kept = (y_acc, ud_acc, dx_acc, dug_acc)
-        for ref in kept:
-            ref[...] = jnp.zeros(ref.shape, F32)
+        store.start([15, 16])
         run(200)
         tile = 512
-
-        def one_tile(j, carry):
-            at = pl.multiple_of(j * tile, tile)
-            starts = [2 * width + i * hidden + at for i in range(3)]
-            sums, parts = hidden_tile(
-                x_s[...], dy_s[...], ug, dud,
-                bounce_gu[:, pl.ds(at, tile)], bounce_gu[:, pl.ds(hidden + at, tile)], bounce_dn[pl.ds(at, tile), :],
-                padded_rows(compact[ex, :, pl.ds(starts[0], tile)]),
-                padded_rows(compact[ex, :, pl.ds(starts[1], tile)], RANK),
-                padded_rows(compact[ex, :, pl.ds(starts[2], tile)]),
-            )
-            for start, part in zip(starts, parts):
-                own_grads[:, pl.ds(start, tile)] = part
-            for ref, value in zip(kept, sums):
-                ref[...] += value
-            for point in steps:
-                if isinstance(point, int) and point > 200:
-                    pl.when(j == point - 201)(functools.partial(run, point))
-            return carry
-
-        lax.fori_loop(0, hidden // tile, one_tile, 0)
-        out, parts = close_rows(ex, [ref[...] for ref in kept], x_s[...], c_s[...], g, dy_s[...], a_gu, b_dn)
-        own_both[:, :width], own_both[:, width : 2 * width], own_both[:, 2 * width :] = out
-        own_grads[:, :width], own_grads[:, width : 2 * width] = parts[:2]
-        own_grads[:, 2 * width + 3 * hidden : 3 * width + 3 * hidden] = parts[2]
+        kept = (y_acc, ud_acc, dx_acc, dug_acc)
+        for which, expert in enumerate((ex, other(ex, 1))):
+            rows = pl.ds(which * HALF, HALF)
+            x, c, g, dy = take_rows(HALF, place_t[pl.ds(expert, 1), :], info_t[pl.ds(expert, 1), :], xb_ref, cot)
+            x_s[...], c_s[...], dy_s[...] = x, c, dy
+            if which:
+                run("changed")
+            a_gu = padded_rows(compact[ex, :, :width]) + padded_rows(compact[ex, :, width : 2 * width], RANK)
+            b_dn = padded_rows(compact[ex, :, 2 * width + 3 * hidden :])
+            ug, dud = mm_t(x, a_gu).astype(BF), mm_t(dy, b_dn).astype(BF)
+            for ref in kept:
+                ref[...] = jnp.zeros(ref.shape, F32)
+
+            def one_tile(j, carry, which=which, ug=ug, dud=dud):
+                at = pl.multiple_of(j * tile, tile)
+                starts = [2 * width + i * hidden + at for i in range(3)]
+                sums, parts = hidden_tile(
+                    x_s[...], dy_s[...], ug, dud,
+                    bounce_gu[:, pl.ds(at, tile)], bounce_gu[:, pl.ds(hidden + at, tile)], bounce_dn[pl.ds(at, tile), :],
+                    padded_rows(compact[ex, :, pl.ds(starts[0], tile)]),
+                    padded_rows(compact[ex, :, pl.ds(starts[1], tile)], RANK),
+                    padded_rows(compact[ex, :, pl.ds(starts[2], tile)]),
+                )
+                for start, part in zip(starts, parts):
+                    own_grads[which, :, pl.ds(start, tile)] = part
+                for ref, value in zip(kept, sums):
+                    ref[...] += value
+                for point in steps:
+                    if isinstance(point, int) and point > 200 + 10 * which and point < 210 + 10 * which:
+                        pl.when(j == point - 201 - 10 * which)(functools.partial(run, point))
+                return carry
+
+            lax.fori_loop(0, hidden // tile, one_tile, 0)
+            out, parts = close_rows(expert, [ref[...] for ref in kept], x_s[...], c_s[...], g, dy_s[...], a_gu, b_dn)
+            if not which:
+                run("change")
+            own_both[rows, :width], own_both[rows, width : 2 * width], own_both[rows, 2 * width :] = out
+            own_grads[which, :, :width], own_grads[which, :, width : 2 * width] = parts[:2]
+            own_grads[which, :, 2 * width + 3 * hidden : 3 * width + 3 * hidden] = parts[2]
         store.wait()
     run("end")
 
@@ -445,7 +467,7 @@
     anys = pl.BlockSpec(memory_space=pl.ANY)
     in_specs, out_specs = [smem, smem] + [vmem] * 12, [vmem] * len(shapes)
     scratch = [pltpu.VMEM((length // HALF, HALF, HALF), F32)]
-    params = dict(vmem_limit_bytes=60 * MIB)
+    params = dict(vmem_limit_bytes=62 * MIB)
     args = (spans, adapters, tok, gain_a, wqkv, down, up, wo, up_out, gain_m, router, mixing, cos, sin)
     if own:
         w_gu, w_dn = own[:2]
@@ -460,10 +482,13 @@
             ((4, *w_gu.shape[1:]), BF),
             ((4, *w_dn.shape[1:]), BF),
             ((4, RANK, columns), BF),
-            ((HALF, 2 * width + 128), BF),
-            ((RANK, padded), BF),
+            ((2 * HALF, 2 * width + 128), BF),
+            ((2, RANK, padded), BF),
+            ((128, length), F32),
+            ((128, length), F32),
         ]
-        out_specs = [anys] * (len(out_specs) + 3) + [vmem] * 2
+        held += [pltpu.VMEM(a, t) for a, t in shapes[-2:]]
+        out_specs = [anys] * (len(out_specs) + 3) + [vmem] * 2 + [anys] * 2
         scratch += [
             pltpu.VMEM(w_gu.shape[1:], BF),
             pltpu.VMEM(w_dn.shape[1:], BF),
@@ -471,8 +496,6 @@
             pltpu.SemaphoreType.DMA((96,)),
             pltpu.SemaphoreType.DMA((48, 2)),
             pltpu.SemaphoreType.DMA((3,)),
-            pltpu.VMEM((128, length), F32),
-            pltpu.VMEM((128, length), F32),
             pltpu.VMEM((HALF, width), BF),
             pltpu.VMEM((HALF, width), BF),
             pltpu.VMEM((HALF, width), BF),
@@ -481,7 +504,7 @@
             pltpu.VMEM((HALF, width), F32),
             pltpu.VMEM((HALF, 128), F32),
         ]
-        scratch += held + [pltpu.SemaphoreType.DMA((16,)), pltpu.SemaphoreType.DMA((16,))]
+        scratch += held + [pltpu.SemaphoreType.DMA((16,)), pltpu.SemaphoreType.DMA((20,))]
         params.update(collective_id=0, has_side_effects=True)
     return pl.pallas_call(
         functools.partial(attention_forward_kernel, bool(own)),
@@ -580,8 +603,10 @@
     def begin():
         meet([(dp, group[k]) for k in group] + [(along[k], ex) for k in along] + [plane[1, k] for k in range(1, 4)])
         for i, to in enumerate(others):
-            mail.post(lambda to=to: maps_in.at[to], lambda: e_got.at[ex], (dp, to), first["e1"] + i)
-        pltpu.make_async_copy(own_maps, e_got.at[ex], local.at[0]).start()
+            mail.post(
+                lambda i=i, to=to: maps_in.at[to] if i else own_maps.at[1], lambda: e_got.at[ex], (dp, to), first["e1"] + i
+            )
+        pltpu.make_async_copy(own_maps.at[0], e_got.at[ex], local.at[0]).start()
 
     def columns(refs, pair, to):
         return refs.at[pl.ds(pair, 2), :, pl.ds(pl.multiple_of(to * share, 128), share)]
@@ -595,7 +620,7 @@
 
     def spread_near():
         mail.arrived(e_got.at[others[0]], first["e1"], s_peer)
-        pltpu.make_async_copy(own_maps, e_got.at[ex], local.at[0]).wait()
+        pltpu.make_async_copy(own_maps.at[0], e_got.at[ex], local.at[0]).wait()
         spread_out(near, "e2")
 
     def spread_far():
@@ -718,31 +743,36 @@
     }
 
 
-def attention_backward_kernel(exchange, *refs):
-    spans, dh1_ref, tok, gain_a, wqkv, wqk, wo, down_ref, up_s, cos, sin = refs[:11]
+def attention_backward_kernel(exchange, numbers, *refs):
+    spans, h1_ref, tok, gain_a, wqkv, wqk, wo, down_ref, up_s, cos, sin = refs[:11]
     xa_ref, q_ref, k_ref, v_ref, ob_ref, ua_ref, uo_ref, lse_ref = refs[11:19]
+    mixed, cot, lin_ref, info, vectors, gain_m, wr = refs[19:26]
     steps = {}
     if exchange:
-        grad_tok, grad_maps, own = refs[22], refs[25], refs[37:]
-        sums = (*refs[19:22], *refs[23:25])
-        bias, dob, datt, duo, lse_t, center_t, dq, dk, dv, dlin, dua = refs[26:37]
+        grad_out, result_out, grad_maps, own = refs[29], refs[30], refs[33], refs[46:]
+        dh1_ref, bias, dob, datt, duo, lse_t, center_t, dq, dk, dv, dlin, dua = refs[34:46]
         own, held = own[:10], own[10:]
         width = wo.shape[0]
         loads = (
-            dh1_ref, up_s, wo, down_ref, ob_ref, lse_ref, q_ref, k_ref, v_ref, cos, sin, ua_ref, xa_ref, uo_ref,
+            up_s, wo, down_ref, ob_ref, lse_ref, lin_ref, info, wr, q_ref, k_ref, v_ref, cos, sin, ua_ref, xa_ref, uo_ref,
             wqk, wqkv.at[:, pl.ds(2 * width, width)], tok,
         )
-        load = Staged([*zip(loads, held), (held[17], grad_tok)], held[18])
+        grad_tok, result = held[19:21]
+        pairs = [
+            (h1_ref, dq), (mixed, dlin.at[:, pl.ds(0, mixed.shape[1])]), (cot, grad_tok), *zip(loads, held),
+            (grad_tok, grad_out), (result, result_out),
+        ]
+        load = Staged(pairs, held[21])
+        h1_ref, mixed, cot = dq, dlin, grad_tok
         (
-            dh1_ref, up_s, wo, down_ref, ob_ref, lse_ref, q_ref, k_ref, v_ref, cos, sin, ua_ref, xa_ref, uo_ref,
+            up_s, wo, down_ref, ob_ref, lse_ref, lin_ref, info, wr, q_ref, k_ref, v_ref, cos, sin, ua_ref, xa_ref, uo_ref,
             wqk, wv, tok,
-        ) = held[:17]
-        grad_tok = held[17]
-        steps = summing_steps((*sums, *own), grad_maps)
+        ) = held[:19]
+        steps = summing_steps((*refs[26:29], *refs[31:33], *own), grad_maps)
     else:
-        grad_tok, grad_maps = refs[19:21]
+        grad_tok, result, grad_maps = refs[26:29]
         wv = wqkv.at[:, pl.ds(2 * wo.shape[0], wo.shape[0])]
-        bias, dob, datt, duo, lse_t, center_t, dq, dk, dv, dlin, dua = refs[21:]
+        dh1_ref, bias, dob, datt, duo, lse_t, center_t, dq, dk, dv, dlin, dua = refs[29:]
     length, width = tok.shape
     groups = width // GROUP
 
@@ -752,16 +782,56 @@
 
     run("begin")
     if exchange:
-        load.start(range(17))
+        load.start(range(22))
     for half in range(length // HALF):
         bias[half] = span_bias(spans[half] - half * HALF, True)
     if exchange:
-        load.wait(range(6))
+        load.wait(range(11))
     of_head = one_hot(iota((128, width), 1) // HD == iota((128, width), 0))
 
     def outer(block, carry):
         at = pl.ds(pl.multiple_of(block * 256, 256), 256)
-        d = dh1_ref[at, :].astype(BF)
+        h1 = h1_ref[at, :]
+        g = info[at, :]
+        lane = iota((1, 128), 1)
+        kinds = numbers + 4
+        ct = cot[at, :].astype(F32)
+        r = lax.rsqrt(jnp.mean(h1 * h1, axis=1, keepdims=True) + EPS)
+        gain = gain_m[...][None]
+        n2 = h1 * r * gain
+        lin = lin_ref[at, :]
+        gc = g[:, numbers + 1 : numbers + 2]
+        g_fix = [g[:, numbers + 2 + i : numbers + 3 + i] for i in range(2)]
+        mixes = []
+        for i in range(2):
+            a, b = lin[:, kinds + 2 * i : kinds + 2 * i + 1], lin[:, kinds + 2 * i + 1 : kinds + 2 * i + 2]
+            top = jnp.maximum(a, b)
+            a, b = jnp.exp(a - top), jnp.exp(b - top)
+            mixes.append((a / (a + b), b / (a + b)))
+        vecs = [vectors[i : i + 1, :] for i in range(2)]
+        to_n2 = gc + g_fix[0] * mixes[0][0] + g_fix[1] * mixes[1][0]
+        out = h1 + mixed[at, :width].astype(F32) + to_n2 * n2
+        out = out + (g_fix[0] * mixes[0][1]) * vecs[0] + (g_fix[1] * mixes[1][1]) * vecs[1]
+        result[at, :] = out.astype(BF)
+        a = jnp.sum(ct * n2, axis=1, keepdims=True)
+        bs = [jnp.sum(ct * v, axis=1, keepdims=True) for v in vecs]
+        packed = mixed[at, 2 * width : 2 * width + 128].astype(F32)
+        dg = jnp.where(lane < numbers, packed + pltpu.roll(packed, 64, 1), 0.0)
+        dg = jnp.where(lane == numbers + 1, a, dg)
+        for i in range(2):
+            dg = jnp.where(lane == numbers + 2 + i, mixes[i][0] * a + mixes[i][1] * bs[i], dg)
+        g = jnp.where(lane < kinds, g, 0.0)
+        dlin = g * (dg - jnp.sum(g * dg, axis=1, keepdims=True))
+        for i in range(2):
+            pull = mixes[i][0] * mixes[i][1] * (g_fix[i] * (a - bs[i]))
+            dlin = jnp.where(lane == kinds + 2 * i, pull, jnp.where(lane == kinds + 2 * i + 1, -pull, dlin))
+        high, low = split(dlin)
+        dn2 = mixed[at, width : 2 * width].astype(F32) + (mm(high, wr[...]) + mm(low, wr[...])) + ct * to_n2
+        dn2 = dn2 * gain
+        back = r * dn2 - h1 * (r * r * r * jnp.mean(dn2 * h1, axis=1, keepdims=True))
+        dh1 = ct + back
+        dh1_ref[at, :] = dh1
+        d = dh1.astype(BF)
         datt[at, :] = d
         u = mm_t(d, up_s[:, pl.ds(3 * width, width)]).astype(BF)
         duo[at, :] = u
@@ -778,7 +848,8 @@
 
     lax.fori_loop(0, length // 256, outer, 0)
     if exchange:
-        load.wait(range(6, 9))
+        load.start([23])
+        load.wait(range(11, 14))
     dq[...] = jnp.zeros(dq.shape, F32)
     dk[...] = jnp.zeros(dk.shape, F32)
     dv[...] = jnp.zeros(dv.shape, F32)
@@ -816,7 +887,7 @@
 
     lax.fori_loop(0, HEADS, attend, 0)
     if exchange:
-        load.wait(range(9, 17))
+        load.wait(range(14, 22))
 
     def turn_back(block, carry):
         at = pl.ds(pl.multiple_of(block * 256, 256), 256)
@@ -861,37 +932,42 @@
 
     lax.fori_loop(0, length // 256, inner, 0)
     if exchange:
-        load.start([17])
+        load.start([22])
     run("end")
     if exchange:
-        load.wait([17])
+        load.wait([22, 23])
 
 
 def attention_backward(
-    spans, dh1, tok, gain_a, wqkv, wqk, wo, down_s, up_s, xa, q, k, v, ob, ua, uo, lse, maps=None, own_maps=None, takers=None
+    numbers, spans, h1, tok, gain_a, wqkv, wqk, wo, down_s, up_s, xa, q, k, v, ob, ua, uo, lse,
+    mixed, cot, lin, info, vectors, gain_m, wr, maps=None, own_maps=None, takers=None,
 ):
     length, width = tok.shape
     cos, sin = rope_tables(length)
     vmem, smem = pl.BlockSpec(memory_space=pltpu.VMEM), pl.BlockSpec(memory_space=pltpu.SMEM)
     anys = pl.BlockSpec(memory_space=pl.ANY)
-    args = (spans, dh1, tok, gain_a, wqkv, wqk, wo, down_s, up_s, cos, sin, xa, q, k, v, ob, ua, uo, lse)
-    in_specs = [smem] + [vmem] * 18
+    args = (
+        spans, h1, tok, gain_a, wqkv, wqk, wo, down_s, up_s, cos, sin, xa, q, k, v, ob, ua, uo, lse,
+        mixed, cot, lin, info, vectors, gain_m, wr,
+    )
+    in_specs = [smem] + [vmem] * 25
     compact = ((8, RANK, width), BF)
-    shapes, out_specs, scratch = [((length, width), BF)], [vmem], []
+    shapes, out_specs, scratch = [((length, width), BF)] * 2, [vmem] * 2, []
     if maps is None:
         shapes.append(compact)
         out_specs.append(vmem)
     else:
         share = maps.shape[2] // 8
-        in_specs = [smem] + [vmem if a.ndim == 1 else anys for a in args[1:]] + [anys, anys, vmem]
-        held = [dh1, up_s, wo, down_s, ob, lse, q, k, v, cos, sin, ua, xa, uo, wqk, wo, tok, tok]
+        in_specs = [smem] + [vmem if a.size < 2048 else anys for a in args[1:]] + [anys, anys, vmem]
+        held = [up_s, wo, down_s, ob, lse, lin, info, wr, q, k, v, cos, sin, ua, xa, uo, wqk, wo, tok, tok, tok]
         held = [pltpu.VMEM(a.shape, a.dtype) for a in held]
         args += (maps, own_maps, takers)
-        out_specs = [anys]
+        out_specs = [anys] * 2
         shapes += [((8, 128, share), BF), ((8, 128, width), BF)]
         out_specs += [anys] * 2
         scratch.append(compact)
     scratch += [
+        ((length, width), F32),
         ((length // HALF, HALF, HALF), F32),
         ((length, width), BF),
         ((length, width), BF),
@@ -917,10 +993,10 @@
             ((32, width), BF),
         ]
         semaphores = [pltpu.SemaphoreType.DMA((64,)), pltpu.SemaphoreType.DMA((64,)), pltpu.SemaphoreType.DMA((3,))]
-        semaphores += [*held, pltpu.SemaphoreType.DMA((18,))]
+        semaphores += [*held, pltpu.SemaphoreType.DMA((24,))]
         params.update(collective_id=1, has_side_effects=True)
     return pl.pallas_call(
-        functools.partial(attention_backward_kernel, maps is not None),
+        functools.partial(attention_backward_kernel, maps is not None, numbers),
         out_shape=[jax.ShapeDtypeStruct(s, t) for s, t in shapes],
         in_specs=in_specs,
         out_specs=out_specs,
@@ -996,7 +1072,6 @@
         before = one_hot(iota((256, length), 1) < iota((256, length), 0) + block * 256)
         place_t[:, pl.ds(block * 256, 256)] = mm_t(member, before)
     place_t[...] = jnp.where(named[0] | named[1], place_t[...], -1.0)
-    return named, member
 
 
 def padded_rows(part, before=0):
@@ -1049,38 +1124,43 @@
 
 
 def experts_kernel(
-    own_first, order, xb, h1_ref, lin_ref, cot, routes, carried, gain_m, wr, vectors, own_both,
+    own_first, order, xb, cot, routes, given, given_too, own_both,
     w_gate, w_up, w_down, maps,
-    result, dh1_ref, grads,
-    count, info, info_t, place_t, both, x_s, c_s, dy_s, g_s, y_acc, dx_acc, ug_s, ud_acc, dud_s, dug_acc, a_gu, b_dn, acc,
+    mixed, info, grads,
+    count, info_t, place_t, both, x_s, c_s, dy_s, g_s, y_acc, dx_acc, ug_s, ud_acc, dud_s, dug_acc, a_gu, b_dn, acc,
 ):
     step, j = pl.program_id(0), pl.program_id(1)
     steps, tiles = pl.num_programs(0), pl.num_programs(1)
     e = order[step]
     length, width = xb.shape
-    kinds = carried.shape[0]
-    numbers = kinds - 4
+    numbers = count.shape[1] - 1
     tile = w_gate.shape[2]
     hidden = (maps.shape[2] - 3 * width) // 3
     rows_of = 128
-    skip = HALF if own_first else 0
+    skip = 2 * HALF if own_first else 0
 
     if grads.shape[2] > maps.shape[2]:
         grads[0, :, maps.shape[2] :] = jnp.zeros((RANK, grads.shape[2] - maps.shape[2]), BF)
 
     @pl.when((step == 0) & (j == 0))
     def _():
-        named, member = route(lin_ref, carried, routes, numbers, info_t, place_t)
+        if own_first:
+            info_t[...], place_t[...] = given[...], given_too[...]
+        else:
+            route(given, given_too, routes, numbers, info_t, place_t)
+        wide = iota((128, length), 0)
+        named = [(wide == routes[k : k + 1, :]) & (wide < numbers) for k in range(2)]
         number = iota((128, 1), 0)
-        counts = jnp.sum(member.astype(F32), axis=1, keepdims=True)
+        counts = jnp.max(place_t[...], axis=1, keepdims=True) + 1.0
         padded = jnp.floor((counts + (rows_of - 1)) * (1.0 / rows_of))
         if own_first:
-            padded = jnp.where(number == lax.axis_index("expert"), 0.0, padded)
+            ex = lax.axis_index("expert")
+            padded = jnp.where((number == ex) | (number == other(ex, 1)), 0.0, padded)
         earlier = one_hot(iota((128, 128), 1) < iota((128, 128), 0))
         starts = rows_of * mm(earlier, jnp.broadcast_to(padded, (128, 128)).astype(BF))[:, :1]
         slots = starts + skip
         if own_first:
-            slots = jnp.where(number == lax.axis_index("expert"), 0.0, slots)
+            slots = jnp.where(number == ex, 0.0, jnp.where(number == other(ex, 1), 1.0 * HALF, slots))
         at_slot = place_t[...] + slots
         for k in range(2):
             spot = jnp.sum(jnp.where(named[k], at_slot + 1.0, 0.0), axis=0, keepdims=True) - 1.0
@@ -1156,8 +1236,6 @@
     def _():
         used = count[1, numbers]
         both[pl.ds(pl.multiple_of(used, rows_of), HALF), :] = jnp.zeros((HALF, both.shape[1]), BF)
-        lane = iota((1, 128), 1)
-
         def combine(block, carry):
             at = pl.ds(pl.multiple_of(block * 256, 256), 256)
             g = info[at, :]
@@ -1168,7 +1246,7 @@
                 return one_hot((slot == spots[:, :1]) | (slot == spots[:, 1:2]))
 
             if own_first:
-                acc[...] = mm(taken(0), own_both[...])
+                acc[...] = mm(taken(0), own_both[:HALF, :]) + mm(taken(HALF), own_both[HALF:, :])
             else:
                 acc[...] = jnp.zeros(acc.shape, F32)
 
@@ -1178,48 +1256,13 @@
                 return carry
 
             lax.fori_loop(0, (used + HALF - 1) // HALF, add, 0)
-            h1 = h1_ref[at, :]
-            ct = cot[at, :].astype(F32)
-            r = lax.rsqrt(jnp.mean(h1 * h1, axis=1, keepdims=True) + EPS)
-            gain = gain_m[...][None]
-            n2 = h1 * r * gain
-            lin = lin_ref[at, :]
-            gc = g[:, numbers + 1 : numbers + 2]
-            g_fix = [g[:, numbers + 2 + i : numbers + 3 + i] for i in range(2)]
-            mixes = []
-            for i in range(2):
-                a, b = lin[:, kinds + 2 * i : kinds + 2 * i + 1], lin[:, kinds + 2 * i + 1 : kinds + 2 * i + 2]
-                top = jnp.maximum(a, b)
-                a, b = jnp.exp(a - top), jnp.exp(b - top)
-                mixes.append((a / (a + b), b / (a + b)))
-            vecs = [vectors[i : i + 1, :] for i in range(2)]
-            to_n2 = gc + g_fix[0] * mixes[0][0] + g_fix[1] * mixes[1][0]
-            out = h1 + acc[:, :width] + to_n2 * n2
-            out = out + (g_fix[0] * mixes[0][1]) * vecs[0] + (g_fix[1] * mixes[1][1]) * vecs[1]
-            result[at, :] = out.astype(BF)
-            a = jnp.sum(ct * n2, axis=1, keepdims=True)
-            bs = [jnp.sum(ct * v, axis=1, keepdims=True) for v in vecs]
-            packed = acc[:, 2 * width :]
-            dg = jnp.where(lane < numbers, packed + pltpu.roll(packed, 64, 1), 0.0)
-            dg = jnp.where(lane == numbers + 1, a, dg)
-            for i in range(2):
-                dg = jnp.where(lane == numbers + 2 + i, mixes[i][0] * a + mixes[i][1] * bs[i], dg)
-            g = jnp.where(lane < kinds, g, 0.0)
-            dlin = g * (dg - jnp.sum(g * dg, axis=1, keepdims=True))
-            for i in range(2):
-                pull = mixes[i][0] * mixes[i][1] * (g_fix[i] * (a - bs[i]))
-                dlin = jnp.where(lane == kinds + 2 * i, pull, jnp.where(lane == kinds + 2 * i + 1, -pull, dlin))
-            high, low = split(dlin)
-            dn2 = acc[:, width : 2 * width] + (mm(high, wr[...]) + mm(low, wr[...])) + ct * to_n2
-            dn2 = dn2 * gain
-            back = r * dn2 - h1 * (r * r * r * jnp.mean(dn2 * h1, axis=1, keepdims=True))
-            dh1_ref[at, :] = ct + back
+            mixed[at, :] = acc[...].astype(BF)
             return carry
 
         lax.fori_loop(0, length // 256, combine, 0)
 
 
-def experts_both_ways(xb, h1, lin, cot, routes, carried, gain_m, wr, vectors, w_gu, w_dn, maps, copies, own_both=None):
+def experts_both_ways(xb, cot, routes, given, given_too, w_gu, w_dn, maps, copies, own_both=None):
     length, width = xb.shape
     experts, hidden = w_dn.shape[0], w_dn.shape[1]
     tile = hidden // 2
@@ -1233,16 +1276,16 @@
 
     own_first = own_both is not None
     if own_first:
-        order = (lax.axis_index("expert") + jnp.arange(1, experts, dtype=jnp.int32)) % experts
+        order = other(2 * (lax.axis_index("expert") // 2), 2) + jnp.arange(2, dtype=jnp.int32)
     else:
         order = jnp.arange(experts, dtype=jnp.int32)
         own_both = jnp.zeros((16, 128), BF)
-    resident = (xb, h1, lin, cot, routes, carried, gain_m, wr, vectors, own_both)
+    resident = (xb, cot, routes, given, given_too, own_both)
     return pl.pallas_call(
         functools.partial(experts_kernel, own_first),
         out_shape=[
-            jax.ShapeDtypeStruct((length, width), BF),
-            jax.ShapeDtypeStruct((length, width), F32),
+            jax.ShapeDtypeStruct((length, 2 * width + 128), BF),
+            jax.ShapeDtypeStruct((length, 128), F32),
             jax.ShapeDtypeStruct((experts, RANK, padded), BF),
         ],
         grid_spec=pltpu.PrefetchScalarGridSpec(
@@ -1256,13 +1299,12 @@
                 pl.BlockSpec((1, RANK, total), lambda e, j, order: (order[e], 0, 0)),
             ],
             out_specs=[
-                pl.BlockSpec((length, width), lambda e, j, order: (0, 0), pipeline_mode=pl.Buffered(1)),
-                pl.BlockSpec((length, width), lambda e, j, order: (0, 0), pipeline_mode=pl.Buffered(1)),
+                pl.BlockSpec((length, 2 * width + 128), lambda e, j, order: (0, 0), pipeline_mode=pl.Buffered(1)),
+                pl.BlockSpec((length, 128), lambda e, j, order: (0, 0), pipeline_mode=pl.Buffered(1)),
                 pl.BlockSpec((1, RANK, padded), lambda e, j, order: (order[e], 0, 0)),
             ],
             scratch_shapes=[
             pltpu.SMEM((2, experts + 1), jnp.int32),
-            pltpu.VMEM((length, 128), F32),
             pltpu.VMEM((128, length), F32),
             pltpu.VMEM((128, length), F32),
             pltpu.VMEM((most + HALF, 2 * width + 128), BF),
@@ -1352,19 +1394,20 @@
     )
     xa, q, k, v, ob, ua, uo, lse, h1, xb, lin, wqk, down_s, up_s, wr = outs[:15]
     weights = outs[15:18] if exchange else gather_experts(own, senders)
-    result, dh1, expert_maps = experts_both_ways(
-        xb, h1, lin, cotangent, routes.T, router_logits_carried.T, experts_norm_gain, wr, constant_expert_vectors, *weights,
-        lax.axis_size("dp"), outs[18] if exchange else None,
+    given = outs[20:22] if exchange else (lin, router_logits_carried.T)
+    mixed, info, expert_maps = experts_both_ways(
+        xb, cotangent, routes.T, *given, *weights, lax.axis_size("dp"), outs[18] if exchange else None
     )
     backward = functools.partial(
-        attention_backward, spans, dh1, tokens, attention_norm_gain, query_key_value_weight, wqk, attention_output_weight, down_s, up_s,
-        xa, q, k, v, ob, ua, uo, lse,
+        attention_backward, weights[1].shape[0], spans, h1, tokens, attention_norm_gain, query_key_value_weight, wqk,
+        attention_output_weight, down_s, up_s, xa, q, k, v, ob, ua, uo, lse,
+        mixed, cotangent, lin, info, constant_expert_vectors, experts_norm_gain, wr,
     )
     if exchange:
         takers = jnp.repeat(sequence_adapter_index, RANK)[None]
-        grad_tokens, all_e, all_a = backward(expert_maps, outs[19], takers)
+        grad_tokens, result, all_e, all_a = backward(expert_maps, outs[19], takers)
         return (result, grad_tokens, *unpack(all_e, all_a, hidden))
-    grad_tokens, attention_maps = backward()
+    grad_tokens, result, attention_maps = backward()
     to = (sequence_adapter_index[:, None] * RANK + jnp.arange(RANK)[None, :]).reshape(-1)
     spread = (jnp.arange(128)[:, None] == to[None, :]).astype(BF)
     of_expert = sum_expert_maps(expert_maps, spread).astype(F32)

time: 299 us -> 281 us (0.940)
  Pallas kernels: 290 us -> 268 us
    pallas_call x1, Pallas kernels: 84.5 us -> 47.5 us  [experts_both_ways(): pl.pallas_call(functools.partial(experts_kernel, own_first), out_shape=[j...]
    pallas_call x1, Pallas kernels: 105 us -> 120 us  [attention_forward(): pl.pallas_call(functools.partial(attention_forward_kernel, bool(own)), ou...]
    unnamed x9 -> x12, local copies, waits for them, and re-layouts: 4.22 us -> 6.19 us
where the time goes in v5:
time: 281 us; the launch traced here: 277 us
  Pallas kernels  268 us (95%)
  local copies, waits for them, and re-layouts  6.93 us (2%)
    pallas_call x1, Pallas kernels, attention_forward(): pl.pallas_call(functools.partial(attention_forward_kernel, bool(own)), ou...  120 us
    pallas_call x1, Pallas kernels, attention_backward(): pl.pallas_call(functools.partial(attention_backward_kernel, maps is not N...  97.3 us
    pallas_call x1, Pallas kernels, experts_both_ways(): pl.pallas_call(functools.partial(experts_kernel, own_first), out_shape=[j...  47.5 us
    unnamed x12, local copies, waits for them, and re-layouts  6.19 us

profile of v5, /device:TPU:0, one launch (start us, length us, event | category | flops | bytes accessed | tf_op | source)
XLA Modules:
  0.0 276.8 jit_solution(9902913830767597821)
XLA Ops:
  0.7 0.5 iota_add_fusion.order
  1.2 120.2 %attention_forward.1 = (bf16[1024,768]{1,0:T(8,128)(2,1)}, bf16[1024,768]{1,0:T(8,128)(2,1)}, bf16[1024,768]{1,0:T(8,128)(2,1)}, bf16[1024,768]{1,0:T(8,128)(2,1...) custom-call(s32[2]{0:T(128)} %bitcast.10, ...), custom_call_target="tpu_custom_call" | custom-call | tf_op jit(solution)/shard_map/attention_forward/pallas_call | solution.py:509
  121.4 0.0 copy-start.4
  121.4 47.5 %experts_both_ways.1 = (bf16[1024,1664]{1,0:T(8,128)(2,1)}, f32[1024,128]{1,0:T(8,128)}, bf16[4,16,9216]{2,1,0:T(8,128)(2,1)}) custom-call(s32[2]{0:T(128)} %iota_add_fusion.order, bf16[1024,768]{1,0:T(8,128)(2,1)} %get-tuple-element.57.xb, bf16[1024,768]{1,0:T(8,128)(2,1)} %refs_20_.3, s32[2,1024]{1,0:T(2,128)} %bitcast.7, ...), custom_call_target="tpu_custom_call" | custom-call | tf_op jit(solution)/shard_map/experts_both_ways/pallas_call | solution.py:1284
  168.9 0.0 copy-done.4
  168.9 0.1 broadcast_in_dim.3
  169.0 0.7 broadcast_in_dim_reshape.3.refs_28_
  169.7 97.3 %attention_backward.1 = (bf16[1024,768]{1,0:T(8,128)(2,1)}, bf16[1024,768]{1,0:T(8,128)(2,1)}, bf16[8,128,1152]{2,1,0:T(8,128)(2,1)}, bf16[8,128,768]{2,1,0:T(8,128)(2,1)}) custom-call(s32[2]{0:T(128)} %bitcast.11, f32[1024,768]{1,0:T(8,128)} %get-tuple-element.45.refs_1_, bf16[1024,768]{1,0:T(8,128)(2,1)} %refs_2_.3, f32[768]{0:T(1024)} %refs_3_.3, ...), custom_call_target="tpu_custom_call" | custom-call | tf_op jit(solution)/shard_map/attention_backward/pallas_call | solution.py:998
  267.0 0.0 copy-start
  267.0 1.7 copy-done
  268.6 0.0 copy-start.1
  268.6 1.4 copy-done.1
  270.0 0.0 copy-start.3
  270.0 3.3 %unpack.1 = (f32[4,768,128]{2,1,0:T(8,128)}, f32[3,128,768]{2,1,0:T(8,128)}, f32[128,768]{1,0:T(8,128)}, f32[1,2,768,128]{3,2,1,0:T(8,128)}, f32[1,2,128,2048]{3...) custom-call(bf16[8,128,1152]{2,1,0:T(8,128)(2,1)S(1)} %copy-done, bf16[8,128,768]{2,1,0:T(8,128)(2,1)S(1)} %copy-done.1), custom_call_target="tpu_custom_call" | custom-call | tf_op jit(solution)/shard_map/unpack/pallas_call | solution.py:1042
  273.3 0.0 copy-done.3
  273.3 0.0 copy-start.2
  273.3 1.1 copy.37
  274.5 0.8 copy-done.2
  275.3 1.1 copy.38
Async XLA Ops:
  121.4 47.5 %copy-start.4 = (s32[32]{0:T(128)S(1)}, s32[32]{0:T(128)}, u32[]{:S(2)}) copy-start(s32[32]{0:T(128)} %refs_1_.1) | copy-start | bytes 388
  267.0 1.7 copy-start
  268.6 1.4 copy-start.1
  270.0 3.3 %copy-start.3 = (bf16[1024,768]{1,0:T(8,128)(2,1)S(1)}, bf16[1024,768]{1,0:T(8,128)(2,1)}, u32[]{:S(2)}) copy-start(bf16[1024,768]{1,0:T(8,128)(2,1)} %get-tuple-element.90) | copy-start | bytes 4718596
  273.3 2.0 copy-start.2

commit v6 on v5

--- a/solution.py
+++ b/solution.py
@@ -316,7 +316,7 @@
     run("ready")
 
     def project(block, carry):
-        at = pl.ds(pl.multiple_of(block * 256, 256), 256)
+        at = pl.ds(pl.multiple_of(block * 512, 512), 512)
         h0 = tok[at, :].astype(F32)
         x = h0 * lax.rsqrt(jnp.mean(h0 * h0, axis=1, keepdims=True) + EPS) * gain_a[...][None]
         x = x.astype(BF)
@@ -333,7 +333,7 @@
         v_ref[at, :] = (mm(x, wqkv[:, lanes]) + mm(u, up_s[:, lanes])).astype(BF)
         return carry
 
-    lax.fori_loop(0, length // 256, project, 0)
+    lax.fori_loop(0, length // 512, project, 0)
     run("projected")
 
     lane = iota((1, GROUP), 1)
@@ -376,7 +376,7 @@
     lax.fori_loop(0, HEADS, attend, 0)
 
     def finish(block, carry):
-        at = pl.ds(pl.multiple_of(block * 256, 256), 256)
+        at = pl.ds(pl.multiple_of(block * 512, 512), 512)
         o = ob_ref[at, :]
         u = mm(o, down_o).astype(BF)
         uo_ref[at, :] = u
@@ -388,7 +388,7 @@
         lin_ref[at, :] = mm_t(x, wr[...])
         return carry
 
-    lax.fori_loop(0, length // 256, finish, 0)
+    lax.fori_loop(0, length // 512, finish, 0)
     if exchange:
         store.start(range(15))
         run("finished")

time: 281 us -> 281 us (level)
    pallas_call x1, Pallas kernels: 97.3 us -> 108 us  [attention_backward(): pl.pallas_call(functools.partial(attention_backward_kernel, maps is not N...]
    pallas_call x1, Pallas kernels: 47.5 us -> 37.6 us  [experts_both_ways(): pl.pallas_call(functools.partial(experts_kernel, own_first), out_shape=[j...]
where the time goes in v6:
time: 281 us; the launch traced here: 278 us
  Pallas kernels  269 us (96%)
  local copies, waits for them, and re-layouts  6.93 us (2%)
    pallas_call x1, Pallas kernels, attention_forward(): pl.pallas_call(functools.partial(attention_forward_kernel, bool(own)), ou...  120 us
    pallas_call x1, Pallas kernels, attention_backward(): pl.pallas_call(functools.partial(attention_backward_kernel, maps is not N...  108 us
    pallas_call x1, Pallas kernels, experts_both_ways(): pl.pallas_call(functools.partial(experts_kernel, own_first), out_shape=[j...  37.6 us
    unnamed x12, local copies, waits for them, and re-layouts  6.19 us

profile of v6, /device:TPU:0, one launch (start us, length us, event | category | flops | bytes accessed | tf_op | source)
XLA Modules:
  0.0 278.0 jit_solution(213026220453209191)
XLA Ops:
  0.7 0.5 iota_add_fusion.order
  1.2 120.2 %attention_forward.1 = (bf16[1024,768]{1,0:T(8,128)(2,1)}, bf16[1024,768]{1,0:T(8,128)(2,1)}, bf16[1024,768]{1,0:T(8,128)(2,1)}, bf16[1024,768]{1,0:T(8,128)(2,1...) custom-call(s32[2]{0:T(128)} %bitcast.10, ...), custom_call_target="tpu_custom_call" | custom-call | tf_op jit(solution)/shard_map/attention_forward/pallas_call | solution.py:509
  121.4 0.0 copy-start.4
  121.4 37.6 %experts_both_ways.1 = (bf16[1024,1664]{1,0:T(8,128)(2,1)}, f32[1024,128]{1,0:T(8,128)}, bf16[4,16,9216]{2,1,0:T(8,128)(2,1)}) custom-call(s32[2]{0:T(128)} %iota_add_fusion.order, bf16[1024,768]{1,0:T(8,128)(2,1)} %get-tuple-element.57.xb, bf16[1024,768]{1,0:T(8,128)(2,1)} %refs_20_.3, s32[2,1024]{1,0:T(2,128)} %bitcast.7, ...), custom_call_target="tpu_custom_call" | custom-call | tf_op jit(solution)/shard_map/experts_both_ways/pallas_call | solution.py:1284
  159.1 0.0 copy-done.4
  159.1 0.1 broadcast_in_dim.3
  159.1 0.7 broadcast_in_dim_reshape.3.refs_28_
  159.8 108.3 %attention_backward.1 = (bf16[1024,768]{1,0:T(8,128)(2,1)}, bf16[1024,768]{1,0:T(8,128)(2,1)}, bf16[8,128,1152]{2,1,0:T(8,128)(2,1)}, bf16[8,128,768]{2,1,0:T(8,128)(2,1)}) custom-call(s32[2]{0:T(128)} %bitcast.11, f32[1024,768]{1,0:T(8,128)} %get-tuple-element.45.refs_1_, bf16[1024,768]{1,0:T(8,128)(2,1)} %refs_2_.3, f32[768]{0:T(1024)} %refs_3_.3, ...), custom_call_target="tpu_custom_call" | custom-call | tf_op jit(solution)/shard_map/attention_backward/pallas_call | solution.py:998
  268.2 0.0 copy-start
  268.2 1.7 copy-done
  269.8 0.0 copy-start.1
  269.8 1.4 copy-done.1
  271.2 0.0 copy-start.3
  271.2 3.3 %unpack.1 = (f32[4,768,128]{2,1,0:T(8,128)}, f32[3,128,768]{2,1,0:T(8,128)}, f32[128,768]{1,0:T(8,128)}, f32[1,2,768,128]{3,2,1,0:T(8,128)}, f32[1,2,128,2048]{3...) custom-call(bf16[8,128,1152]{2,1,0:T(8,128)(2,1)S(1)} %copy-done, bf16[8,128,768]{2,1,0:T(8,128)(2,1)S(1)} %copy-done.1), custom_call_target="tpu_custom_call" | custom-call | tf_op jit(solution)/shard_map/unpack/pallas_call | solution.py:1042
  274.5 0.0 copy-done.3
  274.5 0.0 copy-start.2
  274.5 1.1 copy.37
  275.7 0.8 copy-done.2
  276.5 1.1 copy.38
Async XLA Ops:
  121.4 37.6 %copy-start.4 = (s32[32]{0:T(128)S(1)}, s32[32]{0:T(128)}, u32[]{:S(2)}) copy-start(s32[32]{0:T(128)} %refs_1_.1) | copy-start | bytes 388
  268.2 1.7 copy-start
  269.8 1.4 copy-start.1
  271.2 3.3 %copy-start.3 = (bf16[1024,768]{1,0:T(8,128)(2,1)S(1)}, bf16[1024,768]{1,0:T(8,128)(2,1)}, u32[]{:S(2)}) copy-start(bf16[1024,768]{1,0:T(8,128)(2,1)} %get-tuple-element.90) | copy-start | bytes 4718596
  274.5 2.0 copy-start.2
